TPU v7x, 256 devices: a whole 4x4x8 slice. The times are simulated.
256 devices in a mesh: ctx: 16 (over x_lo, y, core), tp: 16 (over x_hi, z).
Axes of the slice: x: 4 (x_hi: 2, x_lo: 2; x = x_hi * 2 + x_lo), y: 4, z: 8, core: 2. Of those that a mesh axis runs over, the one named last changes fastest.
Arguments:
- features: bfloat16 [4096, 3, 8192], P('ctx', None, 'tp'), may hold values from -6 to 6
- short_filter: float32 [3, 7, 8192], P(None, None, 'tp'), may hold values from -2 to 2
- decay_rate: float32 [16, 8192], P(None, 'tp'), may hold values from 0.05 to 136.533333
- residue: float32 [16, 8192], P(None, 'tp'), may hold values from -1.5 to 1.5
- out_weight: bfloat16 [8192, 8192], P('tp'), may hold values from -0.0625 to 0.0625
Outputs:
- block_output: bfloat16 [4096, 8192], P(('ctx', 'tp'))
All inputs are finite; a program needn't handle non-finite values.
Results may differ from a plain program's by a relative error of at most 0.027.
Values may be sent and summed in bfloat16 or wider, within the bound.
No kernel may reach another device: no remote copies, remote signals or barrier semaphores. Data moves between devices by JAX's collectives and lax.ppermute only.
A program may use at most 64 MiB of HBM per device.

v0:
```python
import math

import jax
import jax.numpy as jnp
from jax import lax
from jax.sharding import PartitionSpec as P

TAPS = 7


def passed_along(shard, axis, by):
    devices = lax.axis_size(axis)
    pairs = [(i, i + by) for i in range(devices) if 0 <= i + by < devices]
    return lax.ppermute(shard, axis, pairs)


def local(features, short_filter, decay_rate, residue, out_weight):
    tok_rows = features.shape[0]
    chan_count = features.shape[2]
    ctx_count = lax.axis_size("ctx")
    inv_tokens = 1.0 / (tok_rows * ctx_count)
    highest = lax.Precision.HIGHEST
    tail_rows = features[tok_rows - (TAPS - 1) :]
    before = passed_along(tail_rows, "ctx", 1)
    padded = jnp.concatenate([before, features], axis=0).astype(jnp.float32)
    featured = short_filter[:, 0, :] * padded[TAPS - 1 : TAPS - 1 + tok_rows]
    for j in range(1, TAPS):
        featured = featured + short_filter[:, j, :] * padded[TAPS - 1 - j : TAPS - 1 - j + tok_rows]
    queries = featured[:, 0]
    signal = featured[:, 1] * featured[:, 2]
    blk_rows = min(tok_rows, 512)
    num_blocks = tok_rows // blk_rows
    mode_gain = jnp.sqrt(inv_tokens - jnp.expm1(-2.0 * decay_rate * inv_tokens))
    mode_coef = residue * mode_gain
    step_index = jnp.arange(blk_rows).astype(jnp.float32)
    powers = jnp.exp(-(step_index[:, None, None] * inv_tokens) * decay_rate[None])
    local_filter = jnp.sum(powers * mode_coef[None], axis=1)
    dft_len = 2 * blk_rows
    freq_index = jnp.arange(dft_len, dtype=jnp.int32)[:, None]
    pos_index = jnp.arange(blk_rows, dtype=jnp.int32)[None, :]
    angles = (freq_index * pos_index % dft_len).astype(jnp.float32) * (2.0 * math.pi / dft_len)
    forward = jnp.concatenate([jnp.cos(angles), jnp.sin(angles)], axis=0)
    inverse = forward.T / dft_len
    sig_blocks = signal.reshape(num_blocks, blk_rows, chan_count)
    filt_spec = jnp.dot(forward, local_filter, precision=highest)
    sig_spec = jnp.einsum("ft,btc->bfc", forward, sig_blocks, precision=highest)
    sig_real = sig_spec[:, :dft_len]
    sig_imag = sig_spec[:, dft_len:]
    filt_real = filt_spec[None, :dft_len]
    filt_imag = filt_spec[None, dft_len:]
    product_spec = jnp.concatenate(
        [sig_real * filt_real - sig_imag * filt_imag, sig_real * filt_imag + sig_imag * filt_real],
        axis=1,
    )
    local_part = jnp.einsum("tf,bfc->btc", inverse, product_spec, precision=highest)
    block_ends = jnp.einsum("jmc,bjc->bmc", powers, sig_blocks[:, ::-1], precision=highest)
    blk_decay = jnp.exp(-decay_rate * (blk_rows * inv_tokens))
    running = jnp.zeros_like(decay_rate)
    entering = [running]
    running = blk_decay * running + block_ends[0]
    device_end = running
    dev_decay = jnp.exp(-decay_rate * (tok_rows * inv_tokens))
    zero_state = jnp.zeros_like(decay_rate)

    def relay_step(index, carried_state):
        return passed_along(
            (dev_decay * carried_state + device_end).astype(jnp.bfloat16), "ctx", 1
        ).astype(jnp.float32)

    incoming = lax.fori_loop(0, ctx_count - 1, relay_step, zero_state)
    inner_state = jnp.stack(entering, axis=0)
    offsets = jnp.arange(num_blocks).astype(jnp.float32) * blk_rows
    block_state = (
        inner_state
        + jnp.exp(-decay_rate[None] * (offsets[:, None, None] * inv_tokens)) * incoming[None]
    )
    step_decay = jnp.exp(-decay_rate * inv_tokens)
    carried = jnp.einsum(
        "tmc,bmc->btc", powers, block_state * (mode_coef * step_decay)[None], precision=highest
    )
    convolved = (local_part + carried).reshape(tok_rows, chan_count)
    gated = (queries * convolved).astype(jnp.bfloat16)
    return lax.psum_scatter(
        jnp.dot(gated, out_weight, preferred_element_type=jnp.float32).astype(jnp.bfloat16),
        "tp",
        scatter_dimension=0,
        tiled=True,
    )


def solution(mesh):
    in_specs = (
        P("ctx", None, "tp"),
        P(None, None, "tp"),
        P(None, "tp"),
        P(None, "tp"),
        P("tp", None),
    )
    out_specs = P(("ctx", "tp"), None)
    return jax.shard_map(local, mesh=mesh, in_specs=in_specs, out_specs=out_specs, check_vma=False)
```

profile of v0, /device:TPU:8, one launch (start us, length us, event | category | flops | bytes accessed | tf_op | source)
XLA Modules:
  0.0 380.6 jit_solution(1851881232687397139)
XLA Ops:
  13.2 3.5 collective-permute-done.1
  17.2 4.2 %fusion.5 = f32[256,3,512]{0,2,1:T(8,128)S(1)} fusion(f32[262,3,512]{0,2,1:T(8,128)S(1)} %maximum_convert_fusion, f32[3,512]{1,0:T(4,128)S(1)} %get-tuple-element.64, f32[3,512]{1,0:T(4,128)S(1)} %get-tuple-element.65, f32[3,512]{1,0:T(4,128)S(1)} %get-tuple-element.66, f32[3,512]{1,0:T(4,128)S(1)} %get-tuple-element.67, f32[3,512]{1,0:T(4,128)S(1)} %get-tuple-element.68, ...), kind=kLoop, calls=%fused_computation.14 | loop fusion | flops 5111808 | bytes 12625920 | tf_op jit(solution)/shard_map/add | solution.py:28
  25.4 87.8 %while.11 = (s32[]{:T(128)}, f32[16,512]{1,0:T(8,128)S(1)}, f32[16,512]{1,0:T(8,128)S(1)}, f32[16,512]{1,0:T(8,128)S(1)}, s32[]{:T(128)}, /*index=5*/s32[]{:T(128)}) while((s32[]{:T(128)}, f32[16,512]{1,0:T(8,128)S(1)}, f32[16,512]{1,0:T(8,128)S(1)}, f32[16,512]{1,0:T(8,128)S(1)}, s32[]{:T(128)}, /*index=5*/s32[]{:T(128)}) %tuple.35), condition=%wide.region_2.3_spmd.clone, body=%wide.region_1.2_spmd.clone.sunk | while | flops 40963 | bytes 229495 | solution.py:70
  27.3 3.1 collective-permute-done
  32.4 3.1 collective-permute-done
  37.5 3.1 collective-permute-done
  42.6 3.1 collective-permute-done
  47.6 3.1 collective-permute-done
  52.7 3.1 collective-permute-done
  57.8 3.1 collective-permute-done
  62.9 3.1 collective-permute-done
  66.0 3.2 collective-permute-start
  71.1 5.3 %collective-permute-start = (bf16[16,512]{1,0:T(8,128)(2,1)S(1)}, bf16[16,512]{1,0:T(8,128)(2,1)S(1)}, u32[]{:S(2)}, u32[]{:S(2)}) collective-permute-start(bf16[16,512]{1,0:T(8,128)(2,1)S(1)} %fusion.38), channel_id=1, source_target_pairs={{0,16},{16,32},{32,48},{48,64},{64,80},{80,96},{96,112},{112,128},... | collective-permute-start | bytes 49160 | tf_op jit(solution)/shard_map/while/body/eval_jaxpr/ppermute | solution.py:14
  77.2 6.3 %collective-permute-start = (bf16[16,512]{1,0:T(8,128)(2,1)S(1)}, bf16[16,512]{1,0:T(8,128)(2,1)S(1)}, u32[]{:S(2)}, u32[]{:S(2)}) collective-permute-start(bf16[16,512]{1,0:T(8,128)(2,1)S(1)} %fusion.38), channel_id=1, source_target_pairs={{0,16},{16,32},{32,48},{48,64},{64,80},{80,96},{96,112},{112,128},... | collective-permute-start | bytes 49160 | tf_op jit(solution)/shard_map/while/body/eval_jaxpr/ppermute | solution.py:14
  84.4 6.3 %collective-permute-start = (bf16[16,512]{1,0:T(8,128)(2,1)S(1)}, bf16[16,512]{1,0:T(8,128)(2,1)S(1)}, u32[]{:S(2)}, u32[]{:S(2)}) collective-permute-start(bf16[16,512]{1,0:T(8,128)(2,1)S(1)} %fusion.38), channel_id=1, source_target_pairs={{0,16},{16,32},{32,48},{48,64},{64,80},{80,96},{96,112},{112,128},... | collective-permute-start | bytes 49160 | tf_op jit(solution)/shard_map/while/body/eval_jaxpr/ppermute | solution.py:14
  91.6 6.3 %collective-permute-start = (bf16[16,512]{1,0:T(8,128)(2,1)S(1)}, bf16[16,512]{1,0:T(8,128)(2,1)S(1)}, u32[]{:S(2)}, u32[]{:S(2)}) collective-permute-start(bf16[16,512]{1,0:T(8,128)(2,1)S(1)} %fusion.38), channel_id=1, source_target_pairs={{0,16},{16,32},{32,48},{48,64},{64,80},{80,96},{96,112},{112,128},... | collective-permute-start | bytes 49160 | tf_op jit(solution)/shard_map/while/body/eval_jaxpr/ppermute | solution.py:14
  98.8 6.3 %collective-permute-start = (bf16[16,512]{1,0:T(8,128)(2,1)S(1)}, bf16[16,512]{1,0:T(8,128)(2,1)S(1)}, u32[]{:S(2)}, u32[]{:S(2)}) collective-permute-start(bf16[16,512]{1,0:T(8,128)(2,1)S(1)} %fusion.38), channel_id=1, source_target_pairs={{0,16},{16,32},{32,48},{48,64},{64,80},{80,96},{96,112},{112,128},... | collective-permute-start | bytes 49160 | tf_op jit(solution)/shard_map/while/body/eval_jaxpr/ppermute | solution.py:14
  106.0 6.3 %collective-permute-start = (bf16[16,512]{1,0:T(8,128)(2,1)S(1)}, bf16[16,512]{1,0:T(8,128)(2,1)S(1)}, u32[]{:S(2)}, u32[]{:S(2)}) collective-permute-start(bf16[16,512]{1,0:T(8,128)(2,1)S(1)} %fusion.38), channel_id=1, source_target_pairs={{0,16},{16,32},{32,48},{48,64},{64,80},{80,96},{96,112},{112,128},... | collective-permute-start | bytes 49160 | tf_op jit(solution)/shard_map/while/body/eval_jaxpr/ppermute | solution.py:14
  113.2 2.4 multiply_reduce_fusion.2
  117.5 3.3 fusion.17
  120.7 3.2 multiply_reduce_fusion
  128.1 2.9 fusion.15
  131.0 7.7 %convolution_convert_fusion = bf16[256,8192]{1,0:T(8,128)(2,1)} fusion(bf16[256,512]{0,1:T(8,128)(2,1)S(1)} %fusion.15, bf16[512,8192]{1,0:T(8,128)(2,1)} %param.11), kind=kOutput, calls=%fused_computation.3 | convolution fusion | flops 2149580800 | bytes 12845056 | tf_op jit(solution)/shard_map/dot_general | solution.py:84
  138.7 235.0 %reduce-scatter.2.cloned.1.call-done = bf16[16,8192]{1,0:T(8,128)(2,1)} async-done(((bf16[256,8192]{1,0:T(8,128)(2,1)}), bf16[16,8192]{1,0:T(8,128)(2,1)}) %reduce-scatter.2.cloned.1.call-update) | async-done | bytes 262160 | tf_op jit(solution)/shard_map/reduce_scatter | solution.py:83
  (83 shorter events, 39.4 us)
Async XLA Ops:
  6.5 6.3 %copy-start.4 = (bf16[256,3,512]{2,0,1:T(8,128)(2,1)S(1)}, bf16[256,3,512]{2,0,1:T(8,128)(2,1)}, u32[]{:S(2)}) copy-start(bf16[256,3,512]{2,0,1:T(8,128)(2,1)} %param.7) | copy-start | bytes 2359300
  6.5 367.2 %reduce-scatter.2.cloned.1.call-start = ((), (), s32[]{:S(2)}) async-start(), calls=%async_computation.1 | async-start | bytes 4456448 | tf_op jit(solution)/shard_map/reduce_scatter | solution.py:83
  7.6 9.1 %collective-permute-start.1 = (bf16[6,3,512]{0,2,1:T(8,128)(2,1)S(1)}, bf16[6,3,512]{0,2,1:T(8,128)(2,1)S(1)}, u32[]{:S(2)}, u32[]{:S(2)}) collective-permute-start(bf16[6,3,512]{0,2,1:T(8,128)(2,1)S(1)} %copy.14), channel_id=1, source_target_pairs={{0,16},{16,32},{32,48},{48,64},{64,80},{80,96},{96,112},{112,128},... | collective-permute-start | bytes 55304 | tf_op jit(solution)/shard_map/ppermute | solution.py:14
  21.5 1.2 copy-start
  22.6 1.0 copy-start.5
  22.7 2.6 copy-start.1
  23.6 89.5 %copy-start.6 = (f32[16,512]{1,0:T(8,128)S(1)}, f32[16,512]{1,0:T(8,128)}, u32[]{:S(2)}) copy-start(f32[16,512]{1,0:T(8,128)} %param.10) | copy-start | bytes 98308
  25.4 5.1 %collective-permute-start = (bf16[16,512]{1,0:T(8,128)(2,1)S(1)}, bf16[16,512]{1,0:T(8,128)(2,1)S(1)}, u32[]{:S(2)}, u32[]{:S(2)}) collective-permute-start(bf16[16,512]{1,0:T(8,128)(2,1)S(1)} %fusion.38), channel_id=1, source_target_pairs={{0,16},{16,32},{32,48},{48,64},{64,80},{80,96},{96,112},{112,128},... | collective-permute-start | bytes 49160 | tf_op jit(solution)/shard_map/while/body/eval_jaxpr/ppermute | solution.py:14
  30.5 5.1 %collective-permute-start = (bf16[16,512]{1,0:T(8,128)(2,1)S(1)}, bf16[16,512]{1,0:T(8,128)(2,1)S(1)}, u32[]{:S(2)}, u32[]{:S(2)}) collective-permute-start(bf16[16,512]{1,0:T(8,128)(2,1)S(1)} %fusion.38), channel_id=1, source_target_pairs={{0,16},{16,32},{32,48},{48,64},{64,80},{80,96},{96,112},{112,128},... | collective-permute-start | bytes 49160 | tf_op jit(solution)/shard_map/while/body/eval_jaxpr/ppermute | solution.py:14
  35.6 5.1 %collective-permute-start = (bf16[16,512]{1,0:T(8,128)(2,1)S(1)}, bf16[16,512]{1,0:T(8,128)(2,1)S(1)}, u32[]{:S(2)}, u32[]{:S(2)}) collective-permute-start(bf16[16,512]{1,0:T(8,128)(2,1)S(1)} %fusion.38), channel_id=1, source_target_pairs={{0,16},{16,32},{32,48},{48,64},{64,80},{80,96},{96,112},{112,128},... | collective-permute-start | bytes 49160 | tf_op jit(solution)/shard_map/while/body/eval_jaxpr/ppermute | solution.py:14
  40.6 5.1 %collective-permute-start = (bf16[16,512]{1,0:T(8,128)(2,1)S(1)}, bf16[16,512]{1,0:T(8,128)(2,1)S(1)}, u32[]{:S(2)}, u32[]{:S(2)}) collective-permute-start(bf16[16,512]{1,0:T(8,128)(2,1)S(1)} %fusion.38), channel_id=1, source_target_pairs={{0,16},{16,32},{32,48},{48,64},{64,80},{80,96},{96,112},{112,128},... | collective-permute-start | bytes 49160 | tf_op jit(solution)/shard_map/while/body/eval_jaxpr/ppermute | solution.py:14
  45.7 5.1 %collective-permute-start = (bf16[16,512]{1,0:T(8,128)(2,1)S(1)}, bf16[16,512]{1,0:T(8,128)(2,1)S(1)}, u32[]{:S(2)}, u32[]{:S(2)}) collective-permute-start(bf16[16,512]{1,0:T(8,128)(2,1)S(1)} %fusion.38), channel_id=1, source_target_pairs={{0,16},{16,32},{32,48},{48,64},{64,80},{80,96},{96,112},{112,128},... | collective-permute-start | bytes 49160 | tf_op jit(solution)/shard_map/while/body/eval_jaxpr/ppermute | solution.py:14
  50.8 5.1 %collective-permute-start = (bf16[16,512]{1,0:T(8,128)(2,1)S(1)}, bf16[16,512]{1,0:T(8,128)(2,1)S(1)}, u32[]{:S(2)}, u32[]{:S(2)}) collective-permute-start(bf16[16,512]{1,0:T(8,128)(2,1)S(1)} %fusion.38), channel_id=1, source_target_pairs={{0,16},{16,32},{32,48},{48,64},{64,80},{80,96},{96,112},{112,128},... | collective-permute-start | bytes 49160 | tf_op jit(solution)/shard_map/while/body/eval_jaxpr/ppermute | solution.py:14
  55.9 5.1 %collective-permute-start = (bf16[16,512]{1,0:T(8,128)(2,1)S(1)}, bf16[16,512]{1,0:T(8,128)(2,1)S(1)}, u32[]{:S(2)}, u32[]{:S(2)}) collective-permute-start(bf16[16,512]{1,0:T(8,128)(2,1)S(1)} %fusion.38), channel_id=1, source_target_pairs={{0,16},{16,32},{32,48},{48,64},{64,80},{80,96},{96,112},{112,128},... | collective-permute-start | bytes 49160 | tf_op jit(solution)/shard_map/while/body/eval_jaxpr/ppermute | solution.py:14
  60.9 5.1 %collective-permute-start = (bf16[16,512]{1,0:T(8,128)(2,1)S(1)}, bf16[16,512]{1,0:T(8,128)(2,1)S(1)}, u32[]{:S(2)}, u32[]{:S(2)}) collective-permute-start(bf16[16,512]{1,0:T(8,128)(2,1)S(1)} %fusion.38), channel_id=1, source_target_pairs={{0,16},{16,32},{32,48},{48,64},{64,80},{80,96},{96,112},{112,128},... | collective-permute-start | bytes 49160 | tf_op jit(solution)/shard_map/while/body/eval_jaxpr/ppermute | solution.py:14
  66.0 5.1 %collective-permute-start = (bf16[16,512]{1,0:T(8,128)(2,1)S(1)}, bf16[16,512]{1,0:T(8,128)(2,1)S(1)}, u32[]{:S(2)}, u32[]{:S(2)}) collective-permute-start(bf16[16,512]{1,0:T(8,128)(2,1)S(1)} %fusion.38), channel_id=1, source_target_pairs={{0,16},{16,32},{32,48},{48,64},{64,80},{80,96},{96,112},{112,128},... | collective-permute-start | bytes 49160 | tf_op jit(solution)/shard_map/while/body/eval_jaxpr/ppermute | solution.py:14
  71.1 6.1 %collective-permute-start = (bf16[16,512]{1,0:T(8,128)(2,1)S(1)}, bf16[16,512]{1,0:T(8,128)(2,1)S(1)}, u32[]{:S(2)}, u32[]{:S(2)}) collective-permute-start(bf16[16,512]{1,0:T(8,128)(2,1)S(1)} %fusion.38), channel_id=1, source_target_pairs={{0,16},{16,32},{32,48},{48,64},{64,80},{80,96},{96,112},{112,128},... | collective-permute-start | bytes 49160 | tf_op jit(solution)/shard_map/while/body/eval_jaxpr/ppermute | solution.py:14
  77.2 7.2 %collective-permute-start = (bf16[16,512]{1,0:T(8,128)(2,1)S(1)}, bf16[16,512]{1,0:T(8,128)(2,1)S(1)}, u32[]{:S(2)}, u32[]{:S(2)}) collective-permute-start(bf16[16,512]{1,0:T(8,128)(2,1)S(1)} %fusion.38), channel_id=1, source_target_pairs={{0,16},{16,32},{32,48},{48,64},{64,80},{80,96},{96,112},{112,128},... | collective-permute-start | bytes 49160 | tf_op jit(solution)/shard_map/while/body/eval_jaxpr/ppermute | solution.py:14
  84.4 7.2 %collective-permute-start = (bf16[16,512]{1,0:T(8,128)(2,1)S(1)}, bf16[16,512]{1,0:T(8,128)(2,1)S(1)}, u32[]{:S(2)}, u32[]{:S(2)}) collective-permute-start(bf16[16,512]{1,0:T(8,128)(2,1)S(1)} %fusion.38), channel_id=1, source_target_pairs={{0,16},{16,32},{32,48},{48,64},{64,80},{80,96},{96,112},{112,128},... | collective-permute-start | bytes 49160 | tf_op jit(solution)/shard_map/while/body/eval_jaxpr/ppermute | solution.py:14
  91.6 7.2 %collective-permute-start = (bf16[16,512]{1,0:T(8,128)(2,1)S(1)}, bf16[16,512]{1,0:T(8,128)(2,1)S(1)}, u32[]{:S(2)}, u32[]{:S(2)}) collective-permute-start(bf16[16,512]{1,0:T(8,128)(2,1)S(1)} %fusion.38), channel_id=1, source_target_pairs={{0,16},{16,32},{32,48},{48,64},{64,80},{80,96},{96,112},{112,128},... | collective-permute-start | bytes 49160 | tf_op jit(solution)/shard_map/while/body/eval_jaxpr/ppermute | solution.py:14
  98.8 7.2 %collective-permute-start = (bf16[16,512]{1,0:T(8,128)(2,1)S(1)}, bf16[16,512]{1,0:T(8,128)(2,1)S(1)}, u32[]{:S(2)}, u32[]{:S(2)}) collective-permute-start(bf16[16,512]{1,0:T(8,128)(2,1)S(1)} %fusion.38), channel_id=1, source_target_pairs={{0,16},{16,32},{32,48},{48,64},{64,80},{80,96},{96,112},{112,128},... | collective-permute-start | bytes 49160 | tf_op jit(solution)/shard_map/while/body/eval_jaxpr/ppermute | solution.py:14
  106.0 7.2 %collective-permute-start = (bf16[16,512]{1,0:T(8,128)(2,1)S(1)}, bf16[16,512]{1,0:T(8,128)(2,1)S(1)}, u32[]{:S(2)}, u32[]{:S(2)}) collective-permute-start(bf16[16,512]{1,0:T(8,128)(2,1)S(1)} %fusion.38), channel_id=1, source_target_pairs={{0,16},{16,32},{32,48},{48,64},{64,80},{80,96},{96,112},{112,128},... | collective-permute-start | bytes 49160 | tf_op jit(solution)/shard_map/while/body/eval_jaxpr/ppermute | solution.py:14
  113.1 2.5 copy-start.2
  126.0 2.1 copy-start.3
Sparse Core Ops, SparseCore 0:
  138.8 234.8 reduce-scatter.1
where the time goes:
time: 381 us
  waiting for transfers between devices  270 us (71%)
  starting transfers between devices  57.4 us (15%)
  other arithmetic  16.5 us (4%)
  matrix products  15.7 us (4%)
  between operations  13.6 us (4%)
  local copies, waits for them, and re-layouts  6.71 us (2%)
    reduce_scatter x1, waiting for transfers between devices, local(): lax.psum_scatter(jnp.dot(gated, out_weight, preferred_element_type=jnp.fl...  235 us
    ppermute x16, starting transfers between devices, passed_along(): return lax.ppermute(shard, axis, pairs)  57.4 us
    ppermute x16, waiting for transfers between devices, passed_along(): return lax.ppermute(shard, axis, pairs)  35.4 us
    dot_general x1, matrix products, local(): jnp.dot(gated, out_weight, preferred_element_type=jnp.float32)  7.71 us
  transfers between devices with their start and end apart: 17, of which 17 were waited for; matrix products, arithmetic and copies ran while one was open for 1% of the time, Pallas kernels for 0%

commit v1 on v0

v1 whole, which is shorter than its diff:
```python
import functools

import jax
import jax.numpy as jnp
from jax import lax
from jax.experimental import pallas as pl
from jax.experimental.pallas import tpu as pltpu
from jax.sharding import PartitionSpec as P

TAPS = 7
MODES = 16
SUB = 8
LANES = 128
NZ = 8
N_CTX = 16
HALO = 16

f32 = jnp.float32
bf16 = jnp.bfloat16


def signal_kernel(ctx_ref, x_ref, halo_ref, taps_ref, a_ref, sig_ref, q_ref, ends_ref, send_ref, pad, ends, step_powers):
    rows = x_ref.shape[1]
    run = rows // SUB
    for b in range(3):
        pad[b, :HALO] = halo_ref[b].astype(f32)
        pad[b, HALO:] = x_ref[b].astype(f32)
    wide = (SUB, LANES)
    for b in range(3):
        taps = [jnp.broadcast_to(taps_ref[b, j : j + 1, :], wide) for j in range(TAPS)]
        window = [pad[b, pl.ds(HALO - j, SUB, stride=run), :] for j in range(1, TAPS)]
        for t in range(run):
            window = [pad[b, pl.ds(HALO + t, SUB, stride=run), :]] + window
            total = taps[0] * window[0]
            for j in range(1, TAPS):
                total = total + taps[j] * window[j]
            if b == 0:
                q_ref[t] = total
            elif b == 1:
                sig_ref[t] = total
            else:
                sig_ref[t] = sig_ref[t] * total
            window = window[: TAPS - 1]
    for first in range(0, MODES, 8):
        decay = [jnp.broadcast_to(a_ref[m : m + 1, :], wide) for m in range(first, first + 8)]
        state = [sig_ref[0]] * 8
        for t in range(1, run):
            now = sig_ref[t]
            state = [d * s + now for d, s in zip(decay, state)]
        for m in range(8):
            ends[first + m] = state[m]
            ends_ref[first + m] = state[m]
    a = a_ref[...]
    power = a
    for _ in range(run.bit_length() - 1):
        power = power * power
    total = ends[:, 0, :]
    for j in range(1, SUB):
        total = power * total + ends[:, j, :]
    whole = power
    for _ in range(SUB.bit_length() - 1):
        whole = whole * whole
    me = ctx_ref[0]
    for d in range(N_CTX):
        step_powers[d] = total
        total = total * whole
    for d in range(N_CTX):
        away = jnp.maximum(d - me - 1, 0)
        sent = step_powers[away]
        send_ref[d] = jnp.where(d > me, sent, 0.0).astype(bf16)


def gate_kernel(pos_ref, sig_ref, q_ref, ends_ref, a_ref, coef_ref, recv_ref, out_ref, starts, conv, gated):
    run = sig_ref.shape[0]
    wide = (SUB, LANES)
    a = a_ref[...]
    power = a
    for _ in range(run.bit_length() - 1):
        power = power * power
    state = recv_ref[0].astype(f32)
    for p in range(1, N_CTX):
        state = state + recv_ref[p].astype(f32)
    for j in range(SUB):
        starts[:, j, :] = state
        if j < SUB - 1:
            state = power * state + ends_ref[:, j, :]
    for first in range(0, MODES, 8):
        decay = [jnp.broadcast_to(a_ref[m : m + 1, :], wide) for m in range(first, first + 8)]
        coef = [jnp.broadcast_to(coef_ref[m : m + 1, :], wide) for m in range(first, first + 8)]
        state = [starts[m] for m in range(first, first + 8)]
        for t in range(run):
            now = sig_ref[t]
            state = [d * s + now for d, s in zip(decay, state)]
            terms = [c * s for c, s in zip(coef, state)]
            while len(terms) > 1:
                terms = [terms[i] + terms[i + 1] for i in range(0, len(terms), 2)]
            if first == 0:
                conv[t] = terms[0]
            else:
                gated[pl.ds(t, SUB, stride=run), :] = (conv[t] + terms[0]) * q_ref[t]
    half, z = pos_ref[0], pos_ref[1]
    for h in range(2):
        for k in range(NZ):
            block = lax.rem(half + h, 2) * NZ + lax.rem(z + k, NZ)
            rows = gated[pl.ds(pl.multiple_of(block * 16, 16), 16), :]
            out_ref[(h * NZ + k) * 16 : (h * NZ + k + 1) * 16, :] = rows.astype(bf16)


def z_pairs(by):
    return [(h * NZ + z, h * NZ + (z + by) % NZ) for h in range(2) for z in range(NZ)]


def half_pairs():
    return [(i, (i + NZ) % (2 * NZ)) for i in range(2 * NZ)]


def ring(blocks, more_left):
    rights, lefts = (NZ // 2 - 1, NZ // 2) if more_left else (NZ // 2, NZ // 2 - 1)
    right = blocks[rights]
    left = blocks[-lefts % NZ]
    for s in range(NZ // 2):
        if s < rights:
            right = lax.ppermute(right, "tp", z_pairs(1))
        if s < lefts:
            left = lax.ppermute(left, "tp", z_pairs(-1))
        if s < rights - 1:
            right = (right.astype(f32) + blocks[rights - 1 - s].astype(f32)).astype(bf16)
        if s < lefts - 1:
            left = (left.astype(f32) + blocks[-(lefts - 1 - s) % NZ].astype(f32)).astype(bf16)
    return right.astype(f32) + left.astype(f32) + blocks[0].astype(f32)


def reduce_columns(gated, weight, more_left):
    part = jnp.dot(gated, weight, preferred_element_type=f32).astype(bf16)
    part = part.reshape(2, NZ, 16, -1)
    both = ring([part[:, k] for k in range(NZ)], more_left)
    other = lax.ppermute(both[1].astype(bf16), "tp", half_pairs())
    return (both[0] + other.astype(f32)).astype(bf16)


def local(features, short_filter, decay_rate, residue, out_weight):
    rows, _, chans = features.shape
    n_ctx = lax.axis_size("ctx")
    inv_tokens = 1.0 / (rows * n_ctx)
    run = rows // SUB
    ctx = lax.axis_index("ctx")
    tp = lax.axis_index("tp")
    halo = lax.ppermute(features[rows - HALO :], "ctx", [(i, i + 1) for i in range(n_ctx - 1)])
    halo = jnp.transpose(halo, (1, 0, 2))
    x = jnp.transpose(features, (1, 0, 2))
    a = jnp.exp(-decay_rate * inv_tokens)
    coef = residue * jnp.sqrt(inv_tokens - jnp.expm1(-2.0 * decay_rate * inv_tokens))
    groups = chans // LANES

    def lanes(*lead):
        return pl.BlockSpec((*lead, LANES), lambda g, *_: (0,) * len(lead) + (g,))

    sig, q, ends, send = pl.pallas_call(
        signal_kernel,
        grid_spec=pltpu.PrefetchScalarGridSpec(
            num_scalar_prefetch=1,
            grid=(groups,),
            in_specs=[lanes(3, rows), lanes(3, HALO), lanes(3, TAPS), lanes(MODES)],
            out_specs=[lanes(run, SUB), lanes(run, SUB), lanes(MODES, SUB), lanes(n_ctx, MODES)],
            scratch_shapes=[
                pltpu.VMEM((3, HALO + rows, LANES), f32),
                pltpu.VMEM((MODES, SUB, LANES), f32),
                pltpu.VMEM((N_CTX, MODES, LANES), f32),
            ],
        ),
        out_shape=[
            jax.ShapeDtypeStruct((run, SUB, chans), f32),
            jax.ShapeDtypeStruct((run, SUB, chans), f32),
            jax.ShapeDtypeStruct((MODES, SUB, chans), f32),
            jax.ShapeDtypeStruct((n_ctx, MODES, chans), bf16),
        ],
        name="signal",
    )(jnp.full((1,), ctx, jnp.int32), x, halo, short_filter, a)
    recv = lax.all_to_all(send, "ctx", 0, 0, tiled=True)
    gated = pl.pallas_call(
        gate_kernel,
        grid_spec=pltpu.PrefetchScalarGridSpec(
            num_scalar_prefetch=1,
            grid=(groups,),
            in_specs=[
                lanes(run, SUB),
                lanes(run, SUB),
                lanes(MODES, SUB),
                lanes(MODES),
                lanes(MODES),
                lanes(n_ctx, MODES),
            ],
            out_specs=lanes(rows),
            scratch_shapes=[
                pltpu.VMEM((MODES, SUB, LANES), f32),
                pltpu.VMEM((run, SUB, LANES), f32),
                pltpu.VMEM((rows, LANES), f32),
            ],
        ),
        out_shape=jax.ShapeDtypeStruct((rows, chans), bf16),
        name="gate",
    )(jnp.stack([tp // NZ, tp % NZ]).astype(jnp.int32), sig, q, ends, a, coef, recv)
    cols = out_weight.shape[1] // 2
    out = [reduce_columns(gated, out_weight[:, i * cols : (i + 1) * cols], i == 1) for i in range(2)]
    return jnp.concatenate(out, axis=1)


def solution(mesh):
    in_specs = (
        P("ctx", None, "tp"),
        P(None, None, "tp"),
        P(None, "tp"),
        P(None, "tp"),
        P("tp", None),
    )
    out_specs = P(("ctx", "tp"), None)
    return jax.shard_map(local, mesh=mesh, in_specs=in_specs, out_specs=out_specs, check_vma=False)
```

time: 381 us -> 94.2 us (0.25)
  waiting for transfers between devices: 270 us -> 30.2 us
  starting transfers between devices: 57.4 us -> 41 us
  between operations: 13.6 us -> 0.15 us
  other arithmetic: 16.5 us -> 3.62 us
  Pallas kernels: 0 us -> 9.17 us
  matrix products: 15.7 us -> 7.07 us
  local copies, waits for them, and re-layouts: 6.71 us -> 2.22 us
    reduce_scatter x1 -> x0, waiting for transfers between devices: 235 us -> none  [local(): lax.psum_scatter(jnp.dot(gated, out_weight, preferred_element_type=jnp.fl...]
    ppermute x16 -> x17, starting transfers between devices: 57.4 us -> 35.2 us  [the longest x7 19.2 us: ring(): left = lax.ppermute(left, 'tp', z_pairs(-1))]
    ppermute x16 -> x17, waiting for transfers between devices: 35.4 us -> 25.3 us  [the longest x7 11.2 us: ring(): right = lax.ppermute(right, 'tp', z_pairs(1))]
    pallas_call x0 -> x2, Pallas kernels: none -> 9.17 us  [the longest x1 4.79 us: local(): pl.pallas_call(gate_kernel, grid_spec=pltpu.PrefetchScalarGridSpec(num_sc...]
    dot_general x4 -> x2, matrix products: 15.7 us -> 7.07 us  [reduce_columns(): part = jnp.dot(gated, weight, preferred_element_type=f32).astype(bf16)]
    all_to_all x0 -> x1, starting transfers between devices: none -> 5.87 us  [local(): recv = lax.all_to_all(send, 'ctx', 0, 0, tiled=True)]
    all_to_all x0 -> x1, waiting for transfers between devices: none -> 4.86 us  [local(): recv = lax.all_to_all(send, 'ctx', 0, 0, tiled=True)]
    add x2, other arithmetic: 4.23 us -> 0.18 us  [ring(): return right.astype(f32) + left.astype(f32) + blocks[0].astype(f32)]
  transfers between devices with their start and end apart: 17 -> 18, of which waited for: 17 -> 12; matrix products, arithmetic and copies ran while one was open for 1% -> 3% of each run, Pallas kernels for 0% -> 0%
where the time goes in v1:
time: 94.2 us; the launch traced here: 93.5 us
  starting transfers between devices  41 us (44%)
  waiting for transfers between devices  30.2 us (32%)
  Pallas kernels  9.17 us (10%)
  matrix products  7.07 us (8%)
  other arithmetic  3.62 us (4%)
  local copies, waits for them, and re-layouts  2.22 us (2%)
    ppermute x7, starting transfers between devices, ring(): left = lax.ppermute(left, 'tp', z_pairs(-1))  19.2 us
    ppermute x7, waiting for transfers between devices, ring(): right = lax.ppermute(right, 'tp', z_pairs(1))  11.2 us
    ppermute x7, waiting for transfers between devices, ring(): left = lax.ppermute(left, 'tp', z_pairs(-1))  8.42 us
    ppermute x7, starting transfers between devices, ring(): right = lax.ppermute(right, 'tp', z_pairs(1))  8.36 us
    dot_general x2, matrix products, reduce_columns(): part = jnp.dot(gated, weight, preferred_element_type=f32).astype(bf16)  7.07 us
    all_to_all x1, starting transfers between devices, local(): recv = lax.all_to_all(send, 'ctx', 0, 0, tiled=True)  5.87 us
    ppermute x2, starting transfers between devices, reduce_columns(): other = lax.ppermute(both[1].astype(bf16), 'tp', half_pairs())  5.67 us
    all_to_all x1, waiting for transfers between devices, local(): recv = lax.all_to_all(send, 'ctx', 0, 0, tiled=True)  4.86 us
  transfers between devices with their start and end apart: 18, of which 12 were waited for; matrix products, arithmetic and copies ran while one was open for 3% of the time, Pallas kernels for 0%

profile of v1, /device:TPU:8, one launch (start us, length us, event | category | flops | bytes accessed | tf_op | source)
XLA Modules:
  0.0 93.5 jit_solution(1910120666231005500)
XLA Ops:
  0.8 1.9 %collective-permute-start = (bf16[16,3,512]{2,0,1:T(8,128)(2,1)S(1)}, bf16[16,3,512]{2,0,1:T(8,128)(2,1)S(1)}, u32[]{:S(2)}, u32[]{:S(2)}) collective-permute-start(bf16[16,3,512]{2,0,1:T(8,128)(2,1)S(1)} %slice.71), channel_id=1, source_target_pairs={{0,16},{16,32},{32,48},{48,64},{64,80},{80,96},{96,112},{112,128},... | collective-permute-start | bytes 147464 | tf_op jit(solution)/shard_map/ppermute | solution.py:148
  4.1 2.1 %collective-permute-done = bf16[16,3,512]{2,0,1:T(8,128)(2,1)S(1)} collective-permute-done((bf16[16,3,512]{2,0,1:T(8,128)(2,1)S(1)}, bf16[16,3,512]{2,0,1:T(8,128)(2,1)S(1)}, u32[]{:S(2)}, u32[]{:S(2)}) %collective-permute-start) | collective-permute-done | bytes 49184 | tf_op jit(solution)/shard_map/ppermute | solution.py:148
  6.8 4.4 %signal.1 = (f32[32,8,512]{2,1,0:T(8,128)}, f32[32,8,512]{2,1,0:T(8,128)}, f32[16,8,512]{2,1,0:T(8,128)}, bf16[16,16,512]{2,1,0:T(8,128)(2,1)}) custom-call(s32[1]{0:T(128)} %bitcast.2.ctx_ref, bf16[3,256,512]{2,1,0:T(8,128)(2,1)} %bitcast.135, bf16[3,16,512]{2,1,0:T(8,128)(2,1)} %bitcast.136, f32[3,7,512]{2,1,0:T(8,128)} %taps_ref.1, ...), custom_call_target="tpu_custom_call" | custom-call | tf_op jit(solution)/shard_map/signal/pallas_call | solution.py:158
  11.2 5.9 %all-to-all-start = ((bf16[16,16,512]{2,1,0:T(8,128)(2,1)}), bf16[16,16,512]{2,1,0:T(8,128)(2,1)S(1)}, u32[]{:S(2)}, u32[]{:S(2)}) async-start(bf16[16,16,512]{2,1,0:T(8,128)(2,1)} %get-tuple-element.12), calls=%async_computation | async-start | bytes 524288 | tf_op jit(solution)/shard_map/all_to_all | solution.py:179
  17.7 4.9 %all-to-all-done.recv_ref = bf16[16,16,512]{2,1,0:T(8,128)(2,1)S(1)} async-done(((bf16[16,16,512]{2,1,0:T(8,128)(2,1)}), bf16[16,16,512]{2,1,0:T(8,128)(2,1)S(1)}, u32[]{:S(2)}, u32[]{:S(2)}) %all-to-all-start) | async-done | bytes 262176 | tf_op jit(solution)/shard_map/all_to_all | solution.py:179
  23.2 4.8 %gate.1 = bf16[256,512]{1,0:T(8,128)(2,1)} custom-call(s32[2]{0:T(128)} %pad_add_fusion.pos_ref, f32[32,8,512]{2,1,0:T(8,128)} %get-tuple-element.9.sig_ref, f32[32,8,512]{2,1,0:T(8,128)} %get-tuple-element.10.q_ref, f32[16,8,512]{2,1,0:T(8,128)} %get-tuple-element.11.ends_ref, f32[16,512]{1,0:T(8,128)} %get-tuple-element.26.a_ref, ...), custom_call_target="tpu_custom_call" | custom-call | tf_op jit(solution)/shard_map/gate/pallas_call | solution.py:180
  28.0 3.6 %convolution_convert_fusion = bf16[256,4096]{1,0:T(8,128)(2,1)S(1)} fusion(bf16[256,512]{1,0:T(8,128)(2,1)} %gate.1, bf16[512,8192]{1,0:T(8,128)(2,1)} %param.9), kind=kOutput, calls=%fused_computation | convolution fusion | flops 1074790400 | bytes 6553600 | tf_op jit(solution)/shard_map/dot_general | solution.py:134
  31.6 3.5 %convolution_convert_fusion.1 = bf16[256,4096]{1,0:T(8,128)(2,1)S(1)} fusion(bf16[256,512]{1,0:T(8,128)(2,1)S(1)} %copy-done.1, bf16[512,8192]{1,0:T(8,128)(2,1)} %param.9), kind=kOutput, calls=%fused_computation.1 | convolution fusion | flops 1074790400 | bytes 6553600 | tf_op jit(solution)/shard_map/dot_general | solution.py:134
  35.1 2.0 %collective-permute-start.9 = (bf16[2,16,4096]{2,1,0:T(8,128)(2,1)S(1)}, bf16[2,16,4096]{2,1,0:T(8,128)(2,1)S(1)}, u32[]{:S(2)}, u32[]{:S(2)}) collective-permute-start(bf16[2,16,4096]{2,1,0:T(8,128)(2,1)S(1)} %get-tuple-element.23), channel_id=1, source_target_pairs={{0,1},{1,2},{2,3},{3,4},{4,5},{5,6},{6,7},{7,0},{8,9},{9,10},{10,1... | collective-permute-start | bytes 786440 | tf_op jit(solution)/shard_map/ppermute | solution.py:123
  37.1 4.0 %collective-permute-start.12 = (bf16[2,16,4096]{2,1,0:T(8,128)(2,1)S(1)}, bf16[2,16,4096]{2,1,0:T(8,128)(2,1)S(1)}, u32[]{:S(2)}, u32[]{:S(2)}) collective-permute-start(bf16[2,16,4096]{2,1,0:T(8,128)(2,1)S(1)} %get-tuple-element.24), channel_id=1, source_target_pairs={{0,7},{1,0},{2,1},{3,2},{4,3},{5,4},{6,5},{7,6},{8,15},{9,8},{10,9... | collective-permute-start | bytes 786440 | tf_op jit(solution)/shard_map/ppermute | solution.py:125
  41.3 3.2 %collective-permute-start.5 = (bf16[2,16,4096]{2,1,0:T(8,128)(2,1)S(1)}, bf16[2,16,4096]{2,1,0:T(8,128)(2,1)S(1)}, u32[]{:S(2)}, u32[]{:S(2)}) collective-permute-start(bf16[2,16,4096]{2,1,0:T(8,128)(2,1)S(1)} %get-tuple-element.18), channel_id=1, source_target_pairs={{0,7},{1,0},{2,1},{3,2},{4,3},{5,4},{6,5},{7,6},{8,15},{9,8},{10,9... | collective-permute-start | bytes 786440 | tf_op jit(solution)/shard_map/ppermute | solution.py:125
  44.5 3.3 %collective-permute-done.12 = bf16[2,16,4096]{2,1,0:T(8,128)(2,1)S(1)} collective-permute-done((bf16[2,16,4096]{2,1,0:T(8,128)(2,1)S(1)}, bf16[2,16,4096]{2,1,0:T(8,128)(2,1)S(1)}, u32[]{:S(2)}, u32[]{:S(2)}) %collective-permute-start.12) | collective-permute-done | bytes 262176 | tf_op jit(solution)/shard_map/ppermute | solution.py:125
  47.9 3.8 %collective-permute-start.13 = (bf16[2,16,4096]{2,1,0:T(8,128)(2,1)S(1)}, bf16[2,16,4096]{2,1,0:T(8,128)(2,1)S(1)}, u32[]{:S(2)}, u32[]{:S(2)}) collective-permute-start(bf16[2,16,4096]{2,1,0:T(8,128)(2,1)S(1)} %fusion.4), channel_id=1, source_target_pairs={{0,7},{1,0},{2,1},{3,2},{4,3},{5,4},{6,5},{7,6},{8,15},{9,8},{10,9... | collective-permute-start | bytes 786440 | tf_op jit(solution)/shard_map/ppermute | solution.py:125
  51.7 2.1 %collective-permute-done.1 = bf16[2,16,4096]{2,1,0:T(8,128)(2,1)S(1)} collective-permute-done((bf16[2,16,4096]{2,1,0:T(8,128)(2,1)S(1)}, bf16[2,16,4096]{2,1,0:T(8,128)(2,1)S(1)}, u32[]{:S(2)}, u32[]{:S(2)}) %collective-permute-start.1) | collective-permute-done | bytes 262176 | tf_op jit(solution)/shard_map/ppermute | solution.py:123
  54.0 4.9 %collective-permute-done.13 = bf16[2,16,4096]{2,1,0:T(8,128)(2,1)S(1)} collective-permute-done((bf16[2,16,4096]{2,1,0:T(8,128)(2,1)S(1)}, bf16[2,16,4096]{2,1,0:T(8,128)(2,1)S(1)}, u32[]{:S(2)}, u32[]{:S(2)}) %collective-permute-start.13) | collective-permute-done | bytes 262176 | tf_op jit(solution)/shard_map/ppermute | solution.py:125
  59.4 3.5 %collective-permute-start.14 = (bf16[2,16,4096]{2,1,0:T(8,128)(2,1)S(1)}, bf16[2,16,4096]{2,1,0:T(8,128)(2,1)S(1)}, u32[]{:S(2)}, u32[]{:S(2)}) collective-permute-start(bf16[2,16,4096]{2,1,0:T(8,128)(2,1)S(1)} %get-tuple-element.22), channel_id=1, source_target_pairs={{0,7},{1,0},{2,1},{3,2},{4,3},{5,4},{6,5},{7,6},{8,15},{9,8},{10,9... | collective-permute-start | bytes 786440 | tf_op jit(solution)/shard_map/ppermute | solution.py:125
  63.7 3.2 %collective-permute-start.6 = (bf16[2,16,4096]{2,1,0:T(8,128)(2,1)S(1)}, bf16[2,16,4096]{2,1,0:T(8,128)(2,1)S(1)}, u32[]{:S(2)}, u32[]{:S(2)}) collective-permute-start(bf16[2,16,4096]{2,1,0:T(8,128)(2,1)S(1)} %get-tuple-element.16), channel_id=1, source_target_pairs={{0,7},{1,0},{2,1},{3,2},{4,3},{5,4},{6,5},{7,6},{8,15},{9,8},{10,9... | collective-permute-start | bytes 786440 | tf_op jit(solution)/shard_map/ppermute | solution.py:125
  66.9 3.0 %collective-permute-done.10 = bf16[2,16,4096]{2,1,0:T(8,128)(2,1)S(1)} collective-permute-done((bf16[2,16,4096]{2,1,0:T(8,128)(2,1)S(1)}, bf16[2,16,4096]{2,1,0:T(8,128)(2,1)S(1)}, u32[]{:S(2)}, u32[]{:S(2)}) %collective-permute-start.10) | collective-permute-done | bytes 262176 | tf_op jit(solution)/shard_map/ppermute | solution.py:123
  70.1 3.0 %collective-permute-start.11 = (bf16[2,16,4096]{2,1,0:T(8,128)(2,1)S(1)}, bf16[2,16,4096]{2,1,0:T(8,128)(2,1)S(1)}, u32[]{:S(2)}, u32[]{:S(2)}) collective-permute-start(bf16[2,16,4096]{2,1,0:T(8,128)(2,1)S(1)} %get-tuple-element.19), channel_id=1, source_target_pairs={{0,1},{1,2},{2,3},{3,4},{4,5},{5,6},{6,7},{7,0},{8,9},{9,10},{10,1... | collective-permute-start | bytes 786440 | tf_op jit(solution)/shard_map/ppermute | solution.py:123
  75.7 2.8 %collective-permute-start.4 = (bf16[2,16,4096]{2,1,0:T(8,128)(2,1)S(1)}, bf16[2,16,4096]{2,1,0:T(8,128)(2,1)S(1)}, u32[]{:S(2)}, u32[]{:S(2)}) collective-permute-start(bf16[2,16,4096]{2,1,0:T(8,128)(2,1)S(1)} %get-tuple-element.13), channel_id=1, source_target_pairs={{0,1},{1,2},{2,3},{3,4},{4,5},{5,6},{6,7},{7,0},{8,9},{9,10},{10,1... | collective-permute-start | bytes 786440 | tf_op jit(solution)/shard_map/ppermute | solution.py:123
  79.2 2.0 %collective-permute-done.11 = bf16[2,16,4096]{2,1,0:T(8,128)(2,1)S(1)} collective-permute-done((bf16[2,16,4096]{2,1,0:T(8,128)(2,1)S(1)}, bf16[2,16,4096]{2,1,0:T(8,128)(2,1)S(1)}, u32[]{:S(2)}, u32[]{:S(2)}) %collective-permute-start.11) | collective-permute-done | bytes 262176 | tf_op jit(solution)/shard_map/ppermute | solution.py:123
  81.4 2.8 %collective-permute-start.16 = (bf16[16,4096]{1,0:T(8,128)(2,1)S(1)}, bf16[16,4096]{1,0:T(8,128)(2,1)S(1)}, u32[]{:S(2)}, u32[]{:S(2)}) collective-permute-start(bf16[16,4096]{1,0:T(8,128)(2,1)S(1)} %fusion.17), channel_id=1, source_target_pairs={{0,8},{1,9},{2,10},{3,11},{4,12},{5,13},{6,14},{7,15},{8,0},{9,1},... | collective-permute-start | bytes 393224 | tf_op jit(solution)/shard_map/ppermute | solution.py:137
  86.2 2.8 %collective-permute-start.8 = (bf16[16,4096]{1,0:T(8,128)(2,1)S(1)}, bf16[16,4096]{1,0:T(8,128)(2,1)S(1)}, u32[]{:S(2)}, u32[]{:S(2)}) collective-permute-start(bf16[16,4096]{1,0:T(8,128)(2,1)S(1)} %fusion.16), channel_id=1, source_target_pairs={{0,8},{1,9},{2,10},{3,11},{4,12},{5,13},{6,14},{7,15},{8,0},{9,1},... | collective-permute-start | bytes 393224 | tf_op jit(solution)/shard_map/ppermute | solution.py:137
  89.0 3.7 %collective-permute-done.8 = bf16[16,4096]{1,0:T(8,128)(2,1)S(1)} collective-permute-done((bf16[16,4096]{1,0:T(8,128)(2,1)S(1)}, bf16[16,4096]{1,0:T(8,128)(2,1)S(1)}, u32[]{:S(2)}, u32[]{:S(2)}) %collective-permute-start.8) | collective-permute-done | bytes 131104 | tf_op jit(solution)/shard_map/ppermute | solution.py:137
  (40 shorter events, 12.2 us)
Async XLA Ops:
  0.8 5.4 %collective-permute-start = (bf16[16,3,512]{2,0,1:T(8,128)(2,1)S(1)}, bf16[16,3,512]{2,0,1:T(8,128)(2,1)S(1)}, u32[]{:S(2)}, u32[]{:S(2)}) collective-permute-start(bf16[16,3,512]{2,0,1:T(8,128)(2,1)S(1)} %slice.71), channel_id=1, source_target_pairs={{0,16},{16,32},{32,48},{48,64},{64,80},{80,96},{96,112},{112,128},... | collective-permute-start | bytes 147464 | tf_op jit(solution)/shard_map/ppermute | solution.py:148
  6.2 0.6 copy-start.2
  11.2 11.3 %all-to-all-start = ((bf16[16,16,512]{2,1,0:T(8,128)(2,1)}), bf16[16,16,512]{2,1,0:T(8,128)(2,1)S(1)}, u32[]{:S(2)}, u32[]{:S(2)}) async-start(bf16[16,16,512]{2,1,0:T(8,128)(2,1)} %get-tuple-element.12), calls=%async_computation | async-start | bytes 524288 | tf_op jit(solution)/shard_map/all_to_all | solution.py:179
  22.5 0.7 copy-start
  28.0 3.6 %copy-start.1 = (bf16[256,512]{1,0:T(8,128)(2,1)S(1)}, bf16[256,512]{1,0:T(8,128)(2,1)}, u32[]{:S(2)}) copy-start(bf16[256,512]{1,0:T(8,128)(2,1)} %gate.1) | copy-start | bytes 786436
  35.1 18.8 %collective-permute-start.9 = (bf16[2,16,4096]{2,1,0:T(8,128)(2,1)S(1)}, bf16[2,16,4096]{2,1,0:T(8,128)(2,1)S(1)}, u32[]{:S(2)}, u32[]{:S(2)}) collective-permute-start(bf16[2,16,4096]{2,1,0:T(8,128)(2,1)S(1)} %get-tuple-element.23), channel_id=1, source_target_pairs={{0,1},{1,2},{2,3},{3,4},{4,5},{5,6},{6,7},{7,0},{8,9},{9,10},{10,1... | collective-permute-start | bytes 786440 | tf_op jit(solution)/shard_map/ppermute | solution.py:123
  37.1 10.7 %collective-permute-start.12 = (bf16[2,16,4096]{2,1,0:T(8,128)(2,1)S(1)}, bf16[2,16,4096]{2,1,0:T(8,128)(2,1)S(1)}, u32[]{:S(2)}, u32[]{:S(2)}) collective-permute-start(bf16[2,16,4096]{2,1,0:T(8,128)(2,1)S(1)} %get-tuple-element.24), channel_id=1, source_target_pairs={{0,7},{1,0},{2,1},{3,2},{4,3},{5,4},{6,5},{7,6},{8,15},{9,8},{10,9... | collective-permute-start | bytes 786440 | tf_op jit(solution)/shard_map/ppermute | solution.py:125
  41.2 12.6 %collective-permute-start.1 = (bf16[2,16,4096]{2,1,0:T(8,128)(2,1)S(1)}, bf16[2,16,4096]{2,1,0:T(8,128)(2,1)S(1)}, u32[]{:S(2)}, u32[]{:S(2)}) collective-permute-start(bf16[2,16,4096]{2,1,0:T(8,128)(2,1)S(1)} %get-tuple-element.17), channel_id=1, source_target_pairs={{0,1},{1,2},{2,3},{3,4},{4,5},{5,6},{6,7},{7,0},{8,9},{9,10},{10,1... | collective-permute-start | bytes 786440 | tf_op jit(solution)/shard_map/ppermute | solution.py:123
  41.3 21.6 %collective-permute-start.5 = (bf16[2,16,4096]{2,1,0:T(8,128)(2,1)S(1)}, bf16[2,16,4096]{2,1,0:T(8,128)(2,1)S(1)}, u32[]{:S(2)}, u32[]{:S(2)}) collective-permute-start(bf16[2,16,4096]{2,1,0:T(8,128)(2,1)S(1)} %get-tuple-element.18), channel_id=1, source_target_pairs={{0,7},{1,0},{2,1},{3,2},{4,3},{5,4},{6,5},{7,6},{8,15},{9,8},{10,9... | collective-permute-start | bytes 786440 | tf_op jit(solution)/shard_map/ppermute | solution.py:125
  47.9 11.0 %collective-permute-start.13 = (bf16[2,16,4096]{2,1,0:T(8,128)(2,1)S(1)}, bf16[2,16,4096]{2,1,0:T(8,128)(2,1)S(1)}, u32[]{:S(2)}, u32[]{:S(2)}) collective-permute-start(bf16[2,16,4096]{2,1,0:T(8,128)(2,1)S(1)} %fusion.4), channel_id=1, source_target_pairs={{0,7},{1,0},{2,1},{3,2},{4,3},{5,4},{6,5},{7,6},{8,15},{9,8},{10,9... | collective-permute-start | bytes 786440 | tf_op jit(solution)/shard_map/ppermute | solution.py:125
  53.9 9.6 %collective-permute-start.2 = (bf16[2,16,4096]{2,1,0:T(8,128)(2,1)S(1)}, bf16[2,16,4096]{2,1,0:T(8,128)(2,1)S(1)}, u32[]{:S(2)}, u32[]{:S(2)}) collective-permute-start(bf16[2,16,4096]{2,1,0:T(8,128)(2,1)S(1)} %fusion.11), channel_id=1, source_target_pairs={{0,1},{1,2},{2,3},{3,4},{4,5},{5,6},{6,7},{7,0},{8,9},{9,10},{10,1... | collective-permute-start | bytes 786440 | tf_op jit(solution)/shard_map/ppermute | solution.py:123
  59.0 10.9 %collective-permute-start.10 = (bf16[2,16,4096]{2,1,0:T(8,128)(2,1)S(1)}, bf16[2,16,4096]{2,1,0:T(8,128)(2,1)S(1)}, u32[]{:S(2)}, u32[]{:S(2)}) collective-permute-start(bf16[2,16,4096]{2,1,0:T(8,128)(2,1)S(1)} %get-tuple-element.21), channel_id=1, source_target_pairs={{0,1},{1,2},{2,3},{3,4},{4,5},{5,6},{6,7},{7,0},{8,9},{9,10},{10,1... | collective-permute-start | bytes 786440 | tf_op jit(solution)/shard_map/ppermute | solution.py:123
  59.4 10.5 %collective-permute-start.14 = (bf16[2,16,4096]{2,1,0:T(8,128)(2,1)S(1)}, bf16[2,16,4096]{2,1,0:T(8,128)(2,1)S(1)}, u32[]{:S(2)}, u32[]{:S(2)}) collective-permute-start(bf16[2,16,4096]{2,1,0:T(8,128)(2,1)S(1)} %get-tuple-element.22), channel_id=1, source_target_pairs={{0,7},{1,0},{2,1},{3,2},{4,3},{5,4},{6,5},{7,6},{8,15},{9,8},{10,9... | collective-permute-start | bytes 786440 | tf_op jit(solution)/shard_map/ppermute | solution.py:125
  63.6 11.9 %collective-permute-start.3 = (bf16[2,16,4096]{2,1,0:T(8,128)(2,1)S(1)}, bf16[2,16,4096]{2,1,0:T(8,128)(2,1)S(1)}, u32[]{:S(2)}, u32[]{:S(2)}) collective-permute-start(bf16[2,16,4096]{2,1,0:T(8,128)(2,1)S(1)} %get-tuple-element.15), channel_id=1, source_target_pairs={{0,1},{1,2},{2,3},{3,4},{4,5},{5,6},{6,7},{7,0},{8,9},{9,10},{10,1... | collective-permute-start | bytes 786440 | tf_op jit(solution)/shard_map/ppermute | solution.py:123
  63.7 11.8 %collective-permute-start.6 = (bf16[2,16,4096]{2,1,0:T(8,128)(2,1)S(1)}, bf16[2,16,4096]{2,1,0:T(8,128)(2,1)S(1)}, u32[]{:S(2)}, u32[]{:S(2)}) collective-permute-start(bf16[2,16,4096]{2,1,0:T(8,128)(2,1)S(1)} %get-tuple-element.16), channel_id=1, source_target_pairs={{0,7},{1,0},{2,1},{3,2},{4,3},{5,4},{6,5},{7,6},{8,15},{9,8},{10,9... | collective-permute-start | bytes 786440 | tf_op jit(solution)/shard_map/ppermute | solution.py:125
  70.1 11.1 %collective-permute-start.11 = (bf16[2,16,4096]{2,1,0:T(8,128)(2,1)S(1)}, bf16[2,16,4096]{2,1,0:T(8,128)(2,1)S(1)}, u32[]{:S(2)}, u32[]{:S(2)}) collective-permute-start(bf16[2,16,4096]{2,1,0:T(8,128)(2,1)S(1)} %get-tuple-element.19), channel_id=1, source_target_pairs={{0,1},{1,2},{2,3},{3,4},{4,5},{5,6},{6,7},{7,0},{8,9},{9,10},{10,1... | collective-permute-start | bytes 786440 | tf_op jit(solution)/shard_map/ppermute | solution.py:123
  73.0 8.2 %collective-permute-start.15 = (bf16[2,16,4096]{2,1,0:T(8,128)(2,1)S(1)}, bf16[2,16,4096]{2,1,0:T(8,128)(2,1)S(1)}, u32[]{:S(2)}, u32[]{:S(2)}) collective-permute-start(bf16[2,16,4096]{2,1,0:T(8,128)(2,1)S(1)} %get-tuple-element.20), channel_id=1, source_target_pairs={{0,7},{1,0},{2,1},{3,2},{4,3},{5,4},{6,5},{7,6},{8,15},{9,8},{10,9... | collective-permute-start | bytes 786440 | tf_op jit(solution)/shard_map/ppermute | solution.py:125
  75.7 10.3 %collective-permute-start.4 = (bf16[2,16,4096]{2,1,0:T(8,128)(2,1)S(1)}, bf16[2,16,4096]{2,1,0:T(8,128)(2,1)S(1)}, u32[]{:S(2)}, u32[]{:S(2)}) collective-permute-start(bf16[2,16,4096]{2,1,0:T(8,128)(2,1)S(1)} %get-tuple-element.13), channel_id=1, source_target_pairs={{0,1},{1,2},{2,3},{3,4},{4,5},{5,6},{6,7},{7,0},{8,9},{9,10},{10,1... | collective-permute-start | bytes 786440 | tf_op jit(solution)/shard_map/ppermute | solution.py:123
  78.5 7.6 %collective-permute-start.7 = (bf16[2,16,4096]{2,1,0:T(8,128)(2,1)S(1)}, bf16[2,16,4096]{2,1,0:T(8,128)(2,1)S(1)}, u32[]{:S(2)}, u32[]{:S(2)}) collective-permute-start(bf16[2,16,4096]{2,1,0:T(8,128)(2,1)S(1)} %get-tuple-element.14), channel_id=1, source_target_pairs={{0,7},{1,0},{2,1},{3,2},{4,3},{5,4},{6,5},{7,6},{8,15},{9,8},{10,9... | collective-permute-start | bytes 786440 | tf_op jit(solution)/shard_map/ppermute | solution.py:125
  81.4 7.6 %collective-permute-start.16 = (bf16[16,4096]{1,0:T(8,128)(2,1)S(1)}, bf16[16,4096]{1,0:T(8,128)(2,1)S(1)}, u32[]{:S(2)}, u32[]{:S(2)}) collective-permute-start(bf16[16,4096]{1,0:T(8,128)(2,1)S(1)} %fusion.17), channel_id=1, source_target_pairs={{0,8},{1,9},{2,10},{3,11},{4,12},{5,13},{6,14},{7,15},{8,0},{9,1},... | collective-permute-start | bytes 393224 | tf_op jit(solution)/shard_map/ppermute | solution.py:137
  86.2 6.6 %collective-permute-start.8 = (bf16[16,4096]{1,0:T(8,128)(2,1)S(1)}, bf16[16,4096]{1,0:T(8,128)(2,1)S(1)}, u32[]{:S(2)}, u32[]{:S(2)}) collective-permute-start(bf16[16,4096]{1,0:T(8,128)(2,1)S(1)} %fusion.16), channel_id=1, source_target_pairs={{0,8},{1,9},{2,10},{3,11},{4,12},{5,13},{6,14},{7,15},{8,0},{9,1},... | collective-permute-start | bytes 393224 | tf_op jit(solution)/shard_map/ppermute | solution.py:137

commit v2 on v0

v2 whole, which is shorter than its diff:
```python
import functools

import jax
import jax.numpy as jnp
from jax import lax
from jax.experimental import pallas as pl
from jax.experimental.pallas import tpu as pltpu
from jax.sharding import PartitionSpec as P

TAPS = 7
MODES = 16
SUB = 8
LANES = 128
NZ = 8
HALO = 16
BACK = TAPS - 1

f32 = jnp.float32
bf16 = jnp.bfloat16
VMEM = pltpu.VMEM


def one_hot(rows, cols, pick):
    row = lax.broadcasted_iota(jnp.int32, (rows, LANES), 0)
    want = pick(row)
    col = lax.broadcasted_iota(jnp.int32, (rows, LANES), 1)
    tiles = [jnp.where(want == col + c, 1.0, 0.0).astype(bf16) for c in range(0, cols, LANES)]
    return jnp.concatenate(tiles, axis=1)


def spread_matrix(rows):
    run = rows // SUB
    return one_hot((run + BACK) * SUB, rows, lambda r: run * (r % SUB) + r // SUB - BACK)


def edge_rows(halo_ref, branch):
    first = one_hot(BACK * SUB, LANES, lambda r: jnp.where(r % SUB == 0, r // SUB + HALO - BACK, -1))[:, :HALO]
    return jnp.dot(first, halo_ref[branch], preferred_element_type=f32)


def fir(taps_ref, branch, read, lanes, times, emit):
    taps = [jnp.broadcast_to(taps_ref[branch, j : j + 1, lanes], (SUB, LANES)) for j in range(TAPS)]
    window = [read(times[0] + e) for e in range(BACK)][::-1]
    for t in times:
        window = [read(t + BACK)] + window
        terms = [taps[j] * window[j] for j in range(TAPS)]
        while len(terms) > 1:
            terms = [terms[i] + terms[i + 1] for i in range(0, len(terms) - 1, 2)] + terms[len(terms) // 2 * 2 :]
        emit(t, terms[0])
        window = window[:BACK]


def at(t):
    return slice(t * SUB, (t + 1) * SUB)


def lane_loop(chans, group):
    def step(g, _):
        group(pl.ds(pl.multiple_of(g * LANES, LANES), LANES))
        return 0

    lax.fori_loop(0, chans // LANES, step, 0)


def wide_rows(ref, lanes, modes):
    return [jnp.broadcast_to(ref[m : m + 1, lanes], (SUB, LANES)) for m in modes]


def run_states(decay, state, read, times):
    for t in times:
        now = read(t)
        state = [now] * len(decay) if state is None else [d * s + now for d, s in zip(decay, state)]
    return state


def bulk_kernel(
    tokens, x_hbm, taps_hbm, rate_hbm, zero_ref, head_ref, sig_ref, late_ref, taps_ref, rate_ref, x_ref, px_ref, sems
):
    rows = x_ref.shape[1]
    run = rows // SUB
    copies = {b: pltpu.make_async_copy(x_hbm.at[b], x_ref.at[b], sems.at[b]) for b in (1, 2, 0)}
    small = [
        pltpu.make_async_copy(taps_hbm, taps_ref, sems.at[3]),
        pltpu.make_async_copy(rate_hbm, rate_ref, sems.at[4]),
    ]
    for c in [*copies.values(), *small]:
        c.start()
    move = spread_matrix(rows)
    for b, c in copies.items():
        c.wait()
        moved = jnp.dot(move, x_ref[b], preferred_element_type=f32)
        if b == 0:
            zero_ref[...] = moved
        else:
            px_ref[b - 1] = moved
            head_ref[b - 1] = moved[: 2 * BACK * SUB]
    for c in small:
        c.wait()

    def group(lanes):
        def put(t, v):
            sig_ref[at(t), lanes] = v

        def mul(t, v):
            sig_ref[at(t), lanes] = sig_ref[at(t), lanes] * v

        late = range(BACK, run)
        fir(taps_ref, 1, lambda e: px_ref[0, at(e), lanes], lanes, late, put)
        fir(taps_ref, 2, lambda e: px_ref[1, at(e), lanes], lanes, late, mul)
        decay = [jnp.exp(r * (-1.0 / tokens)) for r in wide_rows(rate_ref, lanes, range(MODES))]
        state = run_states(decay, None, lambda t: sig_ref[at(t), lanes], late)
        for m in range(MODES):
            late_ref[m, :, lanes] = state[m]

    lane_loop(x_ref.shape[2], group)


def edge_kernel(
    rows, tokens, head_ref, halo_ref, taps_ref, rate_ref, late_ref, early_ref, ends_ref, send_ref, edges, faded
):
    run = rows // SUB
    n_ctx = send_ref.shape[0]
    for b in (1, 2):
        edges[b - 1] = head_ref[b - 1, : BACK * SUB] + edge_rows(halo_ref, b)
    me = lax.axis_index("ctx")
    below = (SUB - 1 - lax.broadcasted_iota(jnp.int32, (SUB, LANES), 0)).astype(f32) * (-run / tokens)

    def group(lanes):
        def put(t, v):
            early_ref[at(t), lanes] = v

        def mul(t, v):
            early_ref[at(t), lanes] = early_ref[at(t), lanes] * v

        for b, emit in ((1, put), (2, mul)):
            fir(
                taps_ref,
                b,
                lambda e, b=b: edges[b - 1, at(e), lanes] if e < BACK else head_ref[b - 1, at(e), lanes],
                lanes,
                range(BACK),
                emit,
            )
        rate = wide_rows(rate_ref, lanes, range(MODES))
        decay = [jnp.exp(r * (-1.0 / tokens)) for r in rate]
        state = run_states(decay, None, lambda t: early_ref[at(t), lanes], range(BACK))
        for m in range(MODES):
            end = late_ref[m, :, lanes] + state[m] * jnp.exp(rate[m] * (-(run - BACK) / tokens))
            ends_ref[m, :, lanes] = end
            faded[m] = end * jnp.exp(rate[m] * below)
        total = jnp.sum(faded[...], axis=1)
        whole = jnp.exp(rate_ref[:, lanes] * (-rows / tokens))
        for d in range(n_ctx):
            send_ref[d, :, lanes] = jnp.where(d > me, total, 0.0).astype(bf16)
            total = jnp.where(d > me, total * whole, total)

    lane_loop(head_ref.shape[2], group)


def inner_kernel(
    tokens,
    px_ref,
    halo_ref,
    taps_ref,
    rate_ref,
    coef_ref,
    sig_ref,
    early_ref,
    ends_ref,
    q_ref,
    y_ref,
    lead_ref,
    turn_ref,
    edges,
):
    rows = q_ref.shape[0]
    run = rows // SUB
    edges[...] = px_ref[: BACK * SUB] + edge_rows(halo_ref, 0)
    sub = lax.broadcasted_iota(jnp.int32, (SUB, LANES), 0)
    sub_time = (sub * run + 1).astype(f32) * (-1.0 / tokens)

    def group(lanes):
        def put(t, v):
            q_ref[at(t), lanes] = v

        def signal(t):
            return early_ref[at(t), lanes] if t < BACK else sig_ref[at(t), lanes]

        fir(
            taps_ref,
            0,
            lambda e: edges[at(e), lanes] if e < BACK else px_ref[at(e), lanes],
            lanes,
            range(run),
            put,
        )
        for first in range(0, MODES, 8):
            modes = range(first, first + 8)
            coef = wide_rows(coef_ref, lanes, modes)
            rate = wide_rows(rate_ref, lanes, modes)
            decay = [jnp.exp(r * (-1.0 / tokens)) for r in rate]
            state = []
            for i, m in enumerate(modes):
                lead_ref[m, :, lanes] = coef[i] * jnp.exp(rate[i] * sub_time)
                s = ends_ref[m, :, lanes]
                for by in (1, 2, 4):
                    moved = jnp.where(sub >= by, pltpu.roll(s, by, 0), 0.0)
                    s = s + moved * jnp.exp(rate[i] * (-by * run / tokens))
                state.append(jnp.where(sub >= 1, pltpu.roll(s, 1, 0), 0.0))
            for t in range(run):
                state = run_states(decay, state, signal, [t])
                terms = [c * s for c, s in zip(coef, state)]
                while len(terms) > 1:
                    terms = [terms[i] + terms[i + 1] for i in range(0, len(terms), 2)]
                y_ref[at(t), lanes] = terms[0] if first == 0 else y_ref[at(t), lanes] + terms[0]

    lane_loop(q_ref.shape[1], group)
    tp = lax.axis_index("tp")
    half, z = tp // NZ, tp % NZ

    def natural(o):
        block = ((half + o // (NZ * 16)) % 2) * NZ + (z + o // 16) % NZ
        n = block * 16 + o % 16
        return (n % run) * SUB + n // run

    turn_ref[...] = one_hot(rows, rows, natural)


def column_copies(weight_hbm, weight, sems, base):
    tiles = sems.shape[0]
    tile = weight.shape[1] // tiles
    copies = []
    for i in range(tiles):
        here = slice(i * tile, (i + 1) * tile)
        there = slice(base + i * tile, base + (i + 1) * tile)
        copies.append((here, pltpu.make_async_copy(weight_hbm.at[:, there], weight.at[:, here], sems.at[i])))
    for _, copy in copies:
        copy.start()
    return copies


def times(left, copies, weight, out_ref):
    for here, copy in copies:
        copy.wait()
        out_ref[:, here] = jnp.dot(left, weight[:, here], preferred_element_type=f32).astype(bf16)


def gate_kernel(
    tokens, weight_hbm, recv_ref, rate_ref, lead_ref, y_ref, q_ref, turn_ref, gated_ref, part_ref, flat, weight, sems
):
    copies = column_copies(weight_hbm, weight, sems, 0)
    n_ctx = recv_ref.shape[0]
    run = y_ref.shape[0] // SUB

    def group(lanes):
        start = recv_ref[0, :, lanes].astype(f32)
        for p in range(1, n_ctx):
            start = start + recv_ref[p, :, lanes].astype(f32)
        state = [jnp.broadcast_to(start[m : m + 1], (SUB, LANES)) * lead_ref[m, :, lanes] for m in range(MODES)]
        decay = [jnp.exp(r * (-1.0 / tokens)) for r in wide_rows(rate_ref, lanes, range(MODES))]
        for t in range(run):
            terms = [y_ref[at(t), lanes]] + state
            while len(terms) > 1:
                terms = [terms[i] + terms[i + 1] for i in range(0, len(terms) - 1, 2)] + terms[len(terms) // 2 * 2 :]
            flat[at(t), lanes] = terms[0] * q_ref[at(t), lanes]
            if t < run - 1:
                state = [d * s for d, s in zip(decay, state)]

    lane_loop(y_ref.shape[1], group)
    gated = jnp.dot(turn_ref[...], flat[...].astype(bf16), preferred_element_type=f32).astype(bf16)
    gated_ref[...] = gated
    times(gated, copies, weight, part_ref)


def project_kernel(base, weight_hbm, gated_ref, part_ref, weight, sems):
    copies = column_copies(weight_hbm, weight, sems, base)
    times(gated_ref[...], copies, weight, part_ref)


def z_pairs(by):
    return [(h * NZ + z, h * NZ + (z + by) % NZ) for h in range(2) for z in range(NZ)]


def half_pairs():
    return [(i, (i + NZ) % (2 * NZ)) for i in range(2 * NZ)]


def ring(blocks, more_left):
    rights, lefts = (NZ // 2 - 1, NZ // 2) if more_left else (NZ // 2, NZ // 2 - 1)
    right = blocks[rights]
    left = blocks[-lefts % NZ]
    for s in range(NZ // 2):
        if s < rights:
            right = lax.ppermute(right, "tp", z_pairs(1))
        if s < lefts:
            left = lax.ppermute(left, "tp", z_pairs(-1))
        if s < rights - 1:
            right = (right.astype(f32) + blocks[rights - 1 - s].astype(f32)).astype(bf16)
        if s < lefts - 1:
            left = (left.astype(f32) + blocks[-(lefts - 1 - s) % NZ].astype(f32)).astype(bf16)
    return right.astype(f32) + left.astype(f32) + blocks[0].astype(f32)


def reduce_columns(part, more_left):
    part = part.reshape(2, NZ, 16, -1)
    both = ring([part[:, k] for k in range(NZ)], more_left)
    other = lax.ppermute(both[1].astype(bf16), "tp", half_pairs())
    return (both[0] + other.astype(f32)).astype(bf16)


def call(kernel, outs, scratch, name, flops, *args, far=()):
    in_specs = [pl.BlockSpec(memory_space=pl.ANY)] * len(far) + [pl.BlockSpec(memory_space=VMEM)] * len(args)
    args = [pltpu.with_memory_space_constraint(x, pltpu.HBM) for x in far] + [
        pltpu.with_memory_space_constraint(x, VMEM) for x in args
    ]
    return pl.pallas_call(
        kernel,
        in_specs=in_specs,
        out_specs=[pl.BlockSpec(memory_space=VMEM)] * len(outs),
        out_shape=[VMEM(s, d) for s, d in outs],
        scratch_shapes=[s if not isinstance(s, tuple) else VMEM(*s) for s in scratch],
        compiler_params=pltpu.CompilerParams(vmem_limit_bytes=16 * 2**20),
        cost_estimate=pl.CostEstimate(flops=flops, bytes_accessed=4 * 2**20, transcendentals=0),
        name=name,
    )(*args)


def local(features, short_filter, decay_rate, residue, out_weight):
    rows, branches, chans = features.shape
    n_ctx = lax.axis_size("ctx")
    tokens = rows * n_ctx
    run = rows // SUB
    halo = lax.ppermute(features[rows - HALO :], "ctx", [(i, i + 1) for i in range(n_ctx - 1)])
    halo = jnp.transpose(halo, (1, 0, 2))
    x = jnp.transpose(features, (1, 0, 2))
    wide = ((rows, chans), f32)
    states = ((MODES, SUB, chans), f32)
    moved = ((run + BACK) * SUB, chans)
    head = 2 * BACK * SUB
    zero, heads, sig, late, taps, rate = call(
        functools.partial(bulk_kernel, tokens),
        [(moved, f32), ((2, head, chans), f32), wide, states, (short_filter.shape, f32), (decay_rate.shape, f32)],
        [((branches, rows, chans), bf16), ((2, *moved), f32), pltpu.SemaphoreType.DMA((5,))],
        "bulk",
        4 * rows * chans * MODES,
        far=(x, short_filter, decay_rate),
    )
    early, ends, send = call(
        functools.partial(edge_kernel, rows, tokens),
        [((BACK * SUB, chans), f32), states, ((n_ctx, MODES, chans), bf16)],
        [((2, BACK * SUB, chans), f32), ((MODES, SUB, LANES), f32)],
        "edge",
        rows * chans * MODES,
        heads,
        halo,
        taps,
        rate,
        late,
    )
    recv = lax.all_to_all(send, "ctx", 0, 0, tiled=True)
    late_rate, late_residue, _ = lax.optimization_barrier((decay_rate, residue, early))
    coef = late_residue * jnp.sqrt(1.0 / tokens - jnp.expm1(late_rate * (-2.0 / tokens)))
    q, y, lead, turn = call(
        functools.partial(inner_kernel, tokens),
        [wide, wide, states, ((rows, rows), bf16)],
        [((BACK * SUB, chans), f32)],
        "inner",
        8 * rows * chans * MODES,
        zero,
        halo,
        taps,
        rate,
        coef,
        sig,
        early,
        ends,
    )
    cols = out_weight.shape[1] // 2
    stream = [((chans, cols), bf16), pltpu.SemaphoreType.DMA((8,))]
    gated, first = call(
        functools.partial(gate_kernel, tokens),
        [((rows, chans), bf16), ((rows, cols), bf16)],
        [wide, *stream],
        "gate",
        2 * rows * chans * cols,
        recv,
        rate,
        lead,
        y,
        q,
        turn,
        far=(out_weight,),
    )
    (second,) = call(
        functools.partial(project_kernel, cols),
        [((rows, cols), bf16)],
        stream,
        "project",
        2 * rows * chans * cols,
        gated,
        far=(out_weight,),
    )
    out = [reduce_columns(first, False), reduce_columns(second, True)]
    return jnp.concatenate(out, axis=1)


def solution(mesh):
    in_specs = (
        P("ctx", None, "tp"),
        P(None, None, "tp"),
        P(None, "tp"),
        P(None, "tp"),
        P("tp", None),
    )
    out_specs = P(("ctx", "tp"), None)
    return jax.shard_map(local, mesh=mesh, in_specs=in_specs, out_specs=out_specs, check_vma=False)
```

time: 381 us -> 81.7 us (0.21)
  waiting for transfers between devices: 270 us -> 25.4 us
  starting transfers between devices: 57.4 us -> 40.3 us
  matrix products: 15.7 us -> 0 us
  other arithmetic: 16.5 us -> 1.6 us
  between operations: 13.6 us -> 0.19 us
  Pallas kernels: 0 us -> 13 us
  local copies, waits for them, and re-layouts: 6.71 us -> 0.92 us
    reduce_scatter x1 -> x0, waiting for transfers between devices: 235 us -> none  [local(): lax.psum_scatter(jnp.dot(gated, out_weight, preferred_element_type=jnp.fl...]
    ppermute x16 -> x17, starting transfers between devices: 57.4 us -> 34.4 us  [the longest x7 24 us: ring(): left = lax.ppermute(left, 'tp', z_pairs(-1))]
    dot_general x4 -> x0, matrix products: 15.7 us -> none  [the longest x1 7.71 us: local(): jnp.dot(gated, out_weight, preferred_element_type=jnp.float32)]
    ppermute x16 -> x17, waiting for transfers between devices: 35.4 us -> 22 us  [the longest x7 11.6 us: ring(): right = lax.ppermute(right, 'tp', z_pairs(1))]
    pallas_call x0 -> x5, Pallas kernels: none -> 13 us  [call(): pl.pallas_call(kernel, in_specs=in_specs, out_specs=[pl.BlockSpec(memory_...]
    all_to_all x0 -> x1, starting transfers between devices: none -> 5.96 us  [local(): recv = lax.all_to_all(send, 'ctx', 0, 0, tiled=True)]
    add x2, other arithmetic: 4.23 us -> 0.18 us  [ring(): return right.astype(f32) + left.astype(f32) + blocks[0].astype(f32)]
  transfers between devices with their start and end apart: 17 -> 18, of which waited for: 17 -> 10; matrix products, arithmetic and copies ran while one was open for 1% -> 1% of each run, Pallas kernels for 0% -> 10%
where the time goes in v2:
time: 81.7 us; the launch traced here: 81.5 us
  starting transfers between devices  40.3 us (49%)
  waiting for transfers between devices  25.4 us (31%)
  Pallas kernels  13 us (16%)
  other arithmetic  1.6 us (2%)
  local copies, waits for them, and re-layouts  0.92 us (1%)
    ppermute x7, starting transfers between devices, ring(): left = lax.ppermute(left, 'tp', z_pairs(-1))  24 us
    pallas_call x5, Pallas kernels, call(): pl.pallas_call(kernel, in_specs=in_specs, out_specs=[pl.BlockSpec(memory_...  13 us
    ppermute x7, waiting for transfers between devices, ring(): right = lax.ppermute(right, 'tp', z_pairs(1))  11.6 us
    all_to_all x1, starting transfers between devices, local(): recv = lax.all_to_all(send, 'ctx', 0, 0, tiled=True)  5.96 us
    ppermute x7, waiting for transfers between devices, ring(): left = lax.ppermute(left, 'tp', z_pairs(-1))  5.73 us
    ppermute x2, starting transfers between devices, reduce_columns(): other = lax.ppermute(both[1].astype(bf16), 'tp', half_pairs())  5.61 us
    ppermute x2, waiting for transfers between devices, reduce_columns(): other = lax.ppermute(both[1].astype(bf16), 'tp', half_pairs())  3.72 us
    all_to_all x1, waiting for transfers between devices, local(): recv = lax.all_to_all(send, 'ctx', 0, 0, tiled=True)  3.42 us
  transfers between devices with their start and end apart: 18, of which 10 were waited for; matrix products, arithmetic and copies ran while one was open for 1% of the time, Pallas kernels for 10%

profile of v2, /device:TPU:8, one launch (start us, length us, event | category | flops | bytes accessed | tf_op | source)
XLA Modules:
  0.0 81.5 jit_solution(6136901830705634512)
XLA Ops:
  0.8 1.9 %collective-permute-start = (bf16[16,3,512]{2,0,1:T(8,128)(2,1)S(1)}, bf16[16,3,512]{2,0,1:T(8,128)(2,1)S(1)}, u32[]{:S(2)}, u32[]{:S(2)}) collective-permute-start(bf16[16,3,512]{2,0,1:T(8,128)(2,1)S(1)} %slice.65), channel_id=1, source_target_pairs={{0,16},{16,32},{32,48},{48,64},{64,80},{80,96},{96,112},{112,128},... | collective-permute-start | bytes 147464 | tf_op jit(solution)/shard_map/ppermute | solution.py:333
  2.7 2.6 %bulk.1 = (f32[304,512]{1,0:T(8,128)S(1)}, f32[2,96,512]{2,1,0:T(8,128)S(1)}, f32[256,512]{1,0:T(8,128)S(1)}, f32[16,8,512]{2,1,0:T(8,128)S(1)}, f32[3,7,512]{2,1,0:T(8,128)S(1)}, /*index=5*/f32[16,512]{1,0:T(8,128)S(1)}) custom-call(bf16[3,256,512]{2,1,0:T(8,128)(2,1)} %bitcast.132, f32[3,7,512]{2,1,0:T(8,128)} %taps_hbm.1, f32[16,512]{1,0:T(8,128)} %rate_hbm.1), custom_call_target="tpu_custom_call" | custom-call | flops 8388608 | bytes 4194304 | tf_op jit(solution)/shard_map/bulk/pallas_call | solution.py:316
  7.6 6.0 %all-to-all-start = ((bf16[16,16,512]{2,1,0:T(8,128)(2,1)}), bf16[16,16,512]{2,1,0:T(8,128)(2,1)S(1)}, u32[]{:S(2)}, u32[]{:S(2)}) async-start(bf16[16,16,512]{2,1,0:T(8,128)(2,1)} %get-tuple-element.26), calls=%async_computation | async-start | bytes 524288 | tf_op jit(solution)/shard_map/all_to_all | solution.py:360
  13.6 2.0 %inner.1 = (f32[256,512]{1,0:T(8,128)S(1)}, f32[256,512]{1,0:T(8,128)S(1)}, f32[16,8,512]{2,1,0:T(8,128)S(1)}, bf16[256,256]{1,0:T(8,128)(2,1)S(1)}) custom-call(f32[304,512]{1,0:T(8,128)S(1)} %get-tuple-element.27.px_ref, bf16[3,16,512]{2,1,0:T(8,128)(2,1)S(1)} %bitcast.131, f32[3,7,512]{2,1,0:T(8,128)S(1)} %get-tuple-element.23.taps_ref, ...), custom_call_target="tpu_custom_call" | custom-call | flops 16777216 | bytes 4194304 | tf_op jit(solution)/shard_map/inner/pallas_call | solution.py:316
  15.6 3.4 %all-to-all-done.recv_ref = bf16[16,16,512]{2,1,0:T(8,128)(2,1)S(1)} async-done(((bf16[16,16,512]{2,1,0:T(8,128)(2,1)}), bf16[16,16,512]{2,1,0:T(8,128)(2,1)S(1)}, u32[]{:S(2)}, u32[]{:S(2)}) %all-to-all-start) | async-done | bytes 262176 | tf_op jit(solution)/shard_map/all_to_all | solution.py:360
  19.0 3.6 %gate.1 = (bf16[256,512]{1,0:T(8,128)(2,1)S(1)}, bf16[256,4096]{1,0:T(8,128)(2,1)S(1)}) custom-call(bf16[512,8192]{1,0:T(8,128)(2,1)} %weight_hbm.3, bf16[16,16,512]{2,1,0:T(8,128)(2,1)S(1)} %all-to-all-done.recv_ref, f32[16,512]{1,0:T(8,128)S(1)} %get-tuple-element.24.rate_ref, f32[16,8,512]{2,1,0:T(8,128)S(1)} %get-tuple-element.33.lead_ref, ...), custom_call_target="tpu_custom_call" | custom-call | flops 1073741824 | bytes 4194304 | tf_op jit(solution)/shard_map/gate/pallas_call | solution.py:316
  22.6 2.0 %collective-permute-start.1 = (bf16[2,16,4096]{2,1,0:T(8,128)(2,1)S(1)}, bf16[2,16,4096]{2,1,0:T(8,128)(2,1)S(1)}, u32[]{:S(2)}, u32[]{:S(2)}) collective-permute-start(bf16[2,16,4096]{2,1,0:T(8,128)(2,1)S(1)} %get-tuple-element.43), channel_id=1, source_target_pairs={{0,1},{1,2},{2,3},{3,4},{4,5},{5,6},{6,7},{7,0},{8,9},{9,10},{10,1... | collective-permute-start | bytes 786440 | tf_op jit(solution)/shard_map/ppermute | solution.py:294
  24.6 4.0 %collective-permute-start.5 = (bf16[2,16,4096]{2,1,0:T(8,128)(2,1)S(1)}, bf16[2,16,4096]{2,1,0:T(8,128)(2,1)S(1)}, u32[]{:S(2)}, u32[]{:S(2)}) collective-permute-start(bf16[2,16,4096]{2,1,0:T(8,128)(2,1)S(1)} %get-tuple-element.44), channel_id=1, source_target_pairs={{0,7},{1,0},{2,1},{3,2},{4,3},{5,4},{6,5},{7,6},{8,15},{9,8},{10,9... | collective-permute-start | bytes 786440 | tf_op jit(solution)/shard_map/ppermute | solution.py:296
  28.6 3.6 %project.1 = bf16[256,4096]{1,0:T(8,128)(2,1)S(1)} custom-call(bf16[512,8192]{1,0:T(8,128)(2,1)} %weight_hbm.3, bf16[256,512]{1,0:T(8,128)(2,1)S(1)} %get-tuple-element.38.gated_ref), custom_call_target="tpu_custom_call" | custom-call | flops 1073741824 | bytes 4194304 | tf_op jit(solution)/shard_map/project/pallas_call | solution.py:316
  32.3 3.2 %collective-permute-start.12 = (bf16[2,16,4096]{2,1,0:T(8,128)(2,1)S(1)}, bf16[2,16,4096]{2,1,0:T(8,128)(2,1)S(1)}, u32[]{:S(2)}, u32[]{:S(2)}) collective-permute-start(bf16[2,16,4096]{2,1,0:T(8,128)(2,1)S(1)} %get-tuple-element.50), channel_id=1, source_target_pairs={{0,7},{1,0},{2,1},{3,2},{4,3},{5,4},{6,5},{7,6},{8,15},{9,8},{10,9... | collective-permute-start | bytes 786440 | tf_op jit(solution)/shard_map/ppermute | solution.py:296
  35.8 5.7 %collective-permute-done.12 = bf16[2,16,4096]{2,1,0:T(8,128)(2,1)S(1)} collective-permute-done((bf16[2,16,4096]{2,1,0:T(8,128)(2,1)S(1)}, bf16[2,16,4096]{2,1,0:T(8,128)(2,1)S(1)}, u32[]{:S(2)}, u32[]{:S(2)}) %collective-permute-start.12) | collective-permute-done | bytes 262176 | tf_op jit(solution)/shard_map/ppermute | solution.py:296
  41.6 3.8 %collective-permute-start.13 = (bf16[2,16,4096]{2,1,0:T(8,128)(2,1)S(1)}, bf16[2,16,4096]{2,1,0:T(8,128)(2,1)S(1)}, u32[]{:S(2)}, u32[]{:S(2)}) collective-permute-start(bf16[2,16,4096]{2,1,0:T(8,128)(2,1)S(1)} %fusion.2), channel_id=1, source_target_pairs={{0,7},{1,0},{2,1},{3,2},{4,3},{5,4},{6,5},{7,6},{8,15},{9,8},{10,9... | collective-permute-start | bytes 786440 | tf_op jit(solution)/shard_map/ppermute | solution.py:296
  45.4 2.5 %collective-permute-done.2 = bf16[2,16,4096]{2,1,0:T(8,128)(2,1)S(1)} collective-permute-done((bf16[2,16,4096]{2,1,0:T(8,128)(2,1)S(1)}, bf16[2,16,4096]{2,1,0:T(8,128)(2,1)S(1)}, u32[]{:S(2)}, u32[]{:S(2)}) %collective-permute-start.2) | collective-permute-done | bytes 262176 | tf_op jit(solution)/shard_map/ppermute | solution.py:294
  48.1 3.2 %collective-permute-start.6 = (bf16[2,16,4096]{2,1,0:T(8,128)(2,1)S(1)}, bf16[2,16,4096]{2,1,0:T(8,128)(2,1)S(1)}, u32[]{:S(2)}, u32[]{:S(2)}) collective-permute-start(bf16[2,16,4096]{2,1,0:T(8,128)(2,1)S(1)} %get-tuple-element.42), channel_id=1, source_target_pairs={{0,7},{1,0},{2,1},{3,2},{4,3},{5,4},{6,5},{7,6},{8,15},{9,8},{10,9... | collective-permute-start | bytes 786440 | tf_op jit(solution)/shard_map/ppermute | solution.py:296
  51.9 3.0 %collective-permute-start.14 = (bf16[2,16,4096]{2,1,0:T(8,128)(2,1)S(1)}, bf16[2,16,4096]{2,1,0:T(8,128)(2,1)S(1)}, u32[]{:S(2)}, u32[]{:S(2)}) collective-permute-start(bf16[2,16,4096]{2,1,0:T(8,128)(2,1)S(1)} %get-tuple-element.48), channel_id=1, source_target_pairs={{0,7},{1,0},{2,1},{3,2},{4,3},{5,4},{6,5},{7,6},{8,15},{9,8},{10,9... | collective-permute-start | bytes 786440 | tf_op jit(solution)/shard_map/ppermute | solution.py:296
  54.9 3.6 %collective-permute-done.3 = bf16[2,16,4096]{2,1,0:T(8,128)(2,1)S(1)} collective-permute-done((bf16[2,16,4096]{2,1,0:T(8,128)(2,1)S(1)}, bf16[2,16,4096]{2,1,0:T(8,128)(2,1)S(1)}, u32[]{:S(2)}, u32[]{:S(2)}) %collective-permute-start.3) | collective-permute-done | bytes 262176 | tf_op jit(solution)/shard_map/ppermute | solution.py:294
  58.7 3.3 %collective-permute-start.7 = (bf16[2,16,4096]{2,1,0:T(8,128)(2,1)S(1)}, bf16[2,16,4096]{2,1,0:T(8,128)(2,1)S(1)}, u32[]{:S(2)}, u32[]{:S(2)}) collective-permute-start(bf16[2,16,4096]{2,1,0:T(8,128)(2,1)S(1)} %get-tuple-element.40), channel_id=1, source_target_pairs={{0,7},{1,0},{2,1},{3,2},{4,3},{5,4},{6,5},{7,6},{8,15},{9,8},{10,9... | collective-permute-start | bytes 786440 | tf_op jit(solution)/shard_map/ppermute | solution.py:296
  62.0 2.1 %collective-permute-done.10 = bf16[2,16,4096]{2,1,0:T(8,128)(2,1)S(1)} collective-permute-done((bf16[2,16,4096]{2,1,0:T(8,128)(2,1)S(1)}, bf16[2,16,4096]{2,1,0:T(8,128)(2,1)S(1)}, u32[]{:S(2)}, u32[]{:S(2)}) %collective-permute-start.10) | collective-permute-done | bytes 262176 | tf_op jit(solution)/shard_map/ppermute | solution.py:294
  64.3 3.3 %collective-permute-start.15 = (bf16[2,16,4096]{2,1,0:T(8,128)(2,1)S(1)}, bf16[2,16,4096]{2,1,0:T(8,128)(2,1)S(1)}, u32[]{:S(2)}, u32[]{:S(2)}) collective-permute-start(bf16[2,16,4096]{2,1,0:T(8,128)(2,1)S(1)} %get-tuple-element.46), channel_id=1, source_target_pairs={{0,7},{1,0},{2,1},{3,2},{4,3},{5,4},{6,5},{7,6},{8,15},{9,8},{10,9... | collective-permute-start | bytes 786440 | tf_op jit(solution)/shard_map/ppermute | solution.py:296
  67.7 2.1 %collective-permute-done.4 = bf16[2,16,4096]{2,1,0:T(8,128)(2,1)S(1)} collective-permute-done((bf16[2,16,4096]{2,1,0:T(8,128)(2,1)S(1)}, bf16[2,16,4096]{2,1,0:T(8,128)(2,1)S(1)}, u32[]{:S(2)}, u32[]{:S(2)}) %collective-permute-start.4) | collective-permute-done | bytes 262176 | tf_op jit(solution)/shard_map/ppermute | solution.py:294
  69.8 2.8 %collective-permute-start.8 = (bf16[16,4096]{1,0:T(8,128)(2,1)S(1)}, bf16[16,4096]{1,0:T(8,128)(2,1)S(1)}, u32[]{:S(2)}, u32[]{:S(2)}) collective-permute-start(bf16[16,4096]{1,0:T(8,128)(2,1)S(1)} %fusion.14), channel_id=1, source_target_pairs={{0,8},{1,9},{2,10},{3,11},{4,12},{5,13},{6,14},{7,15},{8,0},{9,1},... | collective-permute-start | bytes 393224 | tf_op jit(solution)/shard_map/ppermute | solution.py:307
  72.6 1.4 %collective-permute-done.11 = bf16[2,16,4096]{2,1,0:T(8,128)(2,1)S(1)} collective-permute-done((bf16[2,16,4096]{2,1,0:T(8,128)(2,1)S(1)}, bf16[2,16,4096]{2,1,0:T(8,128)(2,1)S(1)}, u32[]{:S(2)}, u32[]{:S(2)}) %collective-permute-start.11) | collective-permute-done | bytes 262176 | tf_op jit(solution)/shard_map/ppermute | solution.py:294
  74.2 2.8 %collective-permute-start.16 = (bf16[16,4096]{1,0:T(8,128)(2,1)S(1)}, bf16[16,4096]{1,0:T(8,128)(2,1)S(1)}, u32[]{:S(2)}, u32[]{:S(2)}) collective-permute-start(bf16[16,4096]{1,0:T(8,128)(2,1)S(1)} %fusion.15), channel_id=1, source_target_pairs={{0,8},{1,9},{2,10},{3,11},{4,12},{5,13},{6,14},{7,15},{8,0},{9,1},... | collective-permute-start | bytes 393224 | tf_op jit(solution)/shard_map/ppermute | solution.py:307
  77.0 3.7 %collective-permute-done.16 = bf16[16,4096]{1,0:T(8,128)(2,1)S(1)} collective-permute-done((bf16[16,4096]{1,0:T(8,128)(2,1)S(1)}, bf16[16,4096]{1,0:T(8,128)(2,1)S(1)}, u32[]{:S(2)}, u32[]{:S(2)}) %collective-permute-start.16) | collective-permute-done | bytes 131104 | tf_op jit(solution)/shard_map/ppermute | solution.py:307
  (38 shorter events, 5.7 us)
Async XLA Ops:
  0.0 13.5 %copy-start = (f32[16,512]{1,0:T(8,128)S(1)}, f32[16,512]{1,0:T(8,128)}, u32[]{:S(2)}) copy-start(f32[16,512]{1,0:T(8,128)} %rate_hbm.1) | copy-start | bytes 98308
  0.0 13.5 %copy-start.1 = (f32[16,512]{1,0:T(8,128)S(1)}, f32[16,512]{1,0:T(8,128)}, u32[]{:S(2)}) copy-start(f32[16,512]{1,0:T(8,128)} %param.8) | copy-start | bytes 98308
  0.8 5.4 %collective-permute-start = (bf16[16,3,512]{2,0,1:T(8,128)(2,1)S(1)}, bf16[16,3,512]{2,0,1:T(8,128)(2,1)S(1)}, u32[]{:S(2)}, u32[]{:S(2)}) collective-permute-start(bf16[16,3,512]{2,0,1:T(8,128)(2,1)S(1)} %slice.65), channel_id=1, source_target_pairs={{0,16},{16,32},{32,48},{48,64},{64,80},{80,96},{96,112},{112,128},... | collective-permute-start | bytes 147464 | tf_op jit(solution)/shard_map/ppermute | solution.py:333
  7.6 11.4 %all-to-all-start = ((bf16[16,16,512]{2,1,0:T(8,128)(2,1)}), bf16[16,16,512]{2,1,0:T(8,128)(2,1)S(1)}, u32[]{:S(2)}, u32[]{:S(2)}) async-start(bf16[16,16,512]{2,1,0:T(8,128)(2,1)} %get-tuple-element.26), calls=%async_computation | async-start | bytes 524288 | tf_op jit(solution)/shard_map/all_to_all | solution.py:360
  22.6 13.0 %collective-permute-start.1 = (bf16[2,16,4096]{2,1,0:T(8,128)(2,1)S(1)}, bf16[2,16,4096]{2,1,0:T(8,128)(2,1)S(1)}, u32[]{:S(2)}, u32[]{:S(2)}) collective-permute-start(bf16[2,16,4096]{2,1,0:T(8,128)(2,1)S(1)} %get-tuple-element.43), channel_id=1, source_target_pairs={{0,1},{1,2},{2,3},{3,4},{4,5},{5,6},{6,7},{7,0},{8,9},{9,10},{10,1... | collective-permute-start | bytes 786440 | tf_op jit(solution)/shard_map/ppermute | solution.py:294
  24.6 20.8 %collective-permute-start.5 = (bf16[2,16,4096]{2,1,0:T(8,128)(2,1)S(1)}, bf16[2,16,4096]{2,1,0:T(8,128)(2,1)S(1)}, u32[]{:S(2)}, u32[]{:S(2)}) collective-permute-start(bf16[2,16,4096]{2,1,0:T(8,128)(2,1)S(1)} %get-tuple-element.44), channel_id=1, source_target_pairs={{0,7},{1,0},{2,1},{3,2},{4,3},{5,4},{6,5},{7,6},{8,15},{9,8},{10,9... | collective-permute-start | bytes 786440 | tf_op jit(solution)/shard_map/ppermute | solution.py:296
  32.3 19.0 %collective-permute-start.9 = (bf16[2,16,4096]{2,1,0:T(8,128)(2,1)S(1)}, bf16[2,16,4096]{2,1,0:T(8,128)(2,1)S(1)}, u32[]{:S(2)}, u32[]{:S(2)}) collective-permute-start(bf16[2,16,4096]{2,1,0:T(8,128)(2,1)S(1)} %get-tuple-element.49), channel_id=1, source_target_pairs={{0,1},{1,2},{2,3},{3,4},{4,5},{5,6},{6,7},{7,0},{8,9},{9,10},{10,1... | collective-permute-start | bytes 786440 | tf_op jit(solution)/shard_map/ppermute | solution.py:294
  32.3 9.2 %collective-permute-start.12 = (bf16[2,16,4096]{2,1,0:T(8,128)(2,1)S(1)}, bf16[2,16,4096]{2,1,0:T(8,128)(2,1)S(1)}, u32[]{:S(2)}, u32[]{:S(2)}) collective-permute-start(bf16[2,16,4096]{2,1,0:T(8,128)(2,1)S(1)} %get-tuple-element.50), channel_id=1, source_target_pairs={{0,7},{1,0},{2,1},{3,2},{4,3},{5,4},{6,5},{7,6},{8,15},{9,8},{10,9... | collective-permute-start | bytes 786440 | tf_op jit(solution)/shard_map/ppermute | solution.py:296
  35.7 12.2 %collective-permute-start.2 = (bf16[2,16,4096]{2,1,0:T(8,128)(2,1)S(1)}, bf16[2,16,4096]{2,1,0:T(8,128)(2,1)S(1)}, u32[]{:S(2)}, u32[]{:S(2)}) collective-permute-start(bf16[2,16,4096]{2,1,0:T(8,128)(2,1)S(1)} %fusion.9), channel_id=1, source_target_pairs={{0,1},{1,2},{2,3},{3,4},{4,5},{5,6},{6,7},{7,0},{8,9},{9,10},{10,1... | collective-permute-start | bytes 786440 | tf_op jit(solution)/shard_map/ppermute | solution.py:294
  41.6 9.7 %collective-permute-start.13 = (bf16[2,16,4096]{2,1,0:T(8,128)(2,1)S(1)}, bf16[2,16,4096]{2,1,0:T(8,128)(2,1)S(1)}, u32[]{:S(2)}, u32[]{:S(2)}) collective-permute-start(bf16[2,16,4096]{2,1,0:T(8,128)(2,1)S(1)} %fusion.2), channel_id=1, source_target_pairs={{0,7},{1,0},{2,1},{3,2},{4,3},{5,4},{6,5},{7,6},{8,15},{9,8},{10,9... | collective-permute-start | bytes 786440 | tf_op jit(solution)/shard_map/ppermute | solution.py:296
  48.0 10.5 %collective-permute-start.3 = (bf16[2,16,4096]{2,1,0:T(8,128)(2,1)S(1)}, bf16[2,16,4096]{2,1,0:T(8,128)(2,1)S(1)}, u32[]{:S(2)}, u32[]{:S(2)}) collective-permute-start(bf16[2,16,4096]{2,1,0:T(8,128)(2,1)S(1)} %get-tuple-element.41), channel_id=1, source_target_pairs={{0,1},{1,2},{2,3},{3,4},{4,5},{5,6},{6,7},{7,0},{8,9},{9,10},{10,1... | collective-permute-start | bytes 786440 | tf_op jit(solution)/shard_map/ppermute | solution.py:294
  48.1 10.4 %collective-permute-start.6 = (bf16[2,16,4096]{2,1,0:T(8,128)(2,1)S(1)}, bf16[2,16,4096]{2,1,0:T(8,128)(2,1)S(1)}, u32[]{:S(2)}, u32[]{:S(2)}) collective-permute-start(bf16[2,16,4096]{2,1,0:T(8,128)(2,1)S(1)} %get-tuple-element.42), channel_id=1, source_target_pairs={{0,7},{1,0},{2,1},{3,2},{4,3},{5,4},{6,5},{7,6},{8,15},{9,8},{10,9... | collective-permute-start | bytes 786440 | tf_op jit(solution)/shard_map/ppermute | solution.py:296
  51.4 12.7 %collective-permute-start.10 = (bf16[2,16,4096]{2,1,0:T(8,128)(2,1)S(1)}, bf16[2,16,4096]{2,1,0:T(8,128)(2,1)S(1)}, u32[]{:S(2)}, u32[]{:S(2)}) collective-permute-start(bf16[2,16,4096]{2,1,0:T(8,128)(2,1)S(1)} %get-tuple-element.47), channel_id=1, source_target_pairs={{0,1},{1,2},{2,3},{3,4},{4,5},{5,6},{6,7},{7,0},{8,9},{9,10},{10,1... | collective-permute-start | bytes 786440 | tf_op jit(solution)/shard_map/ppermute | solution.py:294
  51.9 12.2 %collective-permute-start.14 = (bf16[2,16,4096]{2,1,0:T(8,128)(2,1)S(1)}, bf16[2,16,4096]{2,1,0:T(8,128)(2,1)S(1)}, u32[]{:S(2)}, u32[]{:S(2)}) collective-permute-start(bf16[2,16,4096]{2,1,0:T(8,128)(2,1)S(1)} %get-tuple-element.48), channel_id=1, source_target_pairs={{0,7},{1,0},{2,1},{3,2},{4,3},{5,4},{6,5},{7,6},{8,15},{9,8},{10,9... | collective-permute-start | bytes 786440 | tf_op jit(solution)/shard_map/ppermute | solution.py:296
  58.6 11.1 %collective-permute-start.4 = (bf16[2,16,4096]{2,1,0:T(8,128)(2,1)S(1)}, bf16[2,16,4096]{2,1,0:T(8,128)(2,1)S(1)}, u32[]{:S(2)}, u32[]{:S(2)}) collective-permute-start(bf16[2,16,4096]{2,1,0:T(8,128)(2,1)S(1)} %get-tuple-element.39), channel_id=1, source_target_pairs={{0,1},{1,2},{2,3},{3,4},{4,5},{5,6},{6,7},{7,0},{8,9},{9,10},{10,1... | collective-permute-start | bytes 786440 | tf_op jit(solution)/shard_map/ppermute | solution.py:294
  58.7 11.0 %collective-permute-start.7 = (bf16[2,16,4096]{2,1,0:T(8,128)(2,1)S(1)}, bf16[2,16,4096]{2,1,0:T(8,128)(2,1)S(1)}, u32[]{:S(2)}, u32[]{:S(2)}) collective-permute-start(bf16[2,16,4096]{2,1,0:T(8,128)(2,1)S(1)} %get-tuple-element.40), channel_id=1, source_target_pairs={{0,7},{1,0},{2,1},{3,2},{4,3},{5,4},{6,5},{7,6},{8,15},{9,8},{10,9... | collective-permute-start | bytes 786440 | tf_op jit(solution)/shard_map/ppermute | solution.py:296
  64.2 9.8 %collective-permute-start.11 = (bf16[2,16,4096]{2,1,0:T(8,128)(2,1)S(1)}, bf16[2,16,4096]{2,1,0:T(8,128)(2,1)S(1)}, u32[]{:S(2)}, u32[]{:S(2)}) collective-permute-start(bf16[2,16,4096]{2,1,0:T(8,128)(2,1)S(1)} %get-tuple-element.45), channel_id=1, source_target_pairs={{0,1},{1,2},{2,3},{3,4},{4,5},{5,6},{6,7},{7,0},{8,9},{9,10},{10,1... | collective-permute-start | bytes 786440 | tf_op jit(solution)/shard_map/ppermute | solution.py:294
  64.3 9.7 %collective-permute-start.15 = (bf16[2,16,4096]{2,1,0:T(8,128)(2,1)S(1)}, bf16[2,16,4096]{2,1,0:T(8,128)(2,1)S(1)}, u32[]{:S(2)}, u32[]{:S(2)}) collective-permute-start(bf16[2,16,4096]{2,1,0:T(8,128)(2,1)S(1)} %get-tuple-element.46), channel_id=1, source_target_pairs={{0,7},{1,0},{2,1},{3,2},{4,3},{5,4},{6,5},{7,6},{8,15},{9,8},{10,9... | collective-permute-start | bytes 786440 | tf_op jit(solution)/shard_map/ppermute | solution.py:296
  69.8 7.1 %collective-permute-start.8 = (bf16[16,4096]{1,0:T(8,128)(2,1)S(1)}, bf16[16,4096]{1,0:T(8,128)(2,1)S(1)}, u32[]{:S(2)}, u32[]{:S(2)}) collective-permute-start(bf16[16,4096]{1,0:T(8,128)(2,1)S(1)} %fusion.14), channel_id=1, source_target_pairs={{0,8},{1,9},{2,10},{3,11},{4,12},{5,13},{6,14},{7,15},{8,0},{9,1},... | collective-permute-start | bytes 393224 | tf_op jit(solution)/shard_map/ppermute | solution.py:307
  74.2 6.6 %collective-permute-start.16 = (bf16[16,4096]{1,0:T(8,128)(2,1)S(1)}, bf16[16,4096]{1,0:T(8,128)(2,1)S(1)}, u32[]{:S(2)}, u32[]{:S(2)}) collective-permute-start(bf16[16,4096]{1,0:T(8,128)(2,1)S(1)} %fusion.15), channel_id=1, source_target_pairs={{0,8},{1,9},{2,10},{3,11},{4,12},{5,13},{6,14},{7,15},{8,0},{9,1},... | collective-permute-start | bytes 393224 | tf_op jit(solution)/shard_map/ppermute | solution.py:307

commit v3 on v2

--- a/solution.py
+++ b/solution.py
@@ -13,6 +13,9 @@
 LANES = 128
 NZ = 8
 HALO = 16
+READY = 1024
+MEET = (2, 0)
+WIDTHS = (4096, 4096)
 BACK = TAPS - 1
 
 f32 = jnp.float32
@@ -74,26 +77,23 @@
 
 
 def bulk_kernel(
-    tokens, x_hbm, taps_hbm, rate_hbm, zero_ref, head_ref, sig_ref, late_ref, taps_ref, rate_ref, x_ref, px_ref, sems
+    tokens, x_hbm, taps_hbm, rate_hbm, head_ref, sig_ref, late_ref, taps_ref, rate_ref, x_ref, px_ref, sems
 ):
     rows = x_ref.shape[1]
     run = rows // SUB
-    copies = {b: pltpu.make_async_copy(x_hbm.at[b], x_ref.at[b], sems.at[b]) for b in (1, 2, 0)}
+    copies = [pltpu.make_async_copy(x_hbm.at[b + 1], x_ref.at[b], sems.at[b]) for b in range(2)]
     small = [
-        pltpu.make_async_copy(taps_hbm, taps_ref, sems.at[3]),
-        pltpu.make_async_copy(rate_hbm, rate_ref, sems.at[4]),
+        pltpu.make_async_copy(taps_hbm, taps_ref, sems.at[2]),
+        pltpu.make_async_copy(rate_hbm, rate_ref, sems.at[3]),
     ]
-    for c in [*copies.values(), *small]:
+    for c in copies + small:
         c.start()
     move = spread_matrix(rows)
-    for b, c in copies.items():
+    for b, c in enumerate(copies):
         c.wait()
         moved = jnp.dot(move, x_ref[b], preferred_element_type=f32)
-        if b == 0:
-            zero_ref[...] = moved
-        else:
-            px_ref[b - 1] = moved
-            head_ref[b - 1] = moved[: 2 * BACK * SUB]
+        px_ref[b] = moved
+        head_ref[b] = moved[: 2 * BACK * SUB]
     for c in small:
         c.wait()
 
@@ -159,7 +159,8 @@
 
 def inner_kernel(
     tokens,
-    px_ref,
+    x_hbm,
+    weight_hbm,
     halo_ref,
     taps_ref,
     rate_ref,
@@ -171,11 +172,22 @@
     y_ref,
     lead_ref,
     turn_ref,
-    edges,
+    weight_ref,
+    x_ref,
+    px_ref,
+    half_ref,
+    sems,
 ):
+    copy = pltpu.make_async_copy(x_hbm.at[0], x_ref, sems.at[0])
+    fetch = pltpu.make_async_copy(weight_hbm.at[:, : weight_ref.shape[1]], weight_ref, sems.at[1])
+    copy.start()
+    fetch.start()
     rows = q_ref.shape[0]
     run = rows // SUB
-    edges[...] = px_ref[: BACK * SUB] + edge_rows(halo_ref, 0)
+    move = spread_matrix(rows)
+    copy.wait()
+    px_ref[...] = jnp.dot(move, x_ref[...], preferred_element_type=f32)
+    px_ref[: BACK * SUB] = px_ref[: BACK * SUB] + edge_rows(halo_ref, 0)
     sub = lax.broadcasted_iota(jnp.int32, (SUB, LANES), 0)
     sub_time = (sub * run + 1).astype(f32) * (-1.0 / tokens)
 
@@ -189,7 +201,7 @@
         fir(
             taps_ref,
             0,
-            lambda e: edges[at(e), lanes] if e < BACK else px_ref[at(e), lanes],
+            lambda e: px_ref[at(e), lanes],
             lanes,
             range(run),
             put,
@@ -212,18 +224,23 @@
                 terms = [c * s for c, s in zip(coef, state)]
                 while len(terms) > 1:
                     terms = [terms[i] + terms[i + 1] for i in range(0, len(terms), 2)]
-                y_ref[at(t), lanes] = terms[0] if first == 0 else y_ref[at(t), lanes] + terms[0]
+                if first == 0:
+                    half_ref[at(t), lanes] = terms[0]
+                else:
+                    y_ref[at(t), lanes] = half_ref[at(t), lanes] + terms[0]
 
     lane_loop(q_ref.shape[1], group)
     tp = lax.axis_index("tp")
     half, z = tp // NZ, tp % NZ
+    way = 1 - 2 * (lax.axis_index("ctx") % 2)
 
     def natural(o):
-        block = ((half + o // (NZ * 16)) % 2) * NZ + (z + o // 16) % NZ
+        block = ((half + o // (NZ * 16)) % 2) * NZ + (z + way * (o // 16 % NZ) + NZ) % NZ
         n = block * 16 + o % 16
         return (n % run) * SUB + n // run
 
     turn_ref[...] = one_hot(rows, rows, natural)
+    fetch.wait()
 
 
 def column_copies(weight_hbm, weight, sems, base):
@@ -239,16 +256,30 @@
     return copies
 
 
-def times(left, copies, weight, out_ref):
+def times(left, copies, weight, out_ref, base=0):
     for here, copy in copies:
         copy.wait()
-        out_ref[:, here] = jnp.dot(left, weight[:, here], preferred_element_type=f32).astype(bf16)
+        out_ref[:, slice(base + here.start, base + here.stop)] = jnp.dot(left, weight[:, here], preferred_element_type=f32).astype(bf16)
 
 
 def gate_kernel(
-    tokens, weight_hbm, recv_ref, rate_ref, lead_ref, y_ref, q_ref, turn_ref, gated_ref, part_ref, flat, weight, sems
+    tokens,
+    weight_hbm,
+    recv_ref,
+    rate_ref,
+    lead_ref,
+    y_ref,
+    q_ref,
+    turn_ref,
+    ready_ref,
+    gated_ref,
+    part_ref,
+    flat,
+    weight,
+    sems,
 ):
-    copies = column_copies(weight_hbm, weight, sems, 0)
+    ready = ready_ref.shape[1]
+    copies = column_copies(weight_hbm, weight, sems, ready)
     n_ctx = recv_ref.shape[0]
     run = y_ref.shape[0] // SUB
 
@@ -269,7 +300,8 @@
     lane_loop(y_ref.shape[1], group)
     gated = jnp.dot(turn_ref[...], flat[...].astype(bf16), preferred_element_type=f32).astype(bf16)
     gated_ref[...] = gated
-    times(gated, copies, weight, part_ref)
+    part_ref[:, :ready] = jnp.dot(gated, ready_ref[...], preferred_element_type=f32).astype(bf16)
+    times(gated, copies, weight, part_ref, ready)
 
 
 def project_kernel(base, weight_hbm, gated_ref, part_ref, weight, sems):
@@ -277,38 +309,59 @@
     times(gated_ref[...], copies, weight, part_ref)
 
 
-def z_pairs(by):
-    return [(h * NZ + z, h * NZ + (z + by) % NZ) for h in range(2) for z in range(NZ)]
+def ring_pairs(n_ctx, by):
+    return [
+        ((c * 2 + h) * NZ + z, (c * 2 + h) * NZ + (z + by * (1 - 2 * (c % 2))) % NZ)
+        for c in range(n_ctx)
+        for h in range(2)
+        for z in range(NZ)
+    ]
 
 
 def half_pairs():
     return [(i, (i + NZ) % (2 * NZ)) for i in range(2 * NZ)]
 
 
-def ring(blocks, more_left):
-    rights, lefts = (NZ // 2 - 1, NZ // 2) if more_left else (NZ // 2, NZ // 2 - 1)
-    right = blocks[rights]
-    left = blocks[-lefts % NZ]
-    for s in range(NZ // 2):
-        if s < rights:
-            right = lax.ppermute(right, "tp", z_pairs(1))
-        if s < lefts:
-            left = lax.ppermute(left, "tp", z_pairs(-1))
-        if s < rights - 1:
-            right = (right.astype(f32) + blocks[rights - 1 - s].astype(f32)).astype(bf16)
-        if s < lefts - 1:
-            left = (left.astype(f32) + blocks[-(lefts - 1 - s) % NZ].astype(f32)).astype(bf16)
-    return right.astype(f32) + left.astype(f32) + blocks[0].astype(f32)
-
-
-def reduce_columns(part, more_left):
+def plus(*terms):
+    return sum(t.astype(f32) for t in terms).astype(bf16)
+
+
+def along(x, way):
+    return lax.ppermute(x, ("ctx", "tp"), ring_pairs(lax.axis_size("ctx"), way))
+
+
+def across(x):
+    return lax.ppermute(x, "tp", half_pairs())
+
+
+def reduce_columns(part, longer, meet):
     part = part.reshape(2, NZ, 16, -1)
-    both = ring([part[:, k] for k in range(NZ)], more_left)
-    other = lax.ppermute(both[1].astype(bf16), "tp", half_pairs())
-    return (both[0] + other.astype(f32)).astype(bf16)
-
-
-def call(kernel, outs, scratch, name, flops, *args, far=()):
+    left = {longer: NZ // 2, -longer: NZ // 2 - 1}
+    total = {way: part[:, way * k % NZ] for way, k in left.items()}
+    for _ in range(NZ // 2 - meet):
+        for way in left:
+            if left[way] > meet:
+                left[way] -= 1
+                total[way] = along(total[way], way)
+                if left[way]:
+                    total[way] = plus(total[way], part[:, way * left[way] % NZ])
+    if meet == 0:
+        both = total[1].astype(f32) + total[-1].astype(f32) + part[:, 0].astype(f32)
+        return plus(both[0], across(both[1].astype(bf16)))
+    near = range(1 - meet, meet)
+    got = across(jnp.stack([part[1, k % NZ] for k in near]))
+    close = {k: plus(part[0, k % NZ], got[i]) for i, k in enumerate(near)}
+    other = across(jnp.stack([total[1][1], total[-1][1]]))
+    total = {1: plus(total[1][0], other[0]), -1: plus(total[-1][0], other[1])}
+    for k in range(meet - 1, -1, -1):
+        for way in total:
+            total[way] = along(total[way], way)
+            if k:
+                total[way] = plus(total[way], close[way * k])
+    return plus(total[1], total[-1], close[0])
+
+
+def call(kernel, outs, scratch, name, flops, *args, far=(), aliases=None):
     in_specs = [pl.BlockSpec(memory_space=pl.ANY)] * len(far) + [pl.BlockSpec(memory_space=VMEM)] * len(args)
     args = [pltpu.with_memory_space_constraint(x, pltpu.HBM) for x in far] + [
         pltpu.with_memory_space_constraint(x, VMEM) for x in args
@@ -320,13 +373,14 @@
         out_shape=[VMEM(s, d) for s, d in outs],
         scratch_shapes=[s if not isinstance(s, tuple) else VMEM(*s) for s in scratch],
         compiler_params=pltpu.CompilerParams(vmem_limit_bytes=16 * 2**20),
+        input_output_aliases=aliases or {},
         cost_estimate=pl.CostEstimate(flops=flops, bytes_accessed=4 * 2**20, transcendentals=0),
         name=name,
     )(*args)
 
 
 def local(features, short_filter, decay_rate, residue, out_weight):
-    rows, branches, chans = features.shape
+    rows, _, chans = features.shape
     n_ctx = lax.axis_size("ctx")
     tokens = rows * n_ctx
     run = rows // SUB
@@ -337,10 +391,10 @@
     states = ((MODES, SUB, chans), f32)
     moved = ((run + BACK) * SUB, chans)
     head = 2 * BACK * SUB
-    zero, heads, sig, late, taps, rate = call(
+    heads, sig, late, taps, rate = call(
         functools.partial(bulk_kernel, tokens),
-        [(moved, f32), ((2, head, chans), f32), wide, states, (short_filter.shape, f32), (decay_rate.shape, f32)],
-        [((branches, rows, chans), bf16), ((2, *moved), f32), pltpu.SemaphoreType.DMA((5,))],
+        [((2, head, chans), f32), wide, states, (short_filter.shape, f32), (decay_rate.shape, f32)],
+        [((2, rows, chans), bf16), ((2, *moved), f32), pltpu.SemaphoreType.DMA((4,))],
         "bulk",
         4 * rows * chans * MODES,
         far=(x, short_filter, decay_rate),
@@ -360,13 +414,12 @@
     recv = lax.all_to_all(send, "ctx", 0, 0, tiled=True)
     late_rate, late_residue, _ = lax.optimization_barrier((decay_rate, residue, early))
     coef = late_residue * jnp.sqrt(1.0 / tokens - jnp.expm1(late_rate * (-2.0 / tokens)))
-    q, y, lead, turn = call(
+    q, y, lead, turn, ready = call(
         functools.partial(inner_kernel, tokens),
-        [wide, wide, states, ((rows, rows), bf16)],
-        [((BACK * SUB, chans), f32)],
+        [wide, wide, states, ((rows, rows), bf16), ((chans, READY), bf16)],
+        [((rows, chans), bf16), (moved, f32), wide, pltpu.SemaphoreType.DMA((2,))],
         "inner",
         8 * rows * chans * MODES,
-        zero,
         halo,
         taps,
         rate,
@@ -374,34 +427,41 @@
         sig,
         early,
         ends,
+        far=(x, out_weight),
+        aliases={6: 1},
     )
-    cols = out_weight.shape[1] // 2
-    stream = [((chans, cols), bf16), pltpu.SemaphoreType.DMA((8,))]
+
+    def stream(width):
+        return [((chans, width), bf16), pltpu.SemaphoreType.DMA((max(width // 1024, 1),))]
+
     gated, first = call(
         functools.partial(gate_kernel, tokens),
-        [((rows, chans), bf16), ((rows, cols), bf16)],
-        [wide, *stream],
+        [((rows, chans), bf16), ((rows, WIDTHS[0]), bf16)],
+        [wide, *stream(WIDTHS[0] - READY)],
         "gate",
-        2 * rows * chans * cols,
+        2 * rows * chans * WIDTHS[0],
         recv,
         rate,
         lead,
         y,
         q,
         turn,
+        ready,
         far=(out_weight,),
     )
-    (second,) = call(
-        functools.partial(project_kernel, cols),
-        [((rows, cols), bf16)],
-        stream,
-        "project",
-        2 * rows * chans * cols,
-        gated,
-        far=(out_weight,),
-    )
-    out = [reduce_columns(first, False), reduce_columns(second, True)]
-    return jnp.concatenate(out, axis=1)
+    parts, base = [first], WIDTHS[0]
+    for width in WIDTHS[1:]:
+        parts += call(
+            functools.partial(project_kernel, base),
+            [((rows, width), bf16)],
+            stream(width),
+            "project",
+            2 * rows * chans * width,
+            gated,
+            far=(out_weight,),
+        )
+        base += width
+    return jnp.concatenate([reduce_columns(p, 1, m) for p, m in zip(parts, MEET)], axis=1)
 
 
 def solution(mesh):

time: 81.7 us -> 79.2 us (0.969)
  starting transfers between devices: 40.3 us -> 35.3 us
  waiting for transfers between devices: 25.4 us -> 27.7 us
    ppermute x16 -> x17, starting transfers between devices: 32.5 us -> 27.5 us  [the longest x14 22.8 us: along(): return lax.ppermute(x, ('ctx', 'tp'), ring_pairs(lax.axis_size('ctx'), way))]
    ppermute x16 -> x17, waiting for transfers between devices: 21.1 us -> 24.7 us  [the longest x14 16.7 us: along(): return lax.ppermute(x, ('ctx', 'tp'), ring_pairs(lax.axis_size('ctx'), way))]
    all_to_all x1, waiting for transfers between devices: 3.42 us -> 1.92 us  [local(): recv = lax.all_to_all(send, 'ctx', 0, 0, tiled=True)]
  transfers between devices with their start and end apart: 18 -> 19, of which waited for: 10 -> 11; matrix products, arithmetic and copies ran while one was open for 1% -> 1% of each run, Pallas kernels for 10% -> 11%
where the time goes in v3:
time: 79.2 us; the launch traced here: 78.6 us
  starting transfers between devices  35.3 us (45%)
  waiting for transfers between devices  27.7 us (35%)
  Pallas kernels  12.8 us (16%)
  other arithmetic  1.67 us (2%)
  local copies, waits for them, and re-layouts  0.95 us (1%)
    ppermute x14, starting transfers between devices, along(): return lax.ppermute(x, ('ctx', 'tp'), ring_pairs(lax.axis_size('ctx'), way))  22.8 us
    ppermute x14, waiting for transfers between devices, along(): return lax.ppermute(x, ('ctx', 'tp'), ring_pairs(lax.axis_size('ctx'), way))  16.7 us
    pallas_call x5, Pallas kernels, call(): pl.pallas_call(kernel, in_specs=in_specs, out_specs=[pl.BlockSpec(memory_...  12.8 us
    ppermute x3, waiting for transfers between devices, across(): return lax.ppermute(x, 'tp', half_pairs())  7.97 us
    all_to_all x1, starting transfers between devices, local(): recv = lax.all_to_all(send, 'ctx', 0, 0, tiled=True)  5.86 us
    ppermute x3, starting transfers between devices, across(): return lax.ppermute(x, 'tp', half_pairs())  4.69 us
    all_to_all x1, waiting for transfers between devices, local(): recv = lax.all_to_all(send, 'ctx', 0, 0, tiled=True)  1.92 us
    ppermute x1, starting transfers between devices, local(): lax.ppermute(features[rows - HALO:], 'ctx', [(i, i + 1) for i in range(n_...  1.91 us
  transfers between devices with their start and end apart: 19, of which 11 were waited for; matrix products, arithmetic and copies ran while one was open for 1% of the time, Pallas kernels for 11%

profile of v3, /device:TPU:8, one launch (start us, length us, event | category | flops | bytes accessed | tf_op | source)
XLA Modules:
  0.0 78.6 jit_solution(7140540240257584178)
XLA Ops:
  0.8 1.9 %collective-permute-start = (bf16[16,3,512]{2,0,1:T(8,128)(2,1)S(1)}, bf16[16,3,512]{2,0,1:T(8,128)(2,1)S(1)}, u32[]{:S(2)}, u32[]{:S(2)}) collective-permute-start(bf16[16,3,512]{2,0,1:T(8,128)(2,1)S(1)} %slice.94), channel_id=1, source_target_pairs={{0,16},{16,32},{32,48},{48,64},{64,80},{80,96},{96,112},{112,128},... | collective-permute-start | bytes 147464 | tf_op jit(solution)/shard_map/ppermute | solution.py:387
  2.7 2.3 %bulk.1 = (f32[2,96,512]{2,1,0:T(8,128)S(1)}, f32[256,512]{1,0:T(8,128)S(1)}, f32[16,8,512]{2,1,0:T(8,128)S(1)}, f32[3,7,512]{2,1,0:T(8,128)S(1)}, f32[16,512]{1,0:T(8,128)S(1)}) custom-call(bf16[3,256,512]{2,1,0:T(8,128)(2,1)} %bitcast.142, f32[3,7,512]{2,1,0:T(8,128)} %taps_hbm.1, f32[16,512]{1,0:T(8,128)} %rate_hbm.1), custom_call_target="tpu_custom_call" | custom-call | flops 8388608 | bytes 4194304 | tf_op jit(solution)/shard_map/bulk/pallas_call | solution.py:369
  5.1 1.1 %collective-permute-done = bf16[16,3,512]{2,0,1:T(8,128)(2,1)S(1)} collective-permute-done((bf16[16,3,512]{2,0,1:T(8,128)(2,1)S(1)}, bf16[16,3,512]{2,0,1:T(8,128)(2,1)S(1)}, u32[]{:S(2)}, u32[]{:S(2)}) %collective-permute-start) | collective-permute-done | bytes 49184 | tf_op jit(solution)/shard_map/ppermute | solution.py:387
  6.2 1.4 %edge.1 = (f32[48,512]{1,0:T(8,128)S(1)}, f32[16,8,512]{2,1,0:T(8,128)S(1)}, bf16[16,16,512]{2,1,0:T(8,128)(2,1)}) custom-call(f32[2,96,512]{2,1,0:T(8,128)S(1)} %get-tuple-element.22.head_ref, bf16[3,16,512]{2,1,0:T(8,128)(2,1)S(1)} %bitcast.140, f32[3,7,512]{2,1,0:T(8,128)S(1)} %get-tuple-element.23.taps_ref, f32[16,512]{1,0:T(8,128)S(1)} %get-tuple-element.24.rate_ref, ...), custom_call_target="tpu_custom_call" | custom-call | flops 2097152 | bytes 4194304 | tf_op jit(solution)/shard_map/edge/pallas_call | solution.py:369
  7.6 5.9 %all-to-all-start = ((bf16[16,16,512]{2,1,0:T(8,128)(2,1)}), bf16[16,16,512]{2,1,0:T(8,128)(2,1)S(1)}, u32[]{:S(2)}, u32[]{:S(2)}) async-start(bf16[16,16,512]{2,1,0:T(8,128)(2,1)} %get-tuple-element.26), calls=%async_computation | async-start | bytes 524288 | tf_op jit(solution)/shard_map/all_to_all | solution.py:414
  13.5 3.5 %inner.1 = (f32[256,512]{1,0:T(8,128)S(1)}, f32[256,512]{1,0:T(8,128)S(1)}, f32[16,8,512]{2,1,0:T(8,128)S(1)}, bf16[256,256]{1,0:T(8,128)(2,1)S(1)}, bf16[512,1024]{1,0:T(8,128)(2,1)S(1)}) custom-call(bf16[3,256,512]{2,1,0:T(8,128)(2,1)} %bitcast.143, bf16[512,8192]{1,0:T(8,128)(2,1)} %weight_hbm.5, ...), custom_call_target="tpu_custom_call", output_to_operand_aliasing={{1}: (6, {})} | custom-call | flops 16777216 | bytes 4194304 | tf_op jit(solution)/shard_map/inner/pallas_call | solution.py:369
  17.0 1.9 %all-to-all-done.recv_ref = bf16[16,16,512]{2,1,0:T(8,128)(2,1)S(1)} async-done(((bf16[16,16,512]{2,1,0:T(8,128)(2,1)}), bf16[16,16,512]{2,1,0:T(8,128)(2,1)S(1)}, u32[]{:S(2)}, u32[]{:S(2)}) %all-to-all-start) | async-done | bytes 262176 | tf_op jit(solution)/shard_map/all_to_all | solution.py:414
  18.9 2.6 %gate.1 = (bf16[256,512]{1,0:T(8,128)(2,1)S(1)}, bf16[256,4096]{1,0:T(8,128)(2,1)S(1)}) custom-call(bf16[512,8192]{1,0:T(8,128)(2,1)} %weight_hbm.5, bf16[16,16,512]{2,1,0:T(8,128)(2,1)S(1)} %all-to-all-done.recv_ref, f32[16,512]{1,0:T(8,128)S(1)} %get-tuple-element.24.rate_ref, f32[16,8,512]{2,1,0:T(8,128)S(1)} %get-tuple-element.32.lead_ref, ...), custom_call_target="tpu_custom_call" | custom-call | flops 1073741824 | bytes 4194304 | tf_op jit(solution)/shard_map/gate/pallas_call | solution.py:369
  21.6 2.8 %collective-permute-start.6 = (bf16[3,16,4096]{2,1,0:T(8,128)(2,1)S(1)}, bf16[3,16,4096]{2,1,0:T(8,128)(2,1)S(1)}, u32[]{:S(2)}, u32[]{:S(2)}) collective-permute-start(bf16[3,16,4096]{2,1,0:T(8,128)(2,1)S(1)} %pad_maximum_fusion), channel_id=1, source_target_pairs={{0,8},{1,9},{2,10},{3,11},{4,12},{5,13},{6,14},{7,15},{8,0},{9,1},... | collective-permute-start | bytes 1179656 | tf_op jit(solution)/shard_map/ppermute | solution.py:334
  24.4 1.9 %collective-permute-start.1 = (bf16[2,16,4096]{2,1,0:T(8,128)(2,1)S(1)}, bf16[2,16,4096]{2,1,0:T(8,128)(2,1)S(1)}, u32[]{:S(2)}, u32[]{:S(2)}) collective-permute-start(bf16[2,16,4096]{2,1,0:T(8,128)(2,1)S(1)} %get-tuple-element.46), channel_id=1, source_target_pairs={{0,1},{1,2},{2,3},{3,4},{4,5},{5,6},{6,7},{7,0},{8,9},{9,10},{10,1... | collective-permute-start | bytes 786440 | tf_op jit(solution)/shard_map/ppermute | solution.py:330
  26.4 3.9 %collective-permute-start.3 = (bf16[2,16,4096]{2,1,0:T(8,128)(2,1)S(1)}, bf16[2,16,4096]{2,1,0:T(8,128)(2,1)S(1)}, u32[]{:S(2)}, u32[]{:S(2)}) collective-permute-start(bf16[2,16,4096]{2,1,0:T(8,128)(2,1)S(1)} %get-tuple-element.47), channel_id=1, source_target_pairs={{0,7},{1,0},{2,1},{3,2},{4,3},{5,4},{6,5},{7,6},{8,15},{9,8},{10,9... | collective-permute-start | bytes 786440 | tf_op jit(solution)/shard_map/ppermute | solution.py:330
  30.3 3.0 %project.1 = bf16[256,4096]{1,0:T(8,128)(2,1)S(1)} custom-call(bf16[512,8192]{1,0:T(8,128)(2,1)} %weight_hbm.5, bf16[256,512]{1,0:T(8,128)(2,1)S(1)} %get-tuple-element.38.gated_ref), custom_call_target="tpu_custom_call" | custom-call | flops 1073741824 | bytes 4194304 | tf_op jit(solution)/shard_map/project/pallas_call | solution.py:369
  33.5 3.2 %collective-permute-start.14 = (bf16[2,16,4096]{2,1,0:T(8,128)(2,1)S(1)}, bf16[2,16,4096]{2,1,0:T(8,128)(2,1)S(1)}, u32[]{:S(2)}, u32[]{:S(2)}) collective-permute-start(bf16[2,16,4096]{2,1,0:T(8,128)(2,1)S(1)} %get-tuple-element.53), channel_id=1, source_target_pairs={{0,7},{1,0},{2,1},{3,2},{4,3},{5,4},{6,5},{7,6},{8,15},{9,8},{10,9... | collective-permute-start | bytes 786440 | tf_op jit(solution)/shard_map/ppermute | solution.py:330
  36.9 5.0 %collective-permute-done.10 = bf16[2,16,4096]{2,1,0:T(8,128)(2,1)S(1)} collective-permute-done((bf16[2,16,4096]{2,1,0:T(8,128)(2,1)S(1)}, bf16[2,16,4096]{2,1,0:T(8,128)(2,1)S(1)}, u32[]{:S(2)}, u32[]{:S(2)}) %collective-permute-start.10) | collective-permute-done | bytes 262176 | tf_op jit(solution)/shard_map/ppermute | solution.py:330
  42.0 4.6 %collective-permute-done.2 = bf16[2,16,4096]{2,1,0:T(8,128)(2,1)S(1)} collective-permute-done((bf16[2,16,4096]{2,1,0:T(8,128)(2,1)S(1)}, bf16[2,16,4096]{2,1,0:T(8,128)(2,1)S(1)}, u32[]{:S(2)}, u32[]{:S(2)}) %collective-permute-start.2) | collective-permute-done | bytes 262176 | tf_op jit(solution)/shard_map/ppermute | solution.py:330
  47.7 1.8 %collective-permute-done.11 = bf16[2,16,4096]{2,1,0:T(8,128)(2,1)S(1)} collective-permute-done((bf16[2,16,4096]{2,1,0:T(8,128)(2,1)S(1)}, bf16[2,16,4096]{2,1,0:T(8,128)(2,1)S(1)}, u32[]{:S(2)}, u32[]{:S(2)}) %collective-permute-start.11) | collective-permute-done | bytes 262176 | tf_op jit(solution)/shard_map/ppermute | solution.py:330
  49.8 3.2 %collective-permute-start.15 = (bf16[2,16,4096]{2,1,0:T(8,128)(2,1)S(1)}, bf16[2,16,4096]{2,1,0:T(8,128)(2,1)S(1)}, u32[]{:S(2)}, u32[]{:S(2)}) collective-permute-start(bf16[2,16,4096]{2,1,0:T(8,128)(2,1)S(1)} %get-tuple-element.51), channel_id=1, source_target_pairs={{0,7},{1,0},{2,1},{3,2},{4,3},{5,4},{6,5},{7,6},{8,15},{9,8},{10,9... | collective-permute-start | bytes 786440 | tf_op jit(solution)/shard_map/ppermute | solution.py:330
  53.0 2.2 %collective-permute-done.4 = bf16[2,16,4096]{2,1,0:T(8,128)(2,1)S(1)} collective-permute-done((bf16[2,16,4096]{2,1,0:T(8,128)(2,1)S(1)}, bf16[2,16,4096]{2,1,0:T(8,128)(2,1)S(1)}, u32[]{:S(2)}, u32[]{:S(2)}) %collective-permute-start.4) | collective-permute-done | bytes 262176 | tf_op jit(solution)/shard_map/ppermute | solution.py:334
  55.4 3.5 %collective-permute-start.8 = (bf16[16,4096]{1,0:T(8,128)(2,1)S(1)}, bf16[16,4096]{1,0:T(8,128)(2,1)S(1)}, u32[]{:S(2)}, u32[]{:S(2)}) collective-permute-start(bf16[16,4096]{1,0:T(8,128)(2,1)S(1)} %get-tuple-element.55), channel_id=1, source_target_pairs={{0,7},{1,0},{2,1},{3,2},{4,3},{5,4},{6,5},{7,6},{8,15},{9,8},{10,9... | collective-permute-start | bytes 393224 | tf_op jit(solution)/shard_map/ppermute | solution.py:330
  59.6 3.2 %collective-permute-start.16 = (bf16[2,16,4096]{2,1,0:T(8,128)(2,1)S(1)}, bf16[2,16,4096]{2,1,0:T(8,128)(2,1)S(1)}, u32[]{:S(2)}, u32[]{:S(2)}) collective-permute-start(bf16[2,16,4096]{2,1,0:T(8,128)(2,1)S(1)} %get-tuple-element.49), channel_id=1, source_target_pairs={{0,7},{1,0},{2,1},{3,2},{4,3},{5,4},{6,5},{7,6},{8,15},{9,8},{10,9... | collective-permute-start | bytes 786440 | tf_op jit(solution)/shard_map/ppermute | solution.py:330
  63.3 3.0 %collective-permute-start.9 = (bf16[16,4096]{1,0:T(8,128)(2,1)S(1)}, bf16[16,4096]{1,0:T(8,128)(2,1)S(1)}, u32[]{:S(2)}, u32[]{:S(2)}) collective-permute-start(bf16[16,4096]{1,0:T(8,128)(2,1)S(1)} %get-tuple-element.40), channel_id=1, source_target_pairs={{0,7},{1,0},{2,1},{3,2},{4,3},{5,4},{6,5},{7,6},{8,15},{9,8},{10,9... | collective-permute-start | bytes 393224 | tf_op jit(solution)/shard_map/ppermute | solution.py:330
  66.3 3.0 %collective-permute-done.13 = bf16[2,16,4096]{2,1,0:T(8,128)(2,1)S(1)} collective-permute-done((bf16[2,16,4096]{2,1,0:T(8,128)(2,1)S(1)}, bf16[2,16,4096]{2,1,0:T(8,128)(2,1)S(1)}, u32[]{:S(2)}, u32[]{:S(2)}) %collective-permute-start.13) | collective-permute-done | bytes 262176 | tf_op jit(solution)/shard_map/ppermute | solution.py:330
  70.9 1.1 %collective-permute-done.7 = bf16[16,4096]{1,0:T(8,128)(2,1)S(1)} collective-permute-done((bf16[16,4096]{1,0:T(8,128)(2,1)S(1)}, bf16[16,4096]{1,0:T(8,128)(2,1)S(1)}, u32[]{:S(2)}, u32[]{:S(2)}) %collective-permute-start.7) | collective-permute-done | bytes 131104 | tf_op jit(solution)/shard_map/ppermute | solution.py:330
  72.2 5.7 %collective-permute-done.17 = bf16[16,4096]{1,0:T(8,128)(2,1)S(1)} collective-permute-done((bf16[16,4096]{1,0:T(8,128)(2,1)S(1)}, bf16[16,4096]{1,0:T(8,128)(2,1)S(1)}, u32[]{:S(2)}, u32[]{:S(2)}) %collective-permute-start.17) | collective-permute-done | bytes 131104 | tf_op jit(solution)/shard_map/ppermute | solution.py:334
  (44 shorter events, 6.4 us)
Async XLA Ops:
  0.0 13.4 %copy-start = (f32[16,512]{1,0:T(8,128)S(1)}, f32[16,512]{1,0:T(8,128)}, u32[]{:S(2)}) copy-start(f32[16,512]{1,0:T(8,128)} %rate_hbm.1) | copy-start | bytes 98308
  0.0 13.4 %copy-start.1 = (f32[16,512]{1,0:T(8,128)S(1)}, f32[16,512]{1,0:T(8,128)}, u32[]{:S(2)}) copy-start(f32[16,512]{1,0:T(8,128)} %param.8) | copy-start | bytes 98308
  0.8 5.4 %collective-permute-start = (bf16[16,3,512]{2,0,1:T(8,128)(2,1)S(1)}, bf16[16,3,512]{2,0,1:T(8,128)(2,1)S(1)}, u32[]{:S(2)}, u32[]{:S(2)}) collective-permute-start(bf16[16,3,512]{2,0,1:T(8,128)(2,1)S(1)} %slice.94), channel_id=1, source_target_pairs={{0,16},{16,32},{32,48},{48,64},{64,80},{80,96},{96,112},{112,128},... | collective-permute-start | bytes 147464 | tf_op jit(solution)/shard_map/ppermute | solution.py:387
  7.6 11.3 %all-to-all-start = ((bf16[16,16,512]{2,1,0:T(8,128)(2,1)}), bf16[16,16,512]{2,1,0:T(8,128)(2,1)S(1)}, u32[]{:S(2)}, u32[]{:S(2)}) async-start(bf16[16,16,512]{2,1,0:T(8,128)(2,1)} %get-tuple-element.26), calls=%async_computation | async-start | bytes 524288 | tf_op jit(solution)/shard_map/all_to_all | solution.py:414
  21.6 41.2 %collective-permute-start.6 = (bf16[3,16,4096]{2,1,0:T(8,128)(2,1)S(1)}, bf16[3,16,4096]{2,1,0:T(8,128)(2,1)S(1)}, u32[]{:S(2)}, u32[]{:S(2)}) collective-permute-start(bf16[3,16,4096]{2,1,0:T(8,128)(2,1)S(1)} %pad_maximum_fusion), channel_id=1, source_target_pairs={{0,8},{1,9},{2,10},{3,11},{4,12},{5,13},{6,14},{7,15},{8,0},{9,1},... | collective-permute-start | bytes 1179656 | tf_op jit(solution)/shard_map/ppermute | solution.py:334
  24.4 12.3 %collective-permute-start.1 = (bf16[2,16,4096]{2,1,0:T(8,128)(2,1)S(1)}, bf16[2,16,4096]{2,1,0:T(8,128)(2,1)S(1)}, u32[]{:S(2)}, u32[]{:S(2)}) collective-permute-start(bf16[2,16,4096]{2,1,0:T(8,128)(2,1)S(1)} %get-tuple-element.46), channel_id=1, source_target_pairs={{0,1},{1,2},{2,3},{3,4},{4,5},{5,6},{6,7},{7,0},{8,9},{9,10},{10,1... | collective-permute-start | bytes 786440 | tf_op jit(solution)/shard_map/ppermute | solution.py:330
  26.4 15.7 %collective-permute-start.3 = (bf16[2,16,4096]{2,1,0:T(8,128)(2,1)S(1)}, bf16[2,16,4096]{2,1,0:T(8,128)(2,1)S(1)}, u32[]{:S(2)}, u32[]{:S(2)}) collective-permute-start(bf16[2,16,4096]{2,1,0:T(8,128)(2,1)S(1)} %get-tuple-element.47), channel_id=1, source_target_pairs={{0,7},{1,0},{2,1},{3,2},{4,3},{5,4},{6,5},{7,6},{8,15},{9,8},{10,9... | collective-permute-start | bytes 786440 | tf_op jit(solution)/shard_map/ppermute | solution.py:330
  33.4 8.5 %collective-permute-start.10 = (bf16[2,16,4096]{2,1,0:T(8,128)(2,1)S(1)}, bf16[2,16,4096]{2,1,0:T(8,128)(2,1)S(1)}, u32[]{:S(2)}, u32[]{:S(2)}) collective-permute-start(bf16[2,16,4096]{2,1,0:T(8,128)(2,1)S(1)} %get-tuple-element.52), channel_id=1, source_target_pairs={{0,1},{1,2},{2,3},{3,4},{4,5},{5,6},{6,7},{7,0},{8,9},{9,10},{10,1... | collective-permute-start | bytes 786440 | tf_op jit(solution)/shard_map/ppermute | solution.py:330
  33.5 14.3 %collective-permute-start.14 = (bf16[2,16,4096]{2,1,0:T(8,128)(2,1)S(1)}, bf16[2,16,4096]{2,1,0:T(8,128)(2,1)S(1)}, u32[]{:S(2)}, u32[]{:S(2)}) collective-permute-start(bf16[2,16,4096]{2,1,0:T(8,128)(2,1)S(1)} %get-tuple-element.53), channel_id=1, source_target_pairs={{0,7},{1,0},{2,1},{3,2},{4,3},{5,4},{6,5},{7,6},{8,15},{9,8},{10,9... | collective-permute-start | bytes 786440 | tf_op jit(solution)/shard_map/ppermute | solution.py:330
  36.8 9.9 %collective-permute-start.2 = (bf16[2,16,4096]{2,1,0:T(8,128)(2,1)S(1)}, bf16[2,16,4096]{2,1,0:T(8,128)(2,1)S(1)}, u32[]{:S(2)}, u32[]{:S(2)}) collective-permute-start(bf16[2,16,4096]{2,1,0:T(8,128)(2,1)S(1)} %fusion.7), channel_id=1, source_target_pairs={{0,1},{1,2},{2,3},{3,4},{4,5},{5,6},{6,7},{7,0},{8,9},{9,10},{10,1... | collective-permute-start | bytes 786440 | tf_op jit(solution)/shard_map/ppermute | solution.py:330
  41.9 7.7 %collective-permute-start.11 = (bf16[2,16,4096]{2,1,0:T(8,128)(2,1)S(1)}, bf16[2,16,4096]{2,1,0:T(8,128)(2,1)S(1)}, u32[]{:S(2)}, u32[]{:S(2)}) collective-permute-start(bf16[2,16,4096]{2,1,0:T(8,128)(2,1)S(1)} %fusion.4), channel_id=1, source_target_pairs={{0,1},{1,2},{2,3},{3,4},{4,5},{5,6},{6,7},{7,0},{8,9},{9,10},{10,1... | collective-permute-start | bytes 786440 | tf_op jit(solution)/shard_map/ppermute | solution.py:330
  46.9 8.4 %collective-permute-start.4 = (bf16[2,16,4096]{2,1,0:T(8,128)(2,1)S(1)}, bf16[2,16,4096]{2,1,0:T(8,128)(2,1)S(1)}, u32[]{:S(2)}, u32[]{:S(2)}) collective-permute-start(bf16[2,16,4096]{2,1,0:T(8,128)(2,1)S(1)} %pad_maximum_fusion.1), channel_id=1, source_target_pairs={{0,8},{1,9},{2,10},{3,11},{4,12},{5,13},{6,14},{7,15},{8,0},{9,1},... | collective-permute-start | bytes 786440 | tf_op jit(solution)/shard_map/ppermute | solution.py:334
  49.7 9.7 %collective-permute-start.12 = (bf16[2,16,4096]{2,1,0:T(8,128)(2,1)S(1)}, bf16[2,16,4096]{2,1,0:T(8,128)(2,1)S(1)}, u32[]{:S(2)}, u32[]{:S(2)}) collective-permute-start(bf16[2,16,4096]{2,1,0:T(8,128)(2,1)S(1)} %get-tuple-element.50), channel_id=1, source_target_pairs={{0,1},{1,2},{2,3},{3,4},{4,5},{5,6},{6,7},{7,0},{8,9},{9,10},{10,1... | collective-permute-start | bytes 786440 | tf_op jit(solution)/shard_map/ppermute | solution.py:330
  49.8 9.6 %collective-permute-start.15 = (bf16[2,16,4096]{2,1,0:T(8,128)(2,1)S(1)}, bf16[2,16,4096]{2,1,0:T(8,128)(2,1)S(1)}, u32[]{:S(2)}, u32[]{:S(2)}) collective-permute-start(bf16[2,16,4096]{2,1,0:T(8,128)(2,1)S(1)} %get-tuple-element.51), channel_id=1, source_target_pairs={{0,7},{1,0},{2,1},{3,2},{4,3},{5,4},{6,5},{7,6},{8,15},{9,8},{10,9... | collective-permute-start | bytes 786440 | tf_op jit(solution)/shard_map/ppermute | solution.py:330
  55.3 7.5 %collective-permute-start.5 = (bf16[16,4096]{1,0:T(8,128)(2,1)S(1)}, bf16[16,4096]{1,0:T(8,128)(2,1)S(1)}, u32[]{:S(2)}, u32[]{:S(2)}) collective-permute-start(bf16[16,4096]{1,0:T(8,128)(2,1)S(1)} %get-tuple-element.54), channel_id=1, source_target_pairs={{0,1},{1,2},{2,3},{3,4},{4,5},{5,6},{6,7},{7,0},{8,9},{9,10},{10,1... | collective-permute-start | bytes 393224 | tf_op jit(solution)/shard_map/ppermute | solution.py:330
  55.4 7.4 %collective-permute-start.8 = (bf16[16,4096]{1,0:T(8,128)(2,1)S(1)}, bf16[16,4096]{1,0:T(8,128)(2,1)S(1)}, u32[]{:S(2)}, u32[]{:S(2)}) collective-permute-start(bf16[16,4096]{1,0:T(8,128)(2,1)S(1)} %get-tuple-element.55), channel_id=1, source_target_pairs={{0,7},{1,0},{2,1},{3,2},{4,3},{5,4},{6,5},{7,6},{8,15},{9,8},{10,9... | collective-permute-start | bytes 393224 | tf_op jit(solution)/shard_map/ppermute | solution.py:330
  59.5 9.8 %collective-permute-start.13 = (bf16[2,16,4096]{2,1,0:T(8,128)(2,1)S(1)}, bf16[2,16,4096]{2,1,0:T(8,128)(2,1)S(1)}, u32[]{:S(2)}, u32[]{:S(2)}) collective-permute-start(bf16[2,16,4096]{2,1,0:T(8,128)(2,1)S(1)} %get-tuple-element.48), channel_id=1, source_target_pairs={{0,1},{1,2},{2,3},{3,4},{4,5},{5,6},{6,7},{7,0},{8,9},{9,10},{10,1... | collective-permute-start | bytes 786440 | tf_op jit(solution)/shard_map/ppermute | solution.py:330
  59.6 10.2 %collective-permute-start.16 = (bf16[2,16,4096]{2,1,0:T(8,128)(2,1)S(1)}, bf16[2,16,4096]{2,1,0:T(8,128)(2,1)S(1)}, u32[]{:S(2)}, u32[]{:S(2)}) collective-permute-start(bf16[2,16,4096]{2,1,0:T(8,128)(2,1)S(1)} %get-tuple-element.49), channel_id=1, source_target_pairs={{0,7},{1,0},{2,1},{3,2},{4,3},{5,4},{6,5},{7,6},{8,15},{9,8},{10,9... | collective-permute-start | bytes 786440 | tf_op jit(solution)/shard_map/ppermute | solution.py:330
  63.0 9.1 %collective-permute-start.7 = (bf16[16,4096]{1,0:T(8,128)(2,1)S(1)}, bf16[16,4096]{1,0:T(8,128)(2,1)S(1)}, u32[]{:S(2)}, u32[]{:S(2)}) collective-permute-start(bf16[16,4096]{1,0:T(8,128)(2,1)S(1)} %get-tuple-element.39), channel_id=1, source_target_pairs={{0,1},{1,2},{2,3},{3,4},{4,5},{5,6},{6,7},{7,0},{8,9},{9,10},{10,1... | collective-permute-start | bytes 393224 | tf_op jit(solution)/shard_map/ppermute | solution.py:330
  63.3 8.8 %collective-permute-start.9 = (bf16[16,4096]{1,0:T(8,128)(2,1)S(1)}, bf16[16,4096]{1,0:T(8,128)(2,1)S(1)}, u32[]{:S(2)}, u32[]{:S(2)}) collective-permute-start(bf16[16,4096]{1,0:T(8,128)(2,1)S(1)} %get-tuple-element.40), channel_id=1, source_target_pairs={{0,7},{1,0},{2,1},{3,2},{4,3},{5,4},{6,5},{7,6},{8,15},{9,8},{10,9... | collective-permute-start | bytes 393224 | tf_op jit(solution)/shard_map/ppermute | solution.py:330
  69.9 7.9 %collective-permute-start.17 = (bf16[16,4096]{1,0:T(8,128)(2,1)S(1)}, bf16[16,4096]{1,0:T(8,128)(2,1)S(1)}, u32[]{:S(2)}, u32[]{:S(2)}) collective-permute-start(bf16[16,4096]{1,0:T(8,128)(2,1)S(1)} %fusion.15), channel_id=1, source_target_pairs={{0,8},{1,9},{2,10},{3,11},{4,12},{5,13},{6,14},{7,15},{8,0},{9,1},... | collective-permute-start | bytes 393224 | tf_op jit(solution)/shard_map/ppermute | solution.py:334

commit v4 on v3

--- a/solution.py
+++ b/solution.py
@@ -338,6 +338,8 @@
     part = part.reshape(2, NZ, 16, -1)
     left = {longer: NZ // 2, -longer: NZ // 2 - 1}
     total = {way: part[:, way * k % NZ] for way, k in left.items()}
+    near = range(1 - meet, meet)
+    got = None
     for _ in range(NZ // 2 - meet):
         for way in left:
             if left[way] > meet:
@@ -345,11 +347,12 @@
                 total[way] = along(total[way], way)
                 if left[way]:
                     total[way] = plus(total[way], part[:, way * left[way] % NZ])
+        if meet and got is None:
+            mine = jnp.stack([part[1, k % NZ] for k in near])
+            got = across(lax.optimization_barrier((mine, total[-longer]))[0])
     if meet == 0:
         both = total[1].astype(f32) + total[-1].astype(f32) + part[:, 0].astype(f32)
         return plus(both[0], across(both[1].astype(bf16)))
-    near = range(1 - meet, meet)
-    got = across(jnp.stack([part[1, k % NZ] for k in near]))
     close = {k: plus(part[0, k % NZ], got[i]) for i, k in enumerate(near)}
     other = across(jnp.stack([total[1][1], total[-1][1]]))
     total = {1: plus(total[1][0], other[0]), -1: plus(total[-1][0], other[1])}

time: 79.2 us -> 76.9 us (0.971)
  waiting for transfers between devices: 27.7 us -> 23.4 us
  starting transfers between devices: 35.3 us -> 37 us
    ppermute x14, waiting for transfers between devices: 16.7 us -> 12.8 us  [along(): return lax.ppermute(x, ('ctx', 'tp'), ring_pairs(lax.axis_size('ctx'), way))]
    ppermute x3, starting transfers between devices: 4.69 us -> 6.36 us  [across(): return lax.ppermute(x, 'tp', half_pairs())]
  transfers between devices with their start and end apart: 19 -> 19, of which waited for: 11 -> 8; matrix products, arithmetic and copies ran while one was open for 1% -> 1% of each run, Pallas kernels for 11% -> 12%
where the time goes in v4:
time: 76.9 us; the launch traced here: 76 us
  starting transfers between devices  37 us (48%)
  waiting for transfers between devices  23.4 us (30%)
  Pallas kernels  12.8 us (17%)
  other arithmetic  1.67 us (2%)
  local copies, waits for them, and re-layouts  0.95 us (1%)
    ppermute x14, starting transfers between devices, along(): return lax.ppermute(x, ('ctx', 'tp'), ring_pairs(lax.axis_size('ctx'), way))  22.8 us
    ppermute x14, waiting for transfers between devices, along(): return lax.ppermute(x, ('ctx', 'tp'), ring_pairs(lax.axis_size('ctx'), way))  12.8 us
    pallas_call x5, Pallas kernels, call(): pl.pallas_call(kernel, in_specs=in_specs, out_specs=[pl.BlockSpec(memory_...  12.8 us
    ppermute x3, waiting for transfers between devices, across(): return lax.ppermute(x, 'tp', half_pairs())  7.5 us
    ppermute x3, starting transfers between devices, across(): return lax.ppermute(x, 'tp', half_pairs())  6.36 us
    all_to_all x1, starting transfers between devices, local(): recv = lax.all_to_all(send, 'ctx', 0, 0, tiled=True)  5.86 us
    all_to_all x1, waiting for transfers between devices, local(): recv = lax.all_to_all(send, 'ctx', 0, 0, tiled=True)  1.92 us
    ppermute x1, starting transfers between devices, local(): lax.ppermute(features[rows - HALO:], 'ctx', [(i, i + 1) for i in range(n_...  1.91 us
  transfers between devices with their start and end apart: 19, of which 8 were waited for; matrix products, arithmetic and copies ran while one was open for 1% of the time, Pallas kernels for 12%

profile of v4, /device:TPU:8, one launch (start us, length us, event | category | flops | bytes accessed | tf_op | source)
XLA Modules:
  0.0 76.0 jit_solution(4725741770164141484)
XLA Ops:
  0.8 1.9 %collective-permute-start = (bf16[16,3,512]{2,0,1:T(8,128)(2,1)S(1)}, bf16[16,3,512]{2,0,1:T(8,128)(2,1)S(1)}, u32[]{:S(2)}, u32[]{:S(2)}) collective-permute-start(bf16[16,3,512]{2,0,1:T(8,128)(2,1)S(1)} %slice.94), channel_id=1, source_target_pairs={{0,16},{16,32},{32,48},{48,64},{64,80},{80,96},{96,112},{112,128},... | collective-permute-start | bytes 147464 | tf_op jit(solution)/shard_map/ppermute | solution.py:390
  2.7 2.3 %bulk.1 = (f32[2,96,512]{2,1,0:T(8,128)S(1)}, f32[256,512]{1,0:T(8,128)S(1)}, f32[16,8,512]{2,1,0:T(8,128)S(1)}, f32[3,7,512]{2,1,0:T(8,128)S(1)}, f32[16,512]{1,0:T(8,128)S(1)}) custom-call(bf16[3,256,512]{2,1,0:T(8,128)(2,1)} %bitcast.142, f32[3,7,512]{2,1,0:T(8,128)} %taps_hbm.1, f32[16,512]{1,0:T(8,128)} %rate_hbm.1), custom_call_target="tpu_custom_call" | custom-call | flops 8388608 | bytes 4194304 | tf_op jit(solution)/shard_map/bulk/pallas_call | solution.py:372
  5.1 1.1 %collective-permute-done = bf16[16,3,512]{2,0,1:T(8,128)(2,1)S(1)} collective-permute-done((bf16[16,3,512]{2,0,1:T(8,128)(2,1)S(1)}, bf16[16,3,512]{2,0,1:T(8,128)(2,1)S(1)}, u32[]{:S(2)}, u32[]{:S(2)}) %collective-permute-start) | collective-permute-done | bytes 49184 | tf_op jit(solution)/shard_map/ppermute | solution.py:390
  6.2 1.4 %edge.1 = (f32[48,512]{1,0:T(8,128)S(1)}, f32[16,8,512]{2,1,0:T(8,128)S(1)}, bf16[16,16,512]{2,1,0:T(8,128)(2,1)}) custom-call(f32[2,96,512]{2,1,0:T(8,128)S(1)} %get-tuple-element.23.head_ref, bf16[3,16,512]{2,1,0:T(8,128)(2,1)S(1)} %bitcast.140, f32[3,7,512]{2,1,0:T(8,128)S(1)} %get-tuple-element.24.taps_ref, f32[16,512]{1,0:T(8,128)S(1)} %get-tuple-element.25.rate_ref, ...), custom_call_target="tpu_custom_call" | custom-call | flops 2097152 | bytes 4194304 | tf_op jit(solution)/shard_map/edge/pallas_call | solution.py:372
  7.6 5.9 %all-to-all-start = ((bf16[16,16,512]{2,1,0:T(8,128)(2,1)}), bf16[16,16,512]{2,1,0:T(8,128)(2,1)S(1)}, u32[]{:S(2)}, u32[]{:S(2)}) async-start(bf16[16,16,512]{2,1,0:T(8,128)(2,1)} %get-tuple-element.27), calls=%async_computation | async-start | bytes 524288 | tf_op jit(solution)/shard_map/all_to_all | solution.py:417
  13.5 3.5 %inner.1 = (f32[256,512]{1,0:T(8,128)S(1)}, f32[256,512]{1,0:T(8,128)S(1)}, f32[16,8,512]{2,1,0:T(8,128)S(1)}, bf16[256,256]{1,0:T(8,128)(2,1)S(1)}, bf16[512,1024]{1,0:T(8,128)(2,1)S(1)}) custom-call(bf16[3,256,512]{2,1,0:T(8,128)(2,1)} %bitcast.143, bf16[512,8192]{1,0:T(8,128)(2,1)} %weight_hbm.5, ...), custom_call_target="tpu_custom_call", output_to_operand_aliasing={{1}: (6, {})} | custom-call | flops 16777216 | bytes 4194304 | tf_op jit(solution)/shard_map/inner/pallas_call | solution.py:372
  17.0 1.9 %all-to-all-done.recv_ref = bf16[16,16,512]{2,1,0:T(8,128)(2,1)S(1)} async-done(((bf16[16,16,512]{2,1,0:T(8,128)(2,1)}), bf16[16,16,512]{2,1,0:T(8,128)(2,1)S(1)}, u32[]{:S(2)}, u32[]{:S(2)}) %all-to-all-start) | async-done | bytes 262176 | tf_op jit(solution)/shard_map/all_to_all | solution.py:417
  18.9 2.6 %gate.1 = (bf16[256,512]{1,0:T(8,128)(2,1)S(1)}, bf16[256,4096]{1,0:T(8,128)(2,1)S(1)}) custom-call(bf16[512,8192]{1,0:T(8,128)(2,1)} %weight_hbm.5, bf16[16,16,512]{2,1,0:T(8,128)(2,1)S(1)} %all-to-all-done.recv_ref, f32[16,512]{1,0:T(8,128)S(1)} %get-tuple-element.25.rate_ref, f32[16,8,512]{2,1,0:T(8,128)S(1)} %get-tuple-element.33.lead_ref, ...), custom_call_target="tpu_custom_call" | custom-call | flops 1073741824 | bytes 4194304 | tf_op jit(solution)/shard_map/gate/pallas_call | solution.py:372
  21.6 2.0 %collective-permute-start.1 = (bf16[2,16,4096]{2,1,0:T(8,128)(2,1)S(1)}, bf16[2,16,4096]{2,1,0:T(8,128)(2,1)S(1)}, u32[]{:S(2)}, u32[]{:S(2)}) collective-permute-start(bf16[2,16,4096]{2,1,0:T(8,128)(2,1)S(1)} %get-tuple-element.48), channel_id=1, source_target_pairs={{0,1},{1,2},{2,3},{3,4},{4,5},{5,6},{6,7},{7,0},{8,9},{9,10},{10,1... | collective-permute-start | bytes 786440 | tf_op jit(solution)/shard_map/ppermute | solution.py:330
  23.6 4.0 %collective-permute-start.3 = (bf16[2,16,4096]{2,1,0:T(8,128)(2,1)S(1)}, bf16[2,16,4096]{2,1,0:T(8,128)(2,1)S(1)}, u32[]{:S(2)}, u32[]{:S(2)}) collective-permute-start(bf16[2,16,4096]{2,1,0:T(8,128)(2,1)S(1)} %get-tuple-element.49), channel_id=1, source_target_pairs={{0,7},{1,0},{2,1},{3,2},{4,3},{5,4},{6,5},{7,6},{8,15},{9,8},{10,9... | collective-permute-start | bytes 786440 | tf_op jit(solution)/shard_map/ppermute | solution.py:330
  27.6 3.0 %project.1 = bf16[256,4096]{1,0:T(8,128)(2,1)S(1)} custom-call(bf16[512,8192]{1,0:T(8,128)(2,1)} %weight_hbm.5, bf16[256,512]{1,0:T(8,128)(2,1)S(1)} %get-tuple-element.40.gated_ref), custom_call_target="tpu_custom_call" | custom-call | flops 1073741824 | bytes 4194304 | tf_op jit(solution)/shard_map/project/pallas_call | solution.py:372
  30.8 3.2 %collective-permute-start.14 = (bf16[2,16,4096]{2,1,0:T(8,128)(2,1)S(1)}, bf16[2,16,4096]{2,1,0:T(8,128)(2,1)S(1)}, u32[]{:S(2)}, u32[]{:S(2)}) collective-permute-start(bf16[2,16,4096]{2,1,0:T(8,128)(2,1)S(1)} %get-tuple-element.55), channel_id=1, source_target_pairs={{0,7},{1,0},{2,1},{3,2},{4,3},{5,4},{6,5},{7,6},{8,15},{9,8},{10,9... | collective-permute-start | bytes 786440 | tf_op jit(solution)/shard_map/ppermute | solution.py:330
  34.2 4.8 %collective-permute-done.10 = bf16[2,16,4096]{2,1,0:T(8,128)(2,1)S(1)} collective-permute-done((bf16[2,16,4096]{2,1,0:T(8,128)(2,1)S(1)}, bf16[2,16,4096]{2,1,0:T(8,128)(2,1)S(1)}, u32[]{:S(2)}, u32[]{:S(2)}) %collective-permute-start.10) | collective-permute-done | bytes 262176 | tf_op jit(solution)/shard_map/ppermute | solution.py:330
  39.1 4.8 %collective-permute-done.2 = bf16[2,16,4096]{2,1,0:T(8,128)(2,1)S(1)} collective-permute-done((bf16[2,16,4096]{2,1,0:T(8,128)(2,1)S(1)}, bf16[2,16,4096]{2,1,0:T(8,128)(2,1)S(1)}, u32[]{:S(2)}, u32[]{:S(2)}) %collective-permute-start.2) | collective-permute-done | bytes 262176 | tf_op jit(solution)/shard_map/ppermute | solution.py:330
  44.1 2.8 %collective-permute-start.4 = (bf16[2,16,4096]{2,1,0:T(8,128)(2,1)S(1)}, bf16[2,16,4096]{2,1,0:T(8,128)(2,1)S(1)}, u32[]{:S(2)}, u32[]{:S(2)}) collective-permute-start(bf16[2,16,4096]{2,1,0:T(8,128)(2,1)S(1)} %pad_maximum_fusion.1), channel_id=1, source_target_pairs={{0,8},{1,9},{2,10},{3,11},{4,12},{5,13},{6,14},{7,15},{8,0},{9,1},... | collective-permute-start | bytes 786440 | tf_op jit(solution)/shard_map/ppermute | solution.py:334
  48.0 3.2 %collective-permute-start.15 = (bf16[2,16,4096]{2,1,0:T(8,128)(2,1)S(1)}, bf16[2,16,4096]{2,1,0:T(8,128)(2,1)S(1)}, u32[]{:S(2)}, u32[]{:S(2)}) collective-permute-start(bf16[2,16,4096]{2,1,0:T(8,128)(2,1)S(1)} %get-tuple-element.53), channel_id=1, source_target_pairs={{0,7},{1,0},{2,1},{3,2},{4,3},{5,4},{6,5},{7,6},{8,15},{9,8},{10,9... | collective-permute-start | bytes 786440 | tf_op jit(solution)/shard_map/ppermute | solution.py:330
  51.2 3.8 %collective-permute-done.4 = bf16[2,16,4096]{2,1,0:T(8,128)(2,1)S(1)} collective-permute-done((bf16[2,16,4096]{2,1,0:T(8,128)(2,1)S(1)}, bf16[2,16,4096]{2,1,0:T(8,128)(2,1)S(1)}, u32[]{:S(2)}, u32[]{:S(2)}) %collective-permute-start.4) | collective-permute-done | bytes 262176 | tf_op jit(solution)/shard_map/ppermute | solution.py:334
  55.1 3.2 %collective-permute-start.8 = (bf16[16,4096]{1,0:T(8,128)(2,1)S(1)}, bf16[16,4096]{1,0:T(8,128)(2,1)S(1)}, u32[]{:S(2)}, u32[]{:S(2)}) collective-permute-start(bf16[16,4096]{1,0:T(8,128)(2,1)S(1)} %get-tuple-element.57), channel_id=1, source_target_pairs={{0,7},{1,0},{2,1},{3,2},{4,3},{5,4},{6,5},{7,6},{8,15},{9,8},{10,9... | collective-permute-start | bytes 393224 | tf_op jit(solution)/shard_map/ppermute | solution.py:330
  58.6 3.2 %collective-permute-start.16 = (bf16[2,16,4096]{2,1,0:T(8,128)(2,1)S(1)}, bf16[2,16,4096]{2,1,0:T(8,128)(2,1)S(1)}, u32[]{:S(2)}, u32[]{:S(2)}) collective-permute-start(bf16[2,16,4096]{2,1,0:T(8,128)(2,1)S(1)} %get-tuple-element.51), channel_id=1, source_target_pairs={{0,7},{1,0},{2,1},{3,2},{4,3},{5,4},{6,5},{7,6},{8,15},{9,8},{10,9... | collective-permute-start | bytes 786440 | tf_op jit(solution)/shard_map/ppermute | solution.py:330
  61.8 0.9 %collective-permute-done.5 = bf16[16,4096]{1,0:T(8,128)(2,1)S(1)} collective-permute-done((bf16[16,4096]{1,0:T(8,128)(2,1)S(1)}, bf16[16,4096]{1,0:T(8,128)(2,1)S(1)}, u32[]{:S(2)}, u32[]{:S(2)}) %collective-permute-start.5) | collective-permute-done | bytes 131104 | tf_op jit(solution)/shard_map/ppermute | solution.py:330
  62.9 3.3 %collective-permute-start.9 = (bf16[16,4096]{1,0:T(8,128)(2,1)S(1)}, bf16[16,4096]{1,0:T(8,128)(2,1)S(1)}, u32[]{:S(2)}, u32[]{:S(2)}) collective-permute-start(bf16[16,4096]{1,0:T(8,128)(2,1)S(1)} %get-tuple-element.42), channel_id=1, source_target_pairs={{0,7},{1,0},{2,1},{3,2},{4,3},{5,4},{6,5},{7,6},{8,15},{9,8},{10,9... | collective-permute-start | bytes 393224 | tf_op jit(solution)/shard_map/ppermute | solution.py:330
  66.2 2.3 %collective-permute-done.13 = bf16[2,16,4096]{2,1,0:T(8,128)(2,1)S(1)} collective-permute-done((bf16[2,16,4096]{2,1,0:T(8,128)(2,1)S(1)}, bf16[2,16,4096]{2,1,0:T(8,128)(2,1)S(1)}, u32[]{:S(2)}, u32[]{:S(2)}) %collective-permute-start.13) | collective-permute-done | bytes 262176 | tf_op jit(solution)/shard_map/ppermute | solution.py:330
  68.7 2.7 %collective-permute-start.17 = (bf16[16,4096]{1,0:T(8,128)(2,1)S(1)}, bf16[16,4096]{1,0:T(8,128)(2,1)S(1)}, u32[]{:S(2)}, u32[]{:S(2)}) collective-permute-start(bf16[16,4096]{1,0:T(8,128)(2,1)S(1)} %fusion.15), channel_id=1, source_target_pairs={{0,8},{1,9},{2,10},{3,11},{4,12},{5,13},{6,14},{7,15},{8,0},{9,1},... | collective-permute-start | bytes 393224 | tf_op jit(solution)/shard_map/ppermute | solution.py:334
  71.5 3.7 %collective-permute-done.17 = bf16[16,4096]{1,0:T(8,128)(2,1)S(1)} collective-permute-done((bf16[16,4096]{1,0:T(8,128)(2,1)S(1)}, bf16[16,4096]{1,0:T(8,128)(2,1)S(1)}, u32[]{:S(2)}, u32[]{:S(2)}) %collective-permute-start.17) | collective-permute-done | bytes 131104 | tf_op jit(solution)/shard_map/ppermute | solution.py:334
  (44 shorter events, 4.0 us)
Async XLA Ops:
  0.0 13.4 %copy-start = (f32[16,512]{1,0:T(8,128)S(1)}, f32[16,512]{1,0:T(8,128)}, u32[]{:S(2)}) copy-start(f32[16,512]{1,0:T(8,128)} %rate_hbm.1) | copy-start | bytes 98308
  0.0 13.4 %copy-start.1 = (f32[16,512]{1,0:T(8,128)S(1)}, f32[16,512]{1,0:T(8,128)}, u32[]{:S(2)}) copy-start(f32[16,512]{1,0:T(8,128)} %param.8) | copy-start | bytes 98308
  0.8 5.4 %collective-permute-start = (bf16[16,3,512]{2,0,1:T(8,128)(2,1)S(1)}, bf16[16,3,512]{2,0,1:T(8,128)(2,1)S(1)}, u32[]{:S(2)}, u32[]{:S(2)}) collective-permute-start(bf16[16,3,512]{2,0,1:T(8,128)(2,1)S(1)} %slice.94), channel_id=1, source_target_pairs={{0,16},{16,32},{32,48},{48,64},{64,80},{80,96},{96,112},{112,128},... | collective-permute-start | bytes 147464 | tf_op jit(solution)/shard_map/ppermute | solution.py:390
  7.6 11.3 %all-to-all-start = ((bf16[16,16,512]{2,1,0:T(8,128)(2,1)}), bf16[16,16,512]{2,1,0:T(8,128)(2,1)S(1)}, u32[]{:S(2)}, u32[]{:S(2)}) async-start(bf16[16,16,512]{2,1,0:T(8,128)(2,1)} %get-tuple-element.27), calls=%async_computation | async-start | bytes 524288 | tf_op jit(solution)/shard_map/all_to_all | solution.py:417
  21.6 12.5 %collective-permute-start.1 = (bf16[2,16,4096]{2,1,0:T(8,128)(2,1)S(1)}, bf16[2,16,4096]{2,1,0:T(8,128)(2,1)S(1)}, u32[]{:S(2)}, u32[]{:S(2)}) collective-permute-start(bf16[2,16,4096]{2,1,0:T(8,128)(2,1)S(1)} %get-tuple-element.48), channel_id=1, source_target_pairs={{0,1},{1,2},{2,3},{3,4},{4,5},{5,6},{6,7},{7,0},{8,9},{9,10},{10,1... | collective-permute-start | bytes 786440 | tf_op jit(solution)/shard_map/ppermute | solution.py:330
  23.6 15.6 %collective-permute-start.3 = (bf16[2,16,4096]{2,1,0:T(8,128)(2,1)S(1)}, bf16[2,16,4096]{2,1,0:T(8,128)(2,1)S(1)}, u32[]{:S(2)}, u32[]{:S(2)}) collective-permute-start(bf16[2,16,4096]{2,1,0:T(8,128)(2,1)S(1)} %get-tuple-element.49), channel_id=1, source_target_pairs={{0,7},{1,0},{2,1},{3,2},{4,3},{5,4},{6,5},{7,6},{8,15},{9,8},{10,9... | collective-permute-start | bytes 786440 | tf_op jit(solution)/shard_map/ppermute | solution.py:330
  30.7 8.3 %collective-permute-start.10 = (bf16[2,16,4096]{2,1,0:T(8,128)(2,1)S(1)}, bf16[2,16,4096]{2,1,0:T(8,128)(2,1)S(1)}, u32[]{:S(2)}, u32[]{:S(2)}) collective-permute-start(bf16[2,16,4096]{2,1,0:T(8,128)(2,1)S(1)} %get-tuple-element.54), channel_id=1, source_target_pairs={{0,1},{1,2},{2,3},{3,4},{4,5},{5,6},{6,7},{7,0},{8,9},{9,10},{10,1... | collective-permute-start | bytes 786440 | tf_op jit(solution)/shard_map/ppermute | solution.py:330
  30.8 17.0 %collective-permute-start.14 = (bf16[2,16,4096]{2,1,0:T(8,128)(2,1)S(1)}, bf16[2,16,4096]{2,1,0:T(8,128)(2,1)S(1)}, u32[]{:S(2)}, u32[]{:S(2)}) collective-permute-start(bf16[2,16,4096]{2,1,0:T(8,128)(2,1)S(1)} %get-tuple-element.55), channel_id=1, source_target_pairs={{0,7},{1,0},{2,1},{3,2},{4,3},{5,4},{6,5},{7,6},{8,15},{9,8},{10,9... | collective-permute-start | bytes 786440 | tf_op jit(solution)/shard_map/ppermute | solution.py:330
  34.1 9.8 %collective-permute-start.2 = (bf16[2,16,4096]{2,1,0:T(8,128)(2,1)S(1)}, bf16[2,16,4096]{2,1,0:T(8,128)(2,1)S(1)}, u32[]{:S(2)}, u32[]{:S(2)}) collective-permute-start(bf16[2,16,4096]{2,1,0:T(8,128)(2,1)S(1)} %fusion.7), channel_id=1, source_target_pairs={{0,1},{1,2},{2,3},{3,4},{4,5},{5,6},{6,7},{7,0},{8,9},{9,10},{10,1... | collective-permute-start | bytes 786440 | tf_op jit(solution)/shard_map/ppermute | solution.py:330
  39.0 8.7 %collective-permute-start.11 = (bf16[2,16,4096]{2,1,0:T(8,128)(2,1)S(1)}, bf16[2,16,4096]{2,1,0:T(8,128)(2,1)S(1)}, u32[]{:S(2)}, u32[]{:S(2)}) collective-permute-start(bf16[2,16,4096]{2,1,0:T(8,128)(2,1)S(1)} %fusion.4), channel_id=1, source_target_pairs={{0,1},{1,2},{2,3},{3,4},{4,5},{5,6},{6,7},{7,0},{8,9},{9,10},{10,1... | collective-permute-start | bytes 786440 | tf_op jit(solution)/shard_map/ppermute | solution.py:330
  44.1 10.8 %collective-permute-start.4 = (bf16[2,16,4096]{2,1,0:T(8,128)(2,1)S(1)}, bf16[2,16,4096]{2,1,0:T(8,128)(2,1)S(1)}, u32[]{:S(2)}, u32[]{:S(2)}) collective-permute-start(bf16[2,16,4096]{2,1,0:T(8,128)(2,1)S(1)} %pad_maximum_fusion.1), channel_id=1, source_target_pairs={{0,8},{1,9},{2,10},{3,11},{4,12},{5,13},{6,14},{7,15},{8,0},{9,1},... | collective-permute-start | bytes 786440 | tf_op jit(solution)/shard_map/ppermute | solution.py:334
  47.0 15.7 %collective-permute-start.6 = (bf16[3,16,4096]{2,1,0:T(8,128)(2,1)S(1)}, bf16[3,16,4096]{2,1,0:T(8,128)(2,1)S(1)}, u32[]{:S(2)}, u32[]{:S(2)}) collective-permute-start(bf16[3,16,4096]{2,1,0:T(8,128)(2,1)S(1)} %pad_maximum_fusion), channel_id=1, source_target_pairs={{0,8},{1,9},{2,10},{3,11},{4,12},{5,13},{6,14},{7,15},{8,0},{9,1},... | collective-permute-start | bytes 1179656 | tf_op jit(solution)/shard_map/ppermute | solution.py:334
  47.9 10.5 %collective-permute-start.12 = (bf16[2,16,4096]{2,1,0:T(8,128)(2,1)S(1)}, bf16[2,16,4096]{2,1,0:T(8,128)(2,1)S(1)}, u32[]{:S(2)}, u32[]{:S(2)}) collective-permute-start(bf16[2,16,4096]{2,1,0:T(8,128)(2,1)S(1)} %get-tuple-element.52), channel_id=1, source_target_pairs={{0,1},{1,2},{2,3},{3,4},{4,5},{5,6},{6,7},{7,0},{8,9},{9,10},{10,1... | collective-permute-start | bytes 786440 | tf_op jit(solution)/shard_map/ppermute | solution.py:330
  48.0 10.4 %collective-permute-start.15 = (bf16[2,16,4096]{2,1,0:T(8,128)(2,1)S(1)}, bf16[2,16,4096]{2,1,0:T(8,128)(2,1)S(1)}, u32[]{:S(2)}, u32[]{:S(2)}) collective-permute-start(bf16[2,16,4096]{2,1,0:T(8,128)(2,1)S(1)} %get-tuple-element.53), channel_id=1, source_target_pairs={{0,7},{1,0},{2,1},{3,2},{4,3},{5,4},{6,5},{7,6},{8,15},{9,8},{10,9... | collective-permute-start | bytes 786440 | tf_op jit(solution)/shard_map/ppermute | solution.py:330
  55.1 7.6 %collective-permute-start.5 = (bf16[16,4096]{1,0:T(8,128)(2,1)S(1)}, bf16[16,4096]{1,0:T(8,128)(2,1)S(1)}, u32[]{:S(2)}, u32[]{:S(2)}) collective-permute-start(bf16[16,4096]{1,0:T(8,128)(2,1)S(1)} %get-tuple-element.56), channel_id=1, source_target_pairs={{0,1},{1,2},{2,3},{3,4},{4,5},{5,6},{6,7},{7,0},{8,9},{9,10},{10,1... | collective-permute-start | bytes 393224 | tf_op jit(solution)/shard_map/ppermute | solution.py:330
  55.1 7.5 %collective-permute-start.8 = (bf16[16,4096]{1,0:T(8,128)(2,1)S(1)}, bf16[16,4096]{1,0:T(8,128)(2,1)S(1)}, u32[]{:S(2)}, u32[]{:S(2)}) collective-permute-start(bf16[16,4096]{1,0:T(8,128)(2,1)S(1)} %get-tuple-element.57), channel_id=1, source_target_pairs={{0,7},{1,0},{2,1},{3,2},{4,3},{5,4},{6,5},{7,6},{8,15},{9,8},{10,9... | collective-permute-start | bytes 393224 | tf_op jit(solution)/shard_map/ppermute | solution.py:330
  58.5 10.1 %collective-permute-start.13 = (bf16[2,16,4096]{2,1,0:T(8,128)(2,1)S(1)}, bf16[2,16,4096]{2,1,0:T(8,128)(2,1)S(1)}, u32[]{:S(2)}, u32[]{:S(2)}) collective-permute-start(bf16[2,16,4096]{2,1,0:T(8,128)(2,1)S(1)} %get-tuple-element.50), channel_id=1, source_target_pairs={{0,1},{1,2},{2,3},{3,4},{4,5},{5,6},{6,7},{7,0},{8,9},{9,10},{10,1... | collective-permute-start | bytes 786440 | tf_op jit(solution)/shard_map/ppermute | solution.py:330
  58.6 10.0 %collective-permute-start.16 = (bf16[2,16,4096]{2,1,0:T(8,128)(2,1)S(1)}, bf16[2,16,4096]{2,1,0:T(8,128)(2,1)S(1)}, u32[]{:S(2)}, u32[]{:S(2)}) collective-permute-start(bf16[2,16,4096]{2,1,0:T(8,128)(2,1)S(1)} %get-tuple-element.51), channel_id=1, source_target_pairs={{0,7},{1,0},{2,1},{3,2},{4,3},{5,4},{6,5},{7,6},{8,15},{9,8},{10,9... | collective-permute-start | bytes 786440 | tf_op jit(solution)/shard_map/ppermute | solution.py:330
  62.8 8.6 %collective-permute-start.7 = (bf16[16,4096]{1,0:T(8,128)(2,1)S(1)}, bf16[16,4096]{1,0:T(8,128)(2,1)S(1)}, u32[]{:S(2)}, u32[]{:S(2)}) collective-permute-start(bf16[16,4096]{1,0:T(8,128)(2,1)S(1)} %get-tuple-element.41), channel_id=1, source_target_pairs={{0,1},{1,2},{2,3},{3,4},{4,5},{5,6},{6,7},{7,0},{8,9},{9,10},{10,1... | collective-permute-start | bytes 393224 | tf_op jit(solution)/shard_map/ppermute | solution.py:330
  62.9 8.6 %collective-permute-start.9 = (bf16[16,4096]{1,0:T(8,128)(2,1)S(1)}, bf16[16,4096]{1,0:T(8,128)(2,1)S(1)}, u32[]{:S(2)}, u32[]{:S(2)}) collective-permute-start(bf16[16,4096]{1,0:T(8,128)(2,1)S(1)} %get-tuple-element.42), channel_id=1, source_target_pairs={{0,7},{1,0},{2,1},{3,2},{4,3},{5,4},{6,5},{7,6},{8,15},{9,8},{10,9... | collective-permute-start | bytes 393224 | tf_op jit(solution)/shard_map/ppermute | solution.py:330
  68.7 6.6 %collective-permute-start.17 = (bf16[16,4096]{1,0:T(8,128)(2,1)S(1)}, bf16[16,4096]{1,0:T(8,128)(2,1)S(1)}, u32[]{:S(2)}, u32[]{:S(2)}) collective-permute-start(bf16[16,4096]{1,0:T(8,128)(2,1)S(1)} %fusion.15), channel_id=1, source_target_pairs={{0,8},{1,9},{2,10},{3,11},{4,12},{5,13},{6,14},{7,15},{8,0},{9,1},... | collective-permute-start | bytes 393224 | tf_op jit(solution)/shard_map/ppermute | solution.py:334

commit v5 on v4

--- a/solution.py
+++ b/solution.py
@@ -274,9 +274,11 @@
     ready_ref,
     gated_ref,
     part_ref,
+    ahead_ref,
     flat,
     weight,
     sems,
+    ahead_sem,
 ):
     ready = ready_ref.shape[1]
     copies = column_copies(weight_hbm, weight, sems, ready)
@@ -300,13 +302,19 @@
     lane_loop(y_ref.shape[1], group)
     gated = jnp.dot(turn_ref[...], flat[...].astype(bf16), preferred_element_type=f32).astype(bf16)
     gated_ref[...] = gated
+    first = part_ref.shape[1]
+    ahead = pltpu.make_async_copy(weight_hbm.at[:, first : first + ahead_ref.shape[1]], ahead_ref, ahead_sem)
+    ahead.start()
     part_ref[:, :ready] = jnp.dot(gated, ready_ref[...], preferred_element_type=f32).astype(bf16)
     times(gated, copies, weight, part_ref, ready)
-
-
-def project_kernel(base, weight_hbm, gated_ref, part_ref, weight, sems):
-    copies = column_copies(weight_hbm, weight, sems, base)
-    times(gated_ref[...], copies, weight, part_ref)
+    ahead.wait()
+
+
+def project_kernel(base, weight_hbm, gated_ref, ahead_ref, part_ref, weight, sems):
+    ahead = ahead_ref.shape[1]
+    copies = column_copies(weight_hbm, weight, sems, base + ahead)
+    part_ref[:, :ahead] = jnp.dot(gated_ref[...], ahead_ref[...], preferred_element_type=f32).astype(bf16)
+    times(gated_ref[...], copies, weight, part_ref, ahead)
 
 
 def ring_pairs(n_ctx, by):
@@ -437,10 +445,10 @@
     def stream(width):
         return [((chans, width), bf16), pltpu.SemaphoreType.DMA((max(width // 1024, 1),))]
 
-    gated, first = call(
+    gated, first, ahead = call(
         functools.partial(gate_kernel, tokens),
-        [((rows, chans), bf16), ((rows, WIDTHS[0]), bf16)],
-        [wide, *stream(WIDTHS[0] - READY)],
+        [((rows, chans), bf16), ((rows, WIDTHS[0]), bf16), ((chans, READY), bf16)],
+        [wide, *stream(WIDTHS[0] - READY), pltpu.SemaphoreType.DMA],
         "gate",
         2 * rows * chans * WIDTHS[0],
         recv,
@@ -457,10 +465,11 @@
         parts += call(
             functools.partial(project_kernel, base),
             [((rows, width), bf16)],
-            stream(width),
+            stream(width - READY),
             "project",
             2 * rows * chans * width,
             gated,
+            ahead,
             far=(out_weight,),
         )
         base += width

time: 76.9 us -> 77 us (level)
  transfers between devices with their start and end apart: 19 -> 19, of which waited for: 8 -> 8; matrix products, arithmetic and copies ran while one was open for 1% -> 1% of each run, Pallas kernels for 12% -> 11%
where the time goes in v5:
time: 77 us; the launch traced here: 75.7 us
  starting transfers between devices  37.1 us (48%)
  waiting for transfers between devices  23.4 us (30%)
  Pallas kernels  12.4 us (16%)
  other arithmetic  1.66 us (2%)
  local copies, waits for them, and re-layouts  0.95 us (1%)
    ppermute x14, starting transfers between devices, along(): return lax.ppermute(x, ('ctx', 'tp'), ring_pairs(lax.axis_size('ctx'), way))  22.9 us
    ppermute x14, waiting for transfers between devices, along(): return lax.ppermute(x, ('ctx', 'tp'), ring_pairs(lax.axis_size('ctx'), way))  12.7 us
    pallas_call x5, Pallas kernels, call(): pl.pallas_call(kernel, in_specs=in_specs, out_specs=[pl.BlockSpec(memory_...  12.4 us
    ppermute x3, waiting for transfers between devices, across(): return lax.ppermute(x, 'tp', half_pairs())  7.6 us
    ppermute x3, starting transfers between devices, across(): return lax.ppermute(x, 'tp', half_pairs())  6.43 us
    all_to_all x1, starting transfers between devices, local(): recv = lax.all_to_all(send, 'ctx', 0, 0, tiled=True)  5.86 us
    all_to_all x1, waiting for transfers between devices, local(): recv = lax.all_to_all(send, 'ctx', 0, 0, tiled=True)  1.92 us
    ppermute x1, starting transfers between devices, local(): lax.ppermute(features[rows - HALO:], 'ctx', [(i, i + 1) for i in range(n_...  1.91 us
  transfers between devices with their start and end apart: 19, of which 8 were waited for; matrix products, arithmetic and copies ran while one was open for 1% of the time, Pallas kernels for 11%

profile of v5, /device:TPU:8, one launch (start us, length us, event | category | flops | bytes accessed | tf_op | source)
XLA Modules:
  0.0 75.7 jit_solution(15564742493428377405)
XLA Ops:
  0.0 0.8 %slice.94 = bf16[16,3,512]{2,0,1:T(8,128)(2,1)S(1)} slice(bf16[256,3,512]{2,0,1:T(8,128)(2,1)} %param.5), slice={[240:256], [0:3], [0:512]} | slice | bytes 98304 | tf_op jit(solution)/shard_map/slice | solution.py:398
  0.8 1.9 %collective-permute-start = (bf16[16,3,512]{2,0,1:T(8,128)(2,1)S(1)}, bf16[16,3,512]{2,0,1:T(8,128)(2,1)S(1)}, u32[]{:S(2)}, u32[]{:S(2)}) collective-permute-start(bf16[16,3,512]{2,0,1:T(8,128)(2,1)S(1)} %slice.94), channel_id=1, source_target_pairs={{0,16},{16,32},{32,48},{48,64},{64,80},{80,96},{96,112},{112,128},... | collective-permute-start | bytes 147464 | tf_op jit(solution)/shard_map/ppermute | solution.py:398
  2.7 2.3 %bulk.1 = (f32[2,96,512]{2,1,0:T(8,128)S(1)}, f32[256,512]{1,0:T(8,128)S(1)}, f32[16,8,512]{2,1,0:T(8,128)S(1)}, f32[3,7,512]{2,1,0:T(8,128)S(1)}, f32[16,512]{1,0:T(8,128)S(1)}) custom-call(bf16[3,256,512]{2,1,0:T(8,128)(2,1)} %bitcast.142, f32[3,7,512]{2,1,0:T(8,128)} %taps_hbm.1, f32[16,512]{1,0:T(8,128)} %rate_hbm.1), custom_call_target="tpu_custom_call" | custom-call | flops 8388608 | bytes 4194304 | tf_op jit(solution)/shard_map/bulk/pallas_call | solution.py:380
  5.1 1.1 %collective-permute-done = bf16[16,3,512]{2,0,1:T(8,128)(2,1)S(1)} collective-permute-done((bf16[16,3,512]{2,0,1:T(8,128)(2,1)S(1)}, bf16[16,3,512]{2,0,1:T(8,128)(2,1)S(1)}, u32[]{:S(2)}, u32[]{:S(2)}) %collective-permute-start) | collective-permute-done | bytes 49184 | tf_op jit(solution)/shard_map/ppermute | solution.py:398
  6.2 1.4 %edge.1 = (f32[48,512]{1,0:T(8,128)S(1)}, f32[16,8,512]{2,1,0:T(8,128)S(1)}, bf16[16,16,512]{2,1,0:T(8,128)(2,1)}) custom-call(f32[2,96,512]{2,1,0:T(8,128)S(1)} %get-tuple-element.24.head_ref, bf16[3,16,512]{2,1,0:T(8,128)(2,1)S(1)} %bitcast.140, f32[3,7,512]{2,1,0:T(8,128)S(1)} %get-tuple-element.25.taps_ref, f32[16,512]{1,0:T(8,128)S(1)} %get-tuple-element.26.rate_ref, ...), custom_call_target="tpu_custom_call" | custom-call | flops 2097152 | bytes 4194304 | tf_op jit(solution)/shard_map/edge/pallas_call | solution.py:380
  7.6 5.9 %all-to-all-start = ((bf16[16,16,512]{2,1,0:T(8,128)(2,1)}), bf16[16,16,512]{2,1,0:T(8,128)(2,1)S(1)}, u32[]{:S(2)}, u32[]{:S(2)}) async-start(bf16[16,16,512]{2,1,0:T(8,128)(2,1)} %get-tuple-element.28), calls=%async_computation | async-start | bytes 524288 | tf_op jit(solution)/shard_map/all_to_all | solution.py:425
  13.5 3.5 %inner.1 = (f32[256,512]{1,0:T(8,128)S(1)}, f32[256,512]{1,0:T(8,128)S(1)}, f32[16,8,512]{2,1,0:T(8,128)S(1)}, bf16[256,256]{1,0:T(8,128)(2,1)S(1)}, bf16[512,1024]{1,0:T(8,128)(2,1)S(1)}) custom-call(bf16[3,256,512]{2,1,0:T(8,128)(2,1)} %bitcast.143, bf16[512,8192]{1,0:T(8,128)(2,1)} %weight_hbm.5, ...), custom_call_target="tpu_custom_call", output_to_operand_aliasing={{1}: (6, {})} | custom-call | flops 16777216 | bytes 4194304 | tf_op jit(solution)/shard_map/inner/pallas_call | solution.py:380
  17.0 1.9 %all-to-all-done.recv_ref = bf16[16,16,512]{2,1,0:T(8,128)(2,1)S(1)} async-done(((bf16[16,16,512]{2,1,0:T(8,128)(2,1)}), bf16[16,16,512]{2,1,0:T(8,128)(2,1)S(1)}, u32[]{:S(2)}, u32[]{:S(2)}) %all-to-all-start) | async-done | bytes 262176 | tf_op jit(solution)/shard_map/all_to_all | solution.py:425
  18.9 2.6 %gate.1 = (bf16[256,512]{1,0:T(8,128)(2,1)S(1)}, bf16[256,4096]{1,0:T(8,128)(2,1)S(1)}, bf16[512,1024]{1,0:T(8,128)(2,1)S(1)}) custom-call(bf16[512,8192]{1,0:T(8,128)(2,1)} %weight_hbm.5, bf16[16,16,512]{2,1,0:T(8,128)(2,1)S(1)} %all-to-all-done.recv_ref, f32[16,512]{1,0:T(8,128)S(1)} %get-tuple-element.26.rate_ref, ...), custom_call_target="tpu_custom_call" | custom-call | flops 1073741824 | bytes 4194304 | tf_op jit(solution)/shard_map/gate/pallas_call | solution.py:380
  21.6 2.0 %collective-permute-start.1 = (bf16[2,16,4096]{2,1,0:T(8,128)(2,1)S(1)}, bf16[2,16,4096]{2,1,0:T(8,128)(2,1)S(1)}, u32[]{:S(2)}, u32[]{:S(2)}) collective-permute-start(bf16[2,16,4096]{2,1,0:T(8,128)(2,1)S(1)} %get-tuple-element.50), channel_id=1, source_target_pairs={{0,1},{1,2},{2,3},{3,4},{4,5},{5,6},{6,7},{7,0},{8,9},{9,10},{10,1... | collective-permute-start | bytes 786440 | tf_op jit(solution)/shard_map/ppermute | solution.py:338
  23.6 4.0 %collective-permute-start.3 = (bf16[2,16,4096]{2,1,0:T(8,128)(2,1)S(1)}, bf16[2,16,4096]{2,1,0:T(8,128)(2,1)S(1)}, u32[]{:S(2)}, u32[]{:S(2)}) collective-permute-start(bf16[2,16,4096]{2,1,0:T(8,128)(2,1)S(1)} %get-tuple-element.51), channel_id=1, source_target_pairs={{0,7},{1,0},{2,1},{3,2},{4,3},{5,4},{6,5},{7,6},{8,15},{9,8},{10,9... | collective-permute-start | bytes 786440 | tf_op jit(solution)/shard_map/ppermute | solution.py:338
  27.6 2.6 %project.1 = bf16[256,4096]{1,0:T(8,128)(2,1)S(1)} custom-call(bf16[512,8192]{1,0:T(8,128)(2,1)} %weight_hbm.5, bf16[256,512]{1,0:T(8,128)(2,1)S(1)} %get-tuple-element.41.gated_ref, bf16[512,1024]{1,0:T(8,128)(2,1)S(1)} %get-tuple-element.42.ahead_ref), custom_call_target="tpu_custom_call" | custom-call | flops 1073741824 | bytes 4194304 | tf_op jit(solution)/shard_map/project/pallas_call | solution.py:380
  30.3 3.2 %collective-permute-start.14 = (bf16[2,16,4096]{2,1,0:T(8,128)(2,1)S(1)}, bf16[2,16,4096]{2,1,0:T(8,128)(2,1)S(1)}, u32[]{:S(2)}, u32[]{:S(2)}) collective-permute-start(bf16[2,16,4096]{2,1,0:T(8,128)(2,1)S(1)} %get-tuple-element.57), channel_id=1, source_target_pairs={{0,7},{1,0},{2,1},{3,2},{4,3},{5,4},{6,5},{7,6},{8,15},{9,8},{10,9... | collective-permute-start | bytes 786440 | tf_op jit(solution)/shard_map/ppermute | solution.py:338
  33.8 4.8 %collective-permute-done.10 = bf16[2,16,4096]{2,1,0:T(8,128)(2,1)S(1)} collective-permute-done((bf16[2,16,4096]{2,1,0:T(8,128)(2,1)S(1)}, bf16[2,16,4096]{2,1,0:T(8,128)(2,1)S(1)}, u32[]{:S(2)}, u32[]{:S(2)}) %collective-permute-start.10) | collective-permute-done | bytes 262176 | tf_op jit(solution)/shard_map/ppermute | solution.py:338
  38.7 4.8 %collective-permute-done.2 = bf16[2,16,4096]{2,1,0:T(8,128)(2,1)S(1)} collective-permute-done((bf16[2,16,4096]{2,1,0:T(8,128)(2,1)S(1)}, bf16[2,16,4096]{2,1,0:T(8,128)(2,1)S(1)}, u32[]{:S(2)}, u32[]{:S(2)}) %collective-permute-start.2) | collective-permute-done | bytes 262176 | tf_op jit(solution)/shard_map/ppermute | solution.py:338
  43.7 2.8 %collective-permute-start.4 = (bf16[2,16,4096]{2,1,0:T(8,128)(2,1)S(1)}, bf16[2,16,4096]{2,1,0:T(8,128)(2,1)S(1)}, u32[]{:S(2)}, u32[]{:S(2)}) collective-permute-start(bf16[2,16,4096]{2,1,0:T(8,128)(2,1)S(1)} %pad_maximum_fusion.1), channel_id=1, source_target_pairs={{0,8},{1,9},{2,10},{3,11},{4,12},{5,13},{6,14},{7,15},{8,0},{9,1},... | collective-permute-start | bytes 786440 | tf_op jit(solution)/shard_map/ppermute | solution.py:342
  47.6 3.2 %collective-permute-start.15 = (bf16[2,16,4096]{2,1,0:T(8,128)(2,1)S(1)}, bf16[2,16,4096]{2,1,0:T(8,128)(2,1)S(1)}, u32[]{:S(2)}, u32[]{:S(2)}) collective-permute-start(bf16[2,16,4096]{2,1,0:T(8,128)(2,1)S(1)} %get-tuple-element.55), channel_id=1, source_target_pairs={{0,7},{1,0},{2,1},{3,2},{4,3},{5,4},{6,5},{7,6},{8,15},{9,8},{10,9... | collective-permute-start | bytes 786440 | tf_op jit(solution)/shard_map/ppermute | solution.py:338
  50.8 3.8 %collective-permute-done.4 = bf16[2,16,4096]{2,1,0:T(8,128)(2,1)S(1)} collective-permute-done((bf16[2,16,4096]{2,1,0:T(8,128)(2,1)S(1)}, bf16[2,16,4096]{2,1,0:T(8,128)(2,1)S(1)}, u32[]{:S(2)}, u32[]{:S(2)}) %collective-permute-start.4) | collective-permute-done | bytes 262176 | tf_op jit(solution)/shard_map/ppermute | solution.py:342
  54.7 3.2 %collective-permute-start.8 = (bf16[16,4096]{1,0:T(8,128)(2,1)S(1)}, bf16[16,4096]{1,0:T(8,128)(2,1)S(1)}, u32[]{:S(2)}, u32[]{:S(2)}) collective-permute-start(bf16[16,4096]{1,0:T(8,128)(2,1)S(1)} %get-tuple-element.59), channel_id=1, source_target_pairs={{0,7},{1,0},{2,1},{3,2},{4,3},{5,4},{6,5},{7,6},{8,15},{9,8},{10,9... | collective-permute-start | bytes 393224 | tf_op jit(solution)/shard_map/ppermute | solution.py:338
  58.2 3.2 %collective-permute-start.16 = (bf16[2,16,4096]{2,1,0:T(8,128)(2,1)S(1)}, bf16[2,16,4096]{2,1,0:T(8,128)(2,1)S(1)}, u32[]{:S(2)}, u32[]{:S(2)}) collective-permute-start(bf16[2,16,4096]{2,1,0:T(8,128)(2,1)S(1)} %get-tuple-element.53), channel_id=1, source_target_pairs={{0,7},{1,0},{2,1},{3,2},{4,3},{5,4},{6,5},{7,6},{8,15},{9,8},{10,9... | collective-permute-start | bytes 786440 | tf_op jit(solution)/shard_map/ppermute | solution.py:338
  62.4 3.4 %collective-permute-start.9 = (bf16[16,4096]{1,0:T(8,128)(2,1)S(1)}, bf16[16,4096]{1,0:T(8,128)(2,1)S(1)}, u32[]{:S(2)}, u32[]{:S(2)}) collective-permute-start(bf16[16,4096]{1,0:T(8,128)(2,1)S(1)} %get-tuple-element.44), channel_id=1, source_target_pairs={{0,7},{1,0},{2,1},{3,2},{4,3},{5,4},{6,5},{7,6},{8,15},{9,8},{10,9... | collective-permute-start | bytes 393224 | tf_op jit(solution)/shard_map/ppermute | solution.py:338
  65.8 2.3 %collective-permute-done.13 = bf16[2,16,4096]{2,1,0:T(8,128)(2,1)S(1)} collective-permute-done((bf16[2,16,4096]{2,1,0:T(8,128)(2,1)S(1)}, bf16[2,16,4096]{2,1,0:T(8,128)(2,1)S(1)}, u32[]{:S(2)}, u32[]{:S(2)}) %collective-permute-start.13) | collective-permute-done | bytes 262176 | tf_op jit(solution)/shard_map/ppermute | solution.py:338
  68.2 2.8 %collective-permute-start.17 = (bf16[16,4096]{1,0:T(8,128)(2,1)S(1)}, bf16[16,4096]{1,0:T(8,128)(2,1)S(1)}, u32[]{:S(2)}, u32[]{:S(2)}) collective-permute-start(bf16[16,4096]{1,0:T(8,128)(2,1)S(1)} %fusion.15), channel_id=1, source_target_pairs={{0,8},{1,9},{2,10},{3,11},{4,12},{5,13},{6,14},{7,15},{8,0},{9,1},... | collective-permute-start | bytes 393224 | tf_op jit(solution)/shard_map/ppermute | solution.py:342
  71.1 3.8 %collective-permute-done.17 = bf16[16,4096]{1,0:T(8,128)(2,1)S(1)} collective-permute-done((bf16[16,4096]{1,0:T(8,128)(2,1)S(1)}, bf16[16,4096]{1,0:T(8,128)(2,1)S(1)}, u32[]{:S(2)}, u32[]{:S(2)}) %collective-permute-start.17) | collective-permute-done | bytes 131104 | tf_op jit(solution)/shard_map/ppermute | solution.py:342
  (44 shorter events, 4.0 us)
Async XLA Ops:
  0.0 13.4 %copy-start = (f32[16,512]{1,0:T(8,128)S(1)}, f32[16,512]{1,0:T(8,128)}, u32[]{:S(2)}) copy-start(f32[16,512]{1,0:T(8,128)} %rate_hbm.1) | copy-start | bytes 98308
  0.0 13.4 %copy-start.1 = (f32[16,512]{1,0:T(8,128)S(1)}, f32[16,512]{1,0:T(8,128)}, u32[]{:S(2)}) copy-start(f32[16,512]{1,0:T(8,128)} %param.8) | copy-start | bytes 98308
  0.8 5.4 %collective-permute-start = (bf16[16,3,512]{2,0,1:T(8,128)(2,1)S(1)}, bf16[16,3,512]{2,0,1:T(8,128)(2,1)S(1)}, u32[]{:S(2)}, u32[]{:S(2)}) collective-permute-start(bf16[16,3,512]{2,0,1:T(8,128)(2,1)S(1)} %slice.94), channel_id=1, source_target_pairs={{0,16},{16,32},{32,48},{48,64},{64,80},{80,96},{96,112},{112,128},... | collective-permute-start | bytes 147464 | tf_op jit(solution)/shard_map/ppermute | solution.py:398
  7.6 11.3 %all-to-all-start = ((bf16[16,16,512]{2,1,0:T(8,128)(2,1)}), bf16[16,16,512]{2,1,0:T(8,128)(2,1)S(1)}, u32[]{:S(2)}, u32[]{:S(2)}) async-start(bf16[16,16,512]{2,1,0:T(8,128)(2,1)} %get-tuple-element.28), calls=%async_computation | async-start | bytes 524288 | tf_op jit(solution)/shard_map/all_to_all | solution.py:425
  21.6 12.0 %collective-permute-start.1 = (bf16[2,16,4096]{2,1,0:T(8,128)(2,1)S(1)}, bf16[2,16,4096]{2,1,0:T(8,128)(2,1)S(1)}, u32[]{:S(2)}, u32[]{:S(2)}) collective-permute-start(bf16[2,16,4096]{2,1,0:T(8,128)(2,1)S(1)} %get-tuple-element.50), channel_id=1, source_target_pairs={{0,1},{1,2},{2,3},{3,4},{4,5},{5,6},{6,7},{7,0},{8,9},{9,10},{10,1... | collective-permute-start | bytes 786440 | tf_op jit(solution)/shard_map/ppermute | solution.py:338
  23.6 15.1 %collective-permute-start.3 = (bf16[2,16,4096]{2,1,0:T(8,128)(2,1)S(1)}, bf16[2,16,4096]{2,1,0:T(8,128)(2,1)S(1)}, u32[]{:S(2)}, u32[]{:S(2)}) collective-permute-start(bf16[2,16,4096]{2,1,0:T(8,128)(2,1)S(1)} %get-tuple-element.51), channel_id=1, source_target_pairs={{0,7},{1,0},{2,1},{3,2},{4,3},{5,4},{6,5},{7,6},{8,15},{9,8},{10,9... | collective-permute-start | bytes 786440 | tf_op jit(solution)/shard_map/ppermute | solution.py:338
  30.3 8.3 %collective-permute-start.10 = (bf16[2,16,4096]{2,1,0:T(8,128)(2,1)S(1)}, bf16[2,16,4096]{2,1,0:T(8,128)(2,1)S(1)}, u32[]{:S(2)}, u32[]{:S(2)}) collective-permute-start(bf16[2,16,4096]{2,1,0:T(8,128)(2,1)S(1)} %get-tuple-element.56), channel_id=1, source_target_pairs={{0,1},{1,2},{2,3},{3,4},{4,5},{5,6},{6,7},{7,0},{8,9},{9,10},{10,1... | collective-permute-start | bytes 786440 | tf_op jit(solution)/shard_map/ppermute | solution.py:338
  30.3 17.0 %collective-permute-start.14 = (bf16[2,16,4096]{2,1,0:T(8,128)(2,1)S(1)}, bf16[2,16,4096]{2,1,0:T(8,128)(2,1)S(1)}, u32[]{:S(2)}, u32[]{:S(2)}) collective-permute-start(bf16[2,16,4096]{2,1,0:T(8,128)(2,1)S(1)} %get-tuple-element.57), channel_id=1, source_target_pairs={{0,7},{1,0},{2,1},{3,2},{4,3},{5,4},{6,5},{7,6},{8,15},{9,8},{10,9... | collective-permute-start | bytes 786440 | tf_op jit(solution)/shard_map/ppermute | solution.py:338
  33.7 9.8 %collective-permute-start.2 = (bf16[2,16,4096]{2,1,0:T(8,128)(2,1)S(1)}, bf16[2,16,4096]{2,1,0:T(8,128)(2,1)S(1)}, u32[]{:S(2)}, u32[]{:S(2)}) collective-permute-start(bf16[2,16,4096]{2,1,0:T(8,128)(2,1)S(1)} %fusion.7), channel_id=1, source_target_pairs={{0,1},{1,2},{2,3},{3,4},{4,5},{5,6},{6,7},{7,0},{8,9},{9,10},{10,1... | collective-permute-start | bytes 786440 | tf_op jit(solution)/shard_map/ppermute | solution.py:338
  38.6 8.7 %collective-permute-start.11 = (bf16[2,16,4096]{2,1,0:T(8,128)(2,1)S(1)}, bf16[2,16,4096]{2,1,0:T(8,128)(2,1)S(1)}, u32[]{:S(2)}, u32[]{:S(2)}) collective-permute-start(bf16[2,16,4096]{2,1,0:T(8,128)(2,1)S(1)} %fusion.4), channel_id=1, source_target_pairs={{0,1},{1,2},{2,3},{3,4},{4,5},{5,6},{6,7},{7,0},{8,9},{9,10},{10,1... | collective-permute-start | bytes 786440 | tf_op jit(solution)/shard_map/ppermute | solution.py:338
  43.7 10.8 %collective-permute-start.4 = (bf16[2,16,4096]{2,1,0:T(8,128)(2,1)S(1)}, bf16[2,16,4096]{2,1,0:T(8,128)(2,1)S(1)}, u32[]{:S(2)}, u32[]{:S(2)}) collective-permute-start(bf16[2,16,4096]{2,1,0:T(8,128)(2,1)S(1)} %pad_maximum_fusion.1), channel_id=1, source_target_pairs={{0,8},{1,9},{2,10},{3,11},{4,12},{5,13},{6,14},{7,15},{8,0},{9,1},... | collective-permute-start | bytes 786440 | tf_op jit(solution)/shard_map/ppermute | solution.py:342
  46.5 15.6 %collective-permute-start.6 = (bf16[3,16,4096]{2,1,0:T(8,128)(2,1)S(1)}, bf16[3,16,4096]{2,1,0:T(8,128)(2,1)S(1)}, u32[]{:S(2)}, u32[]{:S(2)}) collective-permute-start(bf16[3,16,4096]{2,1,0:T(8,128)(2,1)S(1)} %pad_maximum_fusion), channel_id=1, source_target_pairs={{0,8},{1,9},{2,10},{3,11},{4,12},{5,13},{6,14},{7,15},{8,0},{9,1},... | collective-permute-start | bytes 1179656 | tf_op jit(solution)/shard_map/ppermute | solution.py:342
  47.5 10.5 %collective-permute-start.12 = (bf16[2,16,4096]{2,1,0:T(8,128)(2,1)S(1)}, bf16[2,16,4096]{2,1,0:T(8,128)(2,1)S(1)}, u32[]{:S(2)}, u32[]{:S(2)}) collective-permute-start(bf16[2,16,4096]{2,1,0:T(8,128)(2,1)S(1)} %get-tuple-element.54), channel_id=1, source_target_pairs={{0,1},{1,2},{2,3},{3,4},{4,5},{5,6},{6,7},{7,0},{8,9},{9,10},{10,1... | collective-permute-start | bytes 786440 | tf_op jit(solution)/shard_map/ppermute | solution.py:338
  47.6 10.4 %collective-permute-start.15 = (bf16[2,16,4096]{2,1,0:T(8,128)(2,1)S(1)}, bf16[2,16,4096]{2,1,0:T(8,128)(2,1)S(1)}, u32[]{:S(2)}, u32[]{:S(2)}) collective-permute-start(bf16[2,16,4096]{2,1,0:T(8,128)(2,1)S(1)} %get-tuple-element.55), channel_id=1, source_target_pairs={{0,7},{1,0},{2,1},{3,2},{4,3},{5,4},{6,5},{7,6},{8,15},{9,8},{10,9... | collective-permute-start | bytes 786440 | tf_op jit(solution)/shard_map/ppermute | solution.py:338
  54.6 7.6 %collective-permute-start.5 = (bf16[16,4096]{1,0:T(8,128)(2,1)S(1)}, bf16[16,4096]{1,0:T(8,128)(2,1)S(1)}, u32[]{:S(2)}, u32[]{:S(2)}) collective-permute-start(bf16[16,4096]{1,0:T(8,128)(2,1)S(1)} %get-tuple-element.58), channel_id=1, source_target_pairs={{0,1},{1,2},{2,3},{3,4},{4,5},{5,6},{6,7},{7,0},{8,9},{9,10},{10,1... | collective-permute-start | bytes 393224 | tf_op jit(solution)/shard_map/ppermute | solution.py:338
  54.7 7.5 %collective-permute-start.8 = (bf16[16,4096]{1,0:T(8,128)(2,1)S(1)}, bf16[16,4096]{1,0:T(8,128)(2,1)S(1)}, u32[]{:S(2)}, u32[]{:S(2)}) collective-permute-start(bf16[16,4096]{1,0:T(8,128)(2,1)S(1)} %get-tuple-element.59), channel_id=1, source_target_pairs={{0,7},{1,0},{2,1},{3,2},{4,3},{5,4},{6,5},{7,6},{8,15},{9,8},{10,9... | collective-permute-start | bytes 393224 | tf_op jit(solution)/shard_map/ppermute | solution.py:338
  58.1 10.0 %collective-permute-start.13 = (bf16[2,16,4096]{2,1,0:T(8,128)(2,1)S(1)}, bf16[2,16,4096]{2,1,0:T(8,128)(2,1)S(1)}, u32[]{:S(2)}, u32[]{:S(2)}) collective-permute-start(bf16[2,16,4096]{2,1,0:T(8,128)(2,1)S(1)} %get-tuple-element.52), channel_id=1, source_target_pairs={{0,1},{1,2},{2,3},{3,4},{4,5},{5,6},{6,7},{7,0},{8,9},{9,10},{10,1... | collective-permute-start | bytes 786440 | tf_op jit(solution)/shard_map/ppermute | solution.py:338
  58.2 9.9 %collective-permute-start.16 = (bf16[2,16,4096]{2,1,0:T(8,128)(2,1)S(1)}, bf16[2,16,4096]{2,1,0:T(8,128)(2,1)S(1)}, u32[]{:S(2)}, u32[]{:S(2)}) collective-permute-start(bf16[2,16,4096]{2,1,0:T(8,128)(2,1)S(1)} %get-tuple-element.53), channel_id=1, source_target_pairs={{0,7},{1,0},{2,1},{3,2},{4,3},{5,4},{6,5},{7,6},{8,15},{9,8},{10,9... | collective-permute-start | bytes 786440 | tf_op jit(solution)/shard_map/ppermute | solution.py:338
  62.3 8.7 %collective-permute-start.7 = (bf16[16,4096]{1,0:T(8,128)(2,1)S(1)}, bf16[16,4096]{1,0:T(8,128)(2,1)S(1)}, u32[]{:S(2)}, u32[]{:S(2)}) collective-permute-start(bf16[16,4096]{1,0:T(8,128)(2,1)S(1)} %get-tuple-element.43), channel_id=1, source_target_pairs={{0,1},{1,2},{2,3},{3,4},{4,5},{5,6},{6,7},{7,0},{8,9},{9,10},{10,1... | collective-permute-start | bytes 393224 | tf_op jit(solution)/shard_map/ppermute | solution.py:338
  62.4 8.6 %collective-permute-start.9 = (bf16[16,4096]{1,0:T(8,128)(2,1)S(1)}, bf16[16,4096]{1,0:T(8,128)(2,1)S(1)}, u32[]{:S(2)}, u32[]{:S(2)}) collective-permute-start(bf16[16,4096]{1,0:T(8,128)(2,1)S(1)} %get-tuple-element.44), channel_id=1, source_target_pairs={{0,7},{1,0},{2,1},{3,2},{4,3},{5,4},{6,5},{7,6},{8,15},{9,8},{10,9... | collective-permute-start | bytes 393224 | tf_op jit(solution)/shard_map/ppermute | solution.py:338
  68.2 6.7 %collective-permute-start.17 = (bf16[16,4096]{1,0:T(8,128)(2,1)S(1)}, bf16[16,4096]{1,0:T(8,128)(2,1)S(1)}, u32[]{:S(2)}, u32[]{:S(2)}) collective-permute-start(bf16[16,4096]{1,0:T(8,128)(2,1)S(1)} %fusion.15), channel_id=1, source_target_pairs={{0,8},{1,9},{2,10},{3,11},{4,12},{5,13},{6,14},{7,15},{8,0},{9,1},... | collective-permute-start | bytes 393224 | tf_op jit(solution)/shard_map/ppermute | solution.py:342
